TPU v7x, 256 devices: a whole 4x4x8 slice. The times are simulated.
256 devices in a mesh: replica: 16 (over z_hi, x), fsdp: 16 (over y, z_lo, core).
Axes of the slice: x: 4, y: 4, z: 8 (z_hi: 4, z_lo: 2; z = z_hi * 2 + z_lo), core: 2. Of those that a mesh axis runs over, the one named last changes fastest.
Arguments:
- hidden: bfloat16 [32768, 4608], P(('replica', 'fsdp')), may hold values from -24 to 24
- key_cotangent: bfloat16 [32768, 1024], P(('replica', 'fsdp')), may hold values from -2 to 2
- norm_gain: float32 [4608], replicated, may hold values from 0.1 to 1.9
- weights: bfloat16 [16, 4, 4608, 1024], P('replica', None, 'fsdp'), may hold values from -0.796875 to 0.796875
- adam_first: float32 [16, 4608, 1024], P('replica', 'fsdp'), may hold values from -6 to 6
- adam_second: float32 [16, 4608, 1024], P('replica', 'fsdp'), may hold values from 0.5 to 50
- inner_step: int32 [], replicated, may hold values from 1 to 4096
- outer_global: float32 [4, 4608, 1024], P(None, 'fsdp', 'replica'), may hold values from -0.8 to 0.8
- outer_momentum: float32 [4, 4608, 1024], P(None, 'fsdp', 'replica'), may hold values from -0.8 to 0.8
Outputs:
- new_weights: bfloat16 [16, 4, 4608, 1024], P('replica', None, 'fsdp')
- hidden_grad: bfloat16 [32768, 4608], P(('replica', 'fsdp'))
- new_first: float32 [16, 4608, 1024], P('replica', 'fsdp')
- new_second: float32 [16, 4608, 1024], P('replica', 'fsdp')
- new_global: float32 [4, 4608, 1024], P(None, 'fsdp', 'replica')
- new_momentum: float32 [4, 4608, 1024], P(None, 'fsdp', 'replica')
All inputs are finite; a program needn't handle non-finite values.
Results may differ from a plain program's by a relative error of at most 0.0006.
Values may be sent and summed in bfloat16 or wider, within the bound.
No kernel may reach another device: no remote copies, remote signals or barrier semaphores. Data moves between devices by JAX's collectives and lax.ppermute only.
A program may use at most 128 MiB of HBM per device.

v0:
```python
import jax
import jax.numpy as jnp
from jax import lax
from jax.sharding import PartitionSpec as P

FRAGS = 4


beta_first = 0.9
beta_second = 0.95
inner_rate = 0.004
warmup_steps = 4096.0
weight_decay = 0.1
outer_rate = 0.7
outer_mom = 0.9
mix_share = 0.5
norm_eps = 1e-06
adam_eps = 1e-08


def local(
    hidden,
    key_cotangent,
    norm_gain,
    weights,
    adam_first,
    adam_second,
    inner_step,
    outer_global,
    outer_momentum,
):
    frag_index = inner_step % FRAGS
    rows_f = hidden.astype(jnp.float32)
    inverse = lax.rsqrt(jnp.mean(rows_f * rows_f, axis=1, keepdims=True) + norm_eps)
    normed = (rows_f * inverse * norm_gain).astype(jnp.bfloat16)
    local_w = lax.dynamic_index_in_dim(weights[0], frag_index, 0, keepdims=False)
    back = lax.dot_general(
        key_cotangent,
        lax.all_gather(local_w, "fsdp", axis=0, tiled=True),
        (((1,), (1,)), ((), ())),
        preferred_element_type=jnp.float32,
    )
    grad = lax.psum_scatter(
        lax.dot_general(
            normed, key_cotangent, (((0,), (0,)), ((), ())), preferred_element_type=jnp.float32
        ),
        "fsdp",
        scatter_dimension=0,
        tiled=True,
    )
    scaled = norm_gain * back
    project = jnp.mean(scaled * rows_f, axis=1, keepdims=True)
    hidden_grad = (inverse * scaled - rows_f * inverse * inverse * inverse * project).astype(
        jnp.bfloat16
    )
    counter = inner_step.astype(jnp.float32)
    step_rate = inner_rate * jnp.minimum(jnp.float32(1.0), counter / warmup_steps)
    first_next = beta_first * adam_first[0] + (1.0 - beta_first) * grad
    second_next = beta_second * adam_second[0] + (1.0 - beta_second) * grad * grad
    first_hat = first_next / (1.0 - jnp.power(jnp.float32(beta_first), counter))
    second_hat = second_next / (1.0 - jnp.power(jnp.float32(beta_second), counter))
    snapshot = local_w.astype(jnp.float32)
    updated = snapshot - step_rate * (
        first_hat / (jnp.sqrt(second_hat) + adam_eps) + weight_decay * snapshot
    )
    glob_slot = lax.dynamic_index_in_dim(outer_global, frag_index, 0, keepdims=False)
    mom_slot = lax.dynamic_index_in_dim(outer_momentum, frag_index, 0, keepdims=False)
    replicas = lax.axis_size("replica")
    whole_sum = lax.psum(snapshot, "replica")
    glob_all, mom_all = (
        lax.all_gather(glob_slot, "replica", axis=1, tiled=True),
        lax.all_gather(mom_slot, "replica", axis=1, tiled=True),
    )
    pseudo_all = glob_all - whole_sum / replicas
    momentum_all = outer_mom * mom_all + pseudo_all
    global_full = glob_all - outer_rate * (pseudo_all + outer_mom * momentum_all)
    share_width = glob_slot.shape[1]
    position = lax.axis_index("replica") * share_width
    global_next = lax.dynamic_slice_in_dim(global_full, position, share_width, 1)
    momentum_next = lax.dynamic_slice_in_dim(momentum_all, position, share_width, 1)
    merged = (mix_share * updated + (1.0 - mix_share) * global_full).astype(jnp.bfloat16)
    layers_out = lax.dynamic_update_index_in_dim(weights[0], merged, frag_index, 0)
    new_global = lax.dynamic_update_index_in_dim(outer_global, global_next, frag_index, 0)
    new_momentum = lax.dynamic_update_index_in_dim(outer_momentum, momentum_next, frag_index, 0)
    return (
        layers_out[None],
        hidden_grad,
        first_next[None],
        second_next[None],
        new_global,
        new_momentum,
    )


def solution(mesh):
    in_specs = (
        P(("replica", "fsdp"), None),
        P(("replica", "fsdp"), None),
        P(),
        P("replica", None, "fsdp", None),
        P("replica", "fsdp", None),
        P("replica", "fsdp", None),
        P(),
        P(None, "fsdp", "replica"),
        P(None, "fsdp", "replica"),
    )
    out_specs = (
        P("replica", None, "fsdp", None),
        P(("replica", "fsdp"), None),
        P("replica", "fsdp", None),
        P("replica", "fsdp", None),
        P(None, "fsdp", "replica"),
        P(None, "fsdp", "replica"),
    )
    return jax.shard_map(local, mesh=mesh, in_specs=in_specs, out_specs=out_specs, check_vma=False)
```

profile of v0, /device:TPU:14, one launch (start us, length us, event | category | flops | bytes accessed | tf_op | source)
XLA Modules:
  0.0 583.8 jit_solution(9931588094474803753)
XLA Ops:
  7.2 1.7 copy.43
  9.8 1.4 bitcast_convert_fusion
  11.4 0.7 copy.33
  12.2 0.7 copy.34
  13.0 0.5 all-reduce.2.cloned.1.call-update
  13.6 0.7 copy.25
  14.4 59.4 %all-gather.11.cloned.1.call-done = bf16[1,1,4608,1024]{3,2,1,0:T(8,128)(2,1)} async-done(((bf16[1,1,288,1024]{3,2,1,0:T(8,128)(2,1)}), bf16[1,1,4608,1024]{3,2,1,0:T(8,128)(2,1)}) %all-gather.11.cloned.1.call-update) | async-done | bytes 9437200 | tf_op jit(solution)/shard_map/all_gather | solution.py:39
  73.7 7.7 %fusion.16 = (f32[128]{0:T(128)S(1)}, f32[128]{0:T(128)S(1)}, f32[128,4608]{0,1:T(8,128)}) fusion(bf16[128,4608]{0,1:T(8,128)(2,1)S(1)} %copy.25, bf16[128,1024]{1,0:T(8,128)(2,1)S(1)} %copy-done, bf16[1,1,4608,1024]{3,2,1,0:T(8,128)(2,1)} %all-gather.11.cloned.1.call-done, f32[4608]{0:T(1024)S(1)} %copy-done.11), kind=kOutput, calls=%fused_computation.15 | convolution fusion | flops 1211498240 | bytes 13257728 | tf_op jit(solution)/shard_map/dot_general | solution.py:37
  81.5 8.3 %fusion.18 = f32[4608,1024]{1,0:T(8,128)} fusion(bf16[128,1024]{1,0:T(8,128)(2,1)S(1)} %copy-done, bf16[128,4608]{0,1:T(8,128)(2,1)S(1)} %copy.25, f32[4608]{0:T(1024)S(1)} %copy-done.11, f32[128]{0:T(128)S(1)} %add_rsqrt_fusion), kind=kOutput, calls=%fused_computation.18 | convolution fusion | flops 1210318848 | bytes 20335104 | tf_op jit(solution)/shard_map/dot_general | solution.py:44
  89.8 42.7 %all-gather.7.cloned.1.call-done = f32[1,288,1024]{1,0,2:T(1,128)} async-done(((f32[1,288,64]{1,0,2:T(1,128)}), f32[1,288,1024]{1,0,2:T(1,128)}) %all-gather.7.cloned.1.call-update) | async-done | bytes 1179664 | tf_op jit(solution)/shard_map/all_gather | solution.py:71
  132.6 3.6 copy.27
  136.1 53.2 %all-gather.9.cloned.1.call-done = f32[1,288,1024]{1,0,2:T(1,128)} async-done(((f32[1,288,64]{1,0,2:T(1,128)}), f32[1,288,1024]{1,0,2:T(1,128)}) %all-gather.9.cloned.1.call-update) | async-done | bytes 1179664 | tf_op jit(solution)/shard_map/all_gather | solution.py:72
  189.3 4.8 copy.29
  194.1 163.3 %all-reduce.2.cloned.1.call-done = f32[288,1024]{1,0:T(8,128)} async-done(((f32[288,1024]{1,0:T(8,128)}), f32[288,1024]{1,0:T(8,128)}) %all-reduce.2.cloned.1.call-update) | async-done | bytes 1179664 | tf_op jit(solution)/shard_map/psum | solution.py:69
  357.3 3.2 bitcast_add_fusion
  360.5 1.6 fusion.14
  362.2 2.5 copy.32
  364.7 201.8 %reduce-scatter.2.cloned.1.call-done = f32[288,1024]{1,0:T(8,128)} async-done(((f32[4608,1024]{1,0:T(8,128)}), f32[288,1024]{1,0:T(8,128)}) %reduce-scatter.2.cloned.1.call-update) | async-done | bytes 1179664 | tf_op jit(solution)/shard_map/reduce_scatter | solution.py:43
  566.5 4.5 bitcast_dynamic-update-slice_fusion
  571.0 1.1 constant_dynamic-slice_fusion
  572.1 0.1 copy.31
  572.3 0.7 bitcast_dynamic-update-slice_fusion.1
  573.0 0.7 bitcast_dynamic-update-slice_fusion.2
  573.7 3.6 fusion.23
  (40 shorter events, 0.6 us)
Async XLA Ops:
  7.2 66.6 %copy-start = (bf16[128,1024]{1,0:T(8,128)(2,1)S(1)}, bf16[128,1024]{1,0:T(8,128)(2,1)}, u32[]{:S(2)}) copy-start(bf16[128,1024]{1,0:T(8,128)(2,1)} %param.10) | copy-start | bytes 786436
  7.2 1.8 copy-start.9
  7.2 66.5 %all-gather.11.cloned.1.call-start = ((), (), s32[]{:S(2)}) async-start(), calls=%async_computation.5 | async-start | bytes 10027008 | tf_op jit(solution)/shard_map/all_gather | solution.py:39
  7.2 1.8 copy-start.10
  9.0 2.2 copy-start.4
  9.1 2.3 copy-start.7
  9.1 3.1 copy-start.8
  11.3 2.4 copy-start.6
  11.3 121.3 %all-gather.7.cloned.1.call-start = ((), (), s32[]{:S(2)}) async-start(), calls=%async_computation.3 | async-start | bytes 1671168 | tf_op jit(solution)/shard_map/all_gather | solution.py:71
  12.1 177.2 %all-gather.9.cloned.1.call-start = ((), (), s32[]{:S(2)}) async-start(), calls=%async_computation.4 | async-start | bytes 1671168 | tf_op jit(solution)/shard_map/all_gather | solution.py:72
  13.0 344.3 %all-reduce.2.cloned.1.call-start = ((), (), s32[]{:S(2)}) async-start(), calls=%async_computation.2 | async-start | bytes 2359296 | tf_op jit(solution)/shard_map/psum | solution.py:69
  13.6 60.2 %copy-start.11 = (f32[4608]{0:T(1024)S(1)}, f32[4608]{0:T(1024)}, u32[]{:S(2)}) copy-start(f32[4608]{0:T(1024)} %param.11) | copy-start | bytes 55300
  13.6 552.9 %reduce-scatter.2.cloned.1.call-start = ((), (), s32[]{:S(2)}) async-start(), calls=%async_computation.1 | async-start | bytes 20054016 | tf_op jit(solution)/shard_map/reduce_scatter | solution.py:43
  357.3 3.2 copy-start.5
  362.2 204.3 %copy-start.1 = (f32[1,288,1024]{2,1,0:T(8,128)S(1)}, f32[1,288,1024]{2,1,0:T(8,128)}, u32[]{:S(2)}) copy-start(f32[1,288,1024]{2,1,0:T(8,128)} %copy.29) | copy-start | bytes 3538948
  362.2 204.3 %copy-start.2 = (bf16[1,1,288,1024]{3,2,1,0:T(8,128)(2,1)S(1)}, bf16[1,1,288,1024]{3,2,1,0:T(8,128)(2,1)}, u32[]{:S(2)}) copy-start(bf16[1,1,288,1024]{3,2,1,0:T(8,128)(2,1)} %get-tuple-element.29) | copy-start | bytes 1769476
  571.0 2.7 copy-start.3
Sparse Core Ops, SparseCore 0:
  11.4 62.3 all-gather.10
  76.7 55.7 all-gather.6
  135.6 53.6 all-gather.8
  192.4 164.9 all-reduce.1
  359.7 206.7 reduce-scatter.1
where the time goes:
time: 587 us; the launch traced here: 584 us
  waiting for transfers between devices  521 us (89%)
  local copies, waits for them, and re-layouts  17.6 us (3%)
  matrix products  16 us (3%)
  between operations  14.7 us (3%)
  other arithmetic  14.3 us (2%)
    reduce_scatter x1, waiting for transfers between devices, local(): lax.psum_scatter(lax.dot_general(normed, key_cotangent, (((0,), (0,)), ((...  202 us
    psum x1, waiting for transfers between devices, local(): whole_sum = lax.psum(snapshot, 'replica')  163 us
    all_gather x1, waiting for transfers between devices, local(): lax.all_gather(local_w, 'fsdp', axis=0, tiled=True)  59.4 us
    all_gather x1, waiting for transfers between devices, local(): lax.all_gather(mom_slot, 'replica', axis=1, tiled=True)  53.2 us
    all_gather x1, waiting for transfers between devices, local(): lax.all_gather(glob_slot, 'replica', axis=1, tiled=True)  42.7 us
  transfers between devices with their start and end apart: 5, of which 5 were waited for; matrix products, arithmetic and copies ran while one was open for 6% of the time, Pallas kernels for 0%

commit v1 on v0

v1 whole, which is shorter than its diff:
```python
import jax
import jax.numpy as jnp
from jax import lax
from jax.sharding import PartitionSpec as P

FRAGS = 4


beta_first = 0.9
beta_second = 0.95
inner_rate = 0.004
warmup_steps = 4096.0
weight_decay = 0.1
outer_rate = 0.7
outer_mom = 0.9
mix_share = 0.5
norm_eps = 1e-06
adam_eps = 1e-08


def pack(share):
    rows, width = share.shape
    return share.reshape(2, rows // 2, width).transpose(1, 0, 2).reshape(rows // 2, 2 * width)


def unpack(packed):
    half, width = packed.shape
    return packed.reshape(half, 2, width // 2).transpose(1, 0, 2).reshape(2 * half, width // 2)


def local(
    hidden,
    key_cotangent,
    norm_gain,
    weights,
    adam_first,
    adam_second,
    inner_step,
    outer_global,
    outer_momentum,
):
    replicas = lax.axis_size("replica")
    shards = lax.axis_size("fsdp")
    tokens, width = hidden.shape
    rows = weights.shape[2]
    kv = weights.shape[3]
    share = kv // replicas
    frag_index = inner_step % FRAGS
    local_w = lax.dynamic_index_in_dim(weights[0], frag_index, 0, keepdims=False)
    glob_slot = lax.dynamic_index_in_dim(outer_global, frag_index, 0, keepdims=False)
    mom_slot = lax.dynamic_index_in_dim(outer_momentum, frag_index, 0, keepdims=False)

    cot_all = lax.all_gather(key_cotangent, "fsdp", axis=0)

    pieces = (
        local_w.reshape(2, rows // 2, replicas, share)
        .transpose(2, 1, 0, 3)
        .reshape(replicas, rows // 2, 2 * share)
    )
    pieces = lax.all_to_all(pieces, "replica", 0, 0, tiled=True)
    total = jnp.sum(pieces.astype(jnp.float32), axis=0)
    glob_packed = pack(glob_slot)
    pseudo = glob_packed - total / replicas
    momentum_packed = outer_mom * pack(mom_slot) + pseudo
    global_packed = glob_packed - outer_rate * (pseudo + outer_mom * momentum_packed)
    global_all = lax.all_gather(global_packed, "replica", axis=0)
    global_full = (
        global_all.reshape(replicas, rows // 2, 2, share)
        .transpose(2, 1, 0, 3)
        .reshape(rows, kv)
    )

    rows_f = hidden.astype(jnp.float32)
    inverse = lax.rsqrt(jnp.mean(rows_f * rows_f, axis=1, keepdims=True) + norm_eps)
    normed = (rows_f * inverse * norm_gain).astype(jnp.bfloat16)
    normed_t = normed.T.reshape(shards, rows, tokens)
    normed_t = lax.all_to_all(normed_t, "fsdp", 0, 0, tiled=True)
    grad = lax.dot_general(
        normed_t.transpose(1, 0, 2).reshape(rows, shards * tokens),
        cot_all.reshape(shards * tokens, kv),
        (((1,), (0,)), ((), ())),
        preferred_element_type=jnp.float32,
    )

    back_t = lax.dot_general(
        local_w,
        cot_all.reshape(shards * tokens, kv),
        (((1,), (1,)), ((), ())),
        preferred_element_type=jnp.float32,
    )
    back_t = back_t.reshape(rows, shards, tokens).transpose(1, 0, 2)
    back_t = lax.all_to_all(back_t, "fsdp", 0, 0, tiled=True)
    back = back_t.reshape(width, tokens).T
    scaled = norm_gain * back
    project = jnp.mean(scaled * rows_f, axis=1, keepdims=True)
    hidden_grad = (inverse * scaled - rows_f * inverse * inverse * inverse * project).astype(
        jnp.bfloat16
    )
    counter = inner_step.astype(jnp.float32)
    step_rate = inner_rate * jnp.minimum(jnp.float32(1.0), counter / warmup_steps)
    first_next = beta_first * adam_first[0] + (1.0 - beta_first) * grad
    second_next = beta_second * adam_second[0] + (1.0 - beta_second) * grad * grad
    first_hat = first_next / (1.0 - jnp.power(jnp.float32(beta_first), counter))
    second_hat = second_next / (1.0 - jnp.power(jnp.float32(beta_second), counter))
    snapshot = local_w.astype(jnp.float32)
    updated = snapshot - step_rate * (
        first_hat / (jnp.sqrt(second_hat) + adam_eps) + weight_decay * snapshot
    )
    merged = (mix_share * updated + (1.0 - mix_share) * global_full).astype(jnp.bfloat16)
    layers_out = lax.dynamic_update_index_in_dim(weights[0], merged, frag_index, 0)
    new_global = lax.dynamic_update_index_in_dim(
        outer_global, unpack(global_packed), frag_index, 0
    )
    new_momentum = lax.dynamic_update_index_in_dim(
        outer_momentum, unpack(momentum_packed), frag_index, 0
    )
    return (
        layers_out[None],
        hidden_grad,
        first_next[None],
        second_next[None],
        new_global,
        new_momentum,
    )


def solution(mesh):
    in_specs = (
        P(("replica", "fsdp"), None),
        P(("replica", "fsdp"), None),
        P(),
        P("replica", None, "fsdp", None),
        P("replica", "fsdp", None),
        P("replica", "fsdp", None),
        P(),
        P(None, "fsdp", "replica"),
        P(None, "fsdp", "replica"),
    )
    out_specs = (
        P("replica", None, "fsdp", None),
        P(("replica", "fsdp"), None),
        P("replica", "fsdp", None),
        P("replica", "fsdp", None),
        P(None, "fsdp", "replica"),
        P(None, "fsdp", "replica"),
    )
    return jax.shard_map(local, mesh=mesh, in_specs=in_specs, out_specs=out_specs, check_vma=False)
```

time: 587 us -> 161 us (0.27)
  waiting for transfers between devices: 521 us -> 78.8 us
  starting transfers between devices: 0.2 us -> 21.3 us
  other arithmetic: 14.3 us -> 7.18 us
    reduce_scatter x1 -> x0, waiting for transfers between devices: 202 us -> none  [local(): lax.psum_scatter(lax.dot_general(normed, key_cotangent, (((0,), (0,)), ((...]
    psum x1 -> x0, waiting for transfers between devices: 163 us -> none  [local(): whole_sum = lax.psum(snapshot, 'replica')]
    all_gather x3 -> x2, waiting for transfers between devices: 155 us -> 48 us  [the longest x1 37.9 us: local(): cot_all = lax.all_gather(key_cotangent, 'fsdp', axis=0)]
    all_to_all x0 -> x3, waiting for transfers between devices: none -> 30.7 us  [the longest x1 29.5 us: local(): back_t = lax.all_to_all(back_t, 'fsdp', 0, 0, tiled=True)]
    all_to_all x0 -> x3, starting transfers between devices: none -> 21.2 us  [the longest x1 11.4 us: local(): pieces = lax.all_to_all(pieces, 'replica', 0, 0, tiled=True)]
    reshape x0 -> x8, local copies, waits for them, and re-layouts: none -> 9.3 us  [the longest x1 2.66 us: local(): global_all.reshape(replicas, rows // 2, 2, share).transpose(2, 1, 0, 3)]
    all_gather x2 -> x0, local copies, waits for them, and re-layouts: 8.31 us -> none  [the longest x1 4.75 us: local(): lax.all_gather(mom_slot, 'replica', axis=1, tiled=True)]
    transpose x0 -> x5, local copies, waits for them, and re-layouts: none -> 6.61 us  [the longest x1 2.82 us: local(): global_full = global_all.reshape(replicas, rows // 2, 2, share).transpose...]
  transfers between devices with their start and end apart: 5 -> 5, of which waited for: 5 -> 4; matrix products, arithmetic and copies ran while one was open for 6% -> 18% of each run, Pallas kernels for 0% -> 0%
where the time goes in v1:
time: 161 us; the launch traced here: 158 us
  waiting for transfers between devices  78.8 us (49%)
  local copies, waits for them, and re-layouts  22.8 us (14%)
  starting transfers between devices  21.3 us (13%)
  between operations  16.5 us (10%)
  matrix products  11.2 us (7%)
  other arithmetic  7.18 us (4%)
    all_gather x1, waiting for transfers between devices, local(): cot_all = lax.all_gather(key_cotangent, 'fsdp', axis=0)  37.9 us
    all_to_all x1, waiting for transfers between devices, local(): back_t = lax.all_to_all(back_t, 'fsdp', 0, 0, tiled=True)  29.5 us
    all_to_all x1, starting transfers between devices, local(): pieces = lax.all_to_all(pieces, 'replica', 0, 0, tiled=True)  11.4 us
    all_gather x1, waiting for transfers between devices, local(): global_all = lax.all_gather(global_packed, 'replica', axis=0)  10.1 us
    dot_general x1, matrix products, local(): lax.dot_general(normed_t.transpose(1, 0, 2).reshape(rows, shards * tokens...  6.13 us
    dot_general x1, matrix products, local(): lax.dot_general(local_w, cot_all.reshape(shards * tokens, kv), (((1,), (1...  5.07 us
    all_to_all x1, starting transfers between devices, local(): normed_t = lax.all_to_all(normed_t, 'fsdp', 0, 0, tiled=True)  5.02 us
    unnamed x35, local copies, waits for them, and re-layouts  4.88 us
  transfers between devices with their start and end apart: 5, of which 4 were waited for; matrix products, arithmetic and copies ran while one was open for 18% of the time, Pallas kernels for 0%

profile of v1, /device:TPU:14, one launch (start us, length us, event | category | flops | bytes accessed | tf_op | source)
XLA Modules:
  0.0 157.7 jit_solution(3992001954476223835)
XLA Ops:
  8.1 1.7 %copy.60 = bf16[1,4,288,1024]{3,2,1,0:T(8,128)(2,1)S(1)} copy(bf16[1,4,288,1024]{3,2,1,0:T(8,128)(2,1)} %param.12) | data formatting | bytes 4718592
  9.8 0.8 copy.61
  10.6 0.9 copy.62
  13.0 1.2 copy.38
  14.2 1.4 reshape.140
  15.6 11.4 %all-to-all-start.1 = ((bf16[16,144,128]{2,1,0:T(8,128)(2,1)}), bf16[16,144,128]{2,1,0:T(8,128)(2,1)S(1)}, u32[]{:S(2)}, u32[]{:S(2)}) async-start(bf16[16,144,128]{2,1,0:T(8,128)(2,1)} %reshape.140), calls=%async_computation.1 | async-start | bytes 1179648 | tf_op jit(solution)/shard_map/all_to_all | solution.py:60
  27.0 37.9 %all-gather.6.cloned.1.call-done = bf16[2048,1024]{1,0:T(8,128)(2,1)} async-done(((bf16[128,1024]{1,0:T(8,128)(2,1)}), bf16[2048,1024]{1,0:T(8,128)(2,1)}) %all-gather.6.cloned.1.call-update) | async-done | bytes 4194320 | tf_op jit(solution)/shard_map/all_gather | solution.py:53
  64.9 5.1 %convolution_bitcast_fusion = f32[16,288,128]{2,1,0:T(8,128)} fusion(bf16[16,128,1024]{2,1,0:T(8,128)(2,1)} %bitcast.99, bf16[1,1,288,1024]{3,2,1,0:T(8,128)(2,1)S(1)} %constant_dynamic-slice_fusion.1), kind=kOutput, calls=%fused_computation.14 | convolution fusion | flops 1207959552 | bytes 7143424 | tf_op jit(solution)/shard_map/dot_general | solution.py:85
  69.9 4.8 %all-to-all-start.2 = ((f32[16,288,128]{2,1,0:T(8,128)}), f32[16,288,128]{2,1,0:T(8,128)S(1)}, u32[]{:S(2)}, u32[]{:S(2)}) async-start(f32[16,288,128]{2,1,0:T(8,128)} %convolution_bitcast_fusion), calls=%async_computation.2 | async-start | bytes 4718592 | tf_op jit(solution)/shard_map/all_to_all | solution.py:92
  74.8 1.0 dynamic-slice_multiply_fusion
  77.1 29.5 %all-to-all-done.2 = f32[16,288,128]{2,1,0:T(8,128)S(1)} async-done(((f32[16,288,128]{2,1,0:T(8,128)}), f32[16,288,128]{2,1,0:T(8,128)S(1)}, u32[]{:S(2)}, u32[]{:S(2)}) %all-to-all-start.2) | async-done | bytes 2359328 | tf_op jit(solution)/shard_map/all_to_all | solution.py:92
  106.6 1.4 copy-done
  108.0 2.1 %copy.42 = f32[4608,128]{0,1:T(8,128)S(1)} copy(f32[4608,128]{1,0:T(8,128)} %bitcast.93) | data formatting | bytes 4718592 | tf_op jit(solution)/shard_map/reshape | solution.py:93
  110.2 1.3 fusion.8
  111.5 2.3 %fusion.6 = (bf16[128,4608]{1,0:T(8,128)(2,1)}, bf16[4608,128]{0,1:T(8,128)(2,1)}) fusion(bf16[128,4608]{1,0:T(8,128)(2,1)S(1)} %copy-done.1, f32[4608,128]{0,1:T(8,128)S(1)} %copy.42, f32[128]{0:T(128)S(1)} %get-tuple-element.19, f32[4608]{0:T(1024)S(1)} %copy-done.15, f32[128]{0:T(128)S(1)} %get-tuple-element.18), kind=kLoop, calls=%fused_computation.9 | loop fusion | flops 6488064 | bytes 5917696 | tf_op jit(solution)/shard_map/convert_element_type | solution.py:96
  113.8 2.4 %copy.35 = bf16[4608,128]{1,0:T(8,128)(2,1)} copy(bf16[4608,128]{0,1:T(8,128)(2,1)} %get-tuple-element.9) | data formatting | bytes 2359296 | tf_op jit(solution)/shard_map/transpose | solution.py:76
  116.2 5.0 %all-to-all-start = ((bf16[16,288,128]{2,1,0:T(8,128)(2,1)}), bf16[16,288,128]{2,1,0:T(8,128)(2,1)S(1)}, u32[]{:S(2)}, u32[]{:S(2)}) async-start(bf16[16,288,128]{2,1,0:T(8,128)(2,1)} %bitcast.3), calls=%async_computation | async-start | bytes 2359296 | tf_op jit(solution)/shard_map/all_to_all | solution.py:77
  123.3 10.1 %all-gather.4.cloned.1.call-done = f32[16,144,128]{2,1,0:T(8,128)} async-done(((f32[1,144,128]{2,1,0:T(8,128)}), f32[16,144,128]{2,1,0:T(8,128)}) %all-gather.4.cloned.1.call-update) | async-done | bytes 1179664 | tf_op jit(solution)/shard_map/all_gather | solution.py:66
  133.4 2.7 %reshape.141 = f32[16,144,2,64]{3,2,1,0:T(2,128)S(1)} reshape(f32[16,144,128]{2,1,0:T(8,128)} %all-gather.4.cloned.1.call-done) | data formatting | bytes 2359296 | tf_op jit(solution)/shard_map/reshape | solution.py:68
  136.1 2.8 %copy.41 = f32[2,144,16,64]{3,2,1,0:T(8,128)} copy(f32[2,144,16,64]{3,0,1,2:T(2,128)S(1)} %bitcast.94) | data formatting | bytes 2359296 | tf_op jit(solution)/shard_map/transpose | solution.py:69
  138.9 2.1 %reshape.142 = f32[288,1024]{1,0:T(8,128)S(1)} reshape(f32[2,144,16,64]{3,2,1,0:T(8,128)} %copy.41) | data formatting | bytes 2359296 | tf_op jit(solution)/shard_map/reshape | solution.py:70
  141.1 1.3 all-to-all-done
  142.3 6.1 %bitcast_dynamic-update-slice_fusion = (bf16[1,4,288,1024]{3,2,1,0:T(8,128)(2,1)}, f32[288,1024]{1,0:T(8,128)S(1)}) fusion(bf16[1,4,288,1024]{3,2,1,0:T(8,128)(2,1)} %copy-done.2, s32[]{:T(128)S(6)} %select_n.20, f32[288,1024]{1,0:T(8,128)S(1)} %reshape.142, f32[]{:T(128)S(6)} %sub.40, f32[]{:T(128)S(6)} %sub.39, f32[]{:T(128)S(6)} %mul_shard_map.3, ...), kind=kOutput, calls=%fused_computation.29 | convolution fusion | flops 1213562880 | bytes 11272208 | tf_op jit(solution)/shard_map/dot_general | solution.py:78
  148.5 1.8 %fusion.19 = (f32[1,288,1024]{2,1,0:T(8,128)}, f32[1,288,1024]{2,1,0:T(8,128)}) fusion(f32[288,1024]{1,0:T(8,128)S(1)} %get-tuple-element.15, f32[1,288,1024]{2,1,0:T(8,128)S(1)} %copy-done.10, f32[1,288,1024]{2,1,0:T(8,128)S(1)} %copy-done.9), kind=kLoop, calls=%fused_computation.31 | loop fusion | flops 2064384 | bytes 5898240 | tf_op jit(solution)/shard_map/broadcast_in_dim | solution.py:121
  (56 shorter events, 4.1 us)
Async XLA Ops:
  8.0 1.8 %copy-start.13 = (f32[4,288,64]{1,2,0:T(8,128)S(1)}, f32[4,288,64]{1,2,0:T(8,128)}, u32[]{:S(2)}) copy-start(f32[4,288,64]{1,2,0:T(8,128)} %param.16) | copy-start | bytes 884740
  8.0 2.6 %copy-start.14 = (f32[4,288,64]{1,2,0:T(8,128)S(1)}, f32[4,288,64]{1,2,0:T(8,128)}, u32[]{:S(2)}) copy-start(f32[4,288,64]{1,2,0:T(8,128)} %param.17) | copy-start | bytes 884740
  8.0 56.9 %all-gather.6.cloned.1.call-start = ((), (), s32[]{:S(2)}) async-start(), calls=%async_computation.4 | async-start | bytes 4456448 | tf_op jit(solution)/shard_map/all_gather | solution.py:53
  9.8 2.3 %copy-start.2 = (bf16[1,4,288,1024]{3,2,1,0:T(8,128)(2,1)}, bf16[1,4,288,1024]{3,2,1,0:T(8,128)(2,1)S(1)}, u32[]{:S(2)}) copy-start(bf16[1,4,288,1024]{3,2,1,0:T(8,128)(2,1)S(1)} %copy.60) | copy-start | bytes 7077892
  12.2 52.7 %copy-start.3 = (bf16[1,1,288,1024]{3,2,1,0:T(8,128)(2,1)}, bf16[1,1,288,1024]{3,2,1,0:T(8,128)(2,1)S(1)}, u32[]{:S(2)}) copy-start(bf16[1,1,288,1024]{3,2,1,0:T(8,128)(2,1)S(1)} %constant_dynamic-slice_fusion.1) | copy-start | bytes 1769476
  15.6 54.4 %all-to-all-start.1 = ((bf16[16,144,128]{2,1,0:T(8,128)(2,1)}), bf16[16,144,128]{2,1,0:T(8,128)(2,1)S(1)}, u32[]{:S(2)}, u32[]{:S(2)}) async-start(bf16[16,144,128]{2,1,0:T(8,128)(2,1)} %reshape.140), calls=%async_computation.1 | async-start | bytes 1179648 | tf_op jit(solution)/shard_map/all_to_all | solution.py:60
  69.9 36.6 %all-to-all-start.2 = ((f32[16,288,128]{2,1,0:T(8,128)}), f32[16,288,128]{2,1,0:T(8,128)S(1)}, u32[]{:S(2)}, u32[]{:S(2)}) async-start(f32[16,288,128]{2,1,0:T(8,128)} %convolution_bitcast_fusion), calls=%async_computation.2 | async-start | bytes 4718592 | tf_op jit(solution)/shard_map/all_to_all | solution.py:92
  74.7 58.7 %all-gather.4.cloned.1.call-start = ((), (), s32[]{:S(2)}) async-start(), calls=%async_computation.3 | async-start | bytes 1253376 | tf_op jit(solution)/shard_map/all_gather | solution.py:66
  75.9 30.6 %copy-start.5 = (f32[2,144,64]{1,0,2:T(2,128)}, f32[2,144,64]{1,0,2:T(2,128)S(1)}, u32[]{:S(2)}) copy-start(f32[2,144,64]{1,0,2:T(2,128)S(1)} %mul.179) | copy-start | bytes 221188
  76.1 30.5 %copy-start.7 = (f32[2,144,64]{1,0,2:T(2,128)}, f32[2,144,64]{1,0,2:T(2,128)S(1)}, u32[]{:S(2)}) copy-start(f32[2,144,64]{1,0,2:T(2,128)S(1)} %reshape.137) | copy-start | bytes 221188
  76.4 30.2 %copy-start.11 = (f32[144,128]{1,0:T(8,128)}, f32[144,128]{1,0:T(8,128)S(1)}, u32[]{:S(2)}) copy-start(f32[144,128]{1,0:T(8,128)S(1)} %convert_reduce_fusion) | copy-start | bytes 221188
  106.6 1.5 copy-start
  108.0 2.1 %copy-start.1 = (bf16[128,4608]{1,0:T(8,128)(2,1)S(1)}, bf16[128,4608]{1,0:T(8,128)(2,1)}, u32[]{:S(2)}) copy-start(bf16[128,4608]{1,0:T(8,128)(2,1)} %param.9) | copy-start | bytes 3538948
  110.2 1.4 copy-start.15
  116.2 5.1 %copy-start.12 = (f32[144,128]{1,0:T(8,128)S(1)}, f32[144,128]{1,0:T(8,128)}, u32[]{:S(2)}) copy-start(f32[144,128]{1,0:T(8,128)} %copy-done.11) | copy-start | bytes 221188
  116.2 5.2 %copy-start.6 = (f32[2,144,64]{1,0,2:T(2,128)S(1)}, f32[2,144,64]{1,0,2:T(2,128)}, u32[]{:S(2)}) copy-start(f32[2,144,64]{1,0,2:T(2,128)} %copy-done.5) | copy-start | bytes 221188
  116.2 5.3 %copy-start.8 = (f32[2,144,64]{1,0,2:T(2,128)S(1)}, f32[2,144,64]{1,0,2:T(2,128)}, u32[]{:S(2)}) copy-start(f32[2,144,64]{1,0,2:T(2,128)} %copy-done.7) | copy-start | bytes 221188
  116.2 26.2 %all-to-all-start = ((bf16[16,288,128]{2,1,0:T(8,128)(2,1)}), bf16[16,288,128]{2,1,0:T(8,128)(2,1)S(1)}, u32[]{:S(2)}, u32[]{:S(2)}) async-start(bf16[16,288,128]{2,1,0:T(8,128)(2,1)} %bitcast.3), calls=%async_computation | async-start | bytes 2359296 | tf_op jit(solution)/shard_map/all_to_all | solution.py:77
  138.9 3.4 %copy-start.4 = (bf16[1,1,288,1024]{3,2,1,0:T(8,128)(2,1)S(1)}, bf16[1,1,288,1024]{3,2,1,0:T(8,128)(2,1)}, u32[]{:S(2)}) copy-start(bf16[1,1,288,1024]{3,2,1,0:T(8,128)(2,1)} %copy-done.3) | copy-start | bytes 1769476
  142.3 6.1 %copy-start.9 = (f32[1,288,1024]{2,1,0:T(8,128)S(1)}, f32[1,288,1024]{2,1,0:T(8,128)}, u32[]{:S(2)}) copy-start(f32[1,288,1024]{2,1,0:T(8,128)} %param.13) | copy-start | bytes 3538948
  142.3 6.1 %copy-start.10 = (f32[1,288,1024]{2,1,0:T(8,128)S(1)}, f32[1,288,1024]{2,1,0:T(8,128)}, u32[]{:S(2)}) copy-start(f32[1,288,1024]{2,1,0:T(8,128)} %param.14) | copy-start | bytes 3538948
Sparse Core Ops, SparseCore 0:
  11.6 53.2 all-gather.5
Sparse Core Ops, SparseCore 1:
  77.6 55.7 all-gather.3

commit v2 on v0

v2 whole, which is shorter than its diff:
```python
import jax
import jax.numpy as jnp
from jax import lax
from jax.experimental import pallas as pl
from jax.experimental.pallas import tpu as pltpu
from jax.sharding import PartitionSpec as P

FRAGS = 4
NY = 4
NX = 4
NH = 4

beta_first = 0.9
beta_second = 0.95
inner_rate = 0.004
warmup_steps = 4096.0
weight_decay = 0.1
outer_rate = 0.7
outer_mom = 0.9
mix_share = 0.5
norm_eps = 1e-06
adam_eps = 1e-08

BF = jnp.bfloat16
F32 = jnp.float32
LIMIT = 60 * 1024 * 1024


def shape(dims, dtype):
    return jax.ShapeDtypeStruct(dims, dtype)


def whole(dims):
    return pl.BlockSpec(dims, lambda *_: (0,) * len(dims))


def call(kernel, name, outs, operands, scratch=(), flops=0):
    moved = sum(a.size * a.dtype.itemsize for a in tuple(operands[1:]) + tuple(outs))
    return pl.pallas_call(
        kernel,
        grid_spec=pltpu.PrefetchScalarGridSpec(
            num_scalar_prefetch=1,
            grid=(1,),
            in_specs=[whole(a.shape) for a in operands[1:]],
            out_specs=[whole(o.shape) for o in outs],
            scratch_shapes=list(scratch),
        ),
        out_shape=list(outs),
        compiler_params=pltpu.CompilerParams(vmem_limit_bytes=LIMIT),
        cost_estimate=pl.CostEstimate(flops=flops, bytes_accessed=moved, transcendentals=0),
        name=name,
    )(*operands)


def fsdp_move(array, dz, dc):
    return lax.ppermute(array, "fsdp", [(i, i ^ (dz * 2 + dc)) for i in range(4 * NY)])


def fsdp_trade(array, over_z):
    if over_z:
        groups = [[i * 2 + c for i in range(2 * NY)] for c in range(2)]
    else:
        groups = [[y * 4 + i for y in range(NY)] for i in range(4)]
    return lax.all_to_all(array, "fsdp", 0, 0, axis_index_groups=groups, tiled=True)


def replica_move(array, dh):
    pairs = [(i, (i // NX + dh) % NH * NX + i % NX) for i in range(NH * NX)]
    return lax.ppermute(array, "replica", pairs)


def replica_trade(array):
    groups = [[h * NX + x for x in range(NX)] for h in range(NH)]
    return lax.all_to_all(array, "replica", 0, 0, axis_index_groups=groups, tiled=True)


def lane_half(block_shape):
    return lax.broadcasted_iota(jnp.int32, block_shape, 1) < 64


def pick_kernel(pos, w_ref, slot_ref, out):
    slot_ref[...] = w_ref[0]
    half = w_ref.shape[1] // 2
    left = lane_half((half, 128))
    for q in range(w_ref.shape[2] // 128):
        block = w_ref[0, :, q * 128 : (q + 1) * 128].astype(F32)
        top, bottom = block[:half], block[half:]
        h, x = 2 * q // NX, 2 * q % NX
        out[x, h] = jnp.where(left, top, pltpu.roll(bottom, 64, 1)).astype(BF)
        out[x + 1, h] = jnp.where(left, pltpu.roll(top, 64, 1), bottom).astype(BF)


def pick(pos, weights):
    _, rows, kv = weights.shape
    piece = (NX, NH, rows // 2, 128)
    return pl.pallas_call(
        pick_kernel,
        grid_spec=pltpu.PrefetchScalarGridSpec(
            num_scalar_prefetch=1,
            grid=(1,),
            in_specs=[pl.BlockSpec((1, rows, kv), lambda i, pos: (pos[0], 0, 0))],
            out_specs=[whole((rows, kv)), whole(piece)],
        ),
        out_shape=[shape((rows, kv), BF), shape(piece, BF)],
        compiler_params=pltpu.CompilerParams(vmem_limit_bytes=LIMIT),
        cost_estimate=pl.CostEstimate(flops=0, bytes_accessed=6 * rows * kv, transcendentals=0),
        name="pick",
    )(pos, weights)


def keep_kernel(w_ref, out):
    out[...] = w_ref[...]


def keep(weights):
    block = pl.BlockSpec((1,) + weights.shape[1:], lambda i: (i, 0, 0))
    return pl.pallas_call(
        keep_kernel,
        grid=(weights.shape[0],),
        in_specs=[block],
        out_specs=block,
        out_shape=shape(weights.shape, BF),
        compiler_params=pltpu.CompilerParams(vmem_limit_bytes=LIMIT),
        cost_estimate=pl.CostEstimate(flops=0, bytes_accessed=4 * weights.size, transcendentals=0),
        name="keep",
    )(weights)


def sum_x_kernel(pos, pieces, *outs):
    for k in range(NH):
        h = lax.rem(pos[2] + k, NH)
        a, b, c, d = (pieces[x, h].astype(F32) for x in range(NX))
        outs[k][...] = (a + b) + (c + d)


def outer_kernel(pos, a, b, c, d, glob, mom, new_glob, new_mom, sent):
    frag = pos[0]
    total = ((a[...] + b[...]) + (c[...] + d[...])).T
    total = jnp.concatenate([total[:64], total[64:]], axis=1)
    new_glob[...] = glob[...]
    new_mom[...] = mom[...]
    slot = glob[frag]
    pseudo = slot - total / (NX * NH)
    momentum = outer_mom * mom[frag] + pseudo
    updated = slot - outer_rate * (pseudo + outer_mom * momentum)
    new_glob[frag] = updated
    new_mom[frag] = momentum
    half = total.shape[1] // 2
    sent[...] = jnp.concatenate([updated[:, :half], updated[:, half:]], axis=0).T


def stack_kernel(pos, a, b, c, d, out):
    for k, piece in enumerate((a, b, c, d)):
        h = lax.rem(pos[2] + NH - k, NH)
        for x in range(NX):
            out[x, h] = piece[...]


def norm_kernel(pos, hidden, gain, out, inv_out):
    width = hidden.shape[1]
    total = jnp.zeros((hidden.shape[0], 128), F32)
    for j in range(width // 128):
        block = hidden[:, j * 128 : (j + 1) * 128].astype(F32)
        total = total + block * block
    mean = jnp.sum(total, axis=1, keepdims=True) / width
    inverse = lax.rsqrt(mean + norm_eps)
    inv_out[...] = jnp.broadcast_to(inverse, inv_out.shape)
    for j in range(width // 128):
        at = slice(j * 128, (j + 1) * 128)
        block = hidden[:, at].astype(F32) * inverse * gain[:, at]
        out[at, :] = block.T.astype(BF)


def back_kernel(pos, w0, wz, wc, wzc, cots, out, turned):
    rows, depth = w0.shape
    tokens = cots.shape[1]
    for y in range(NY):
        for j in range(depth // 128):
            at = slice(j * 128, (j + 1) * 128)
            turned[at, y * tokens : (y + 1) * tokens] = cots[y, :, at].T
    for pair in range(NY // 2):
        cot = turned[:, 2 * pair * tokens : (2 * pair + 2) * tokens]
        for dz, dc, w in ((0, 0, w0), (0, 1, wc), (1, 0, wz), (1, 1, wzc)):
            start = (jnp.bitwise_xor(pos[4], dz) * 2 + jnp.bitwise_xor(pos[5], dc)) * rows
            at = pl.ds(pl.multiple_of(start, 32), rows)
            both = jnp.dot(w[...], cot, preferred_element_type=F32)
            out[2 * pair, at, :] = both[:, :tokens]
            out[2 * pair + 1, at, :] = both[:, tokens:]


def hidden_kernel(pos, hidden, gain, inv, backs, out, scratch):
    width = hidden.shape[1]
    total = jnp.zeros((hidden.shape[0], 128), F32)
    for j in range(width // 128):
        at = slice(j * 128, (j + 1) * 128)
        scaled = gain[:, at] * backs[at, :].T
        total = total + scaled * hidden[:, at].astype(F32)
        scratch[:, at] = scaled
    project = jnp.sum(total, axis=1, keepdims=True) / width
    inverse = inv[...]
    factor = inverse * inverse * inverse * project
    for j in range(width // 128):
        at = slice(j * 128, (j + 1) * 128)
        out[:, at] = (inverse * scratch[:, at] - hidden[:, at].astype(F32) * factor).astype(BF)


def token_sum(pos, normed, cots, cots_z, start, rows, at):
    left = [normed[2 * y + pos[4], pl.ds(start, rows), :] for y in range(NY)]
    left += [normed[2 * y + 1 - pos[4], pl.ds(start, rows), :] for y in range(NY)]
    right = [cots[y, :, at] for y in range(NY)] + [cots_z[y, :, at] for y in range(NY)]
    return jnp.dot(
        jnp.concatenate(left, axis=1), jnp.concatenate(right, axis=0), preferred_element_type=F32
    )


def other_kernel(pos, normed, cots, cots_z, out):
    rows, kv = out.shape
    start = pl.multiple_of((1 - pos[5]) * rows, 16)
    for j in range(kv // 256):
        at = slice(j * 256, (j + 1) * 256)
        out[:, at] = token_sum(pos, normed, cots, cots_z, start, rows, at)


def adam_kernel(
    pos, rates, normed, cots, cots_z, theirs, slot, first, second, shares, _, out, first_out, second_out
):
    rows = theirs.shape[0]
    half = rows // 2
    start = pl.multiple_of(pos[5] * rows, 16)
    grad = token_sum(pos, normed, cots, cots_z, start, rows, slice(None)) + theirs[...]
    first_next = beta_first * first[...] + (1.0 - beta_first) * grad
    second_next = beta_second * second[...] + (1.0 - beta_second) * grad * grad
    first_out[...] = first_next
    second_out[...] = second_next
    snapshot = slot[...].astype(F32)
    updated = snapshot - rates[0] * (
        (first_next / rates[1]) / (jnp.sqrt(second_next / rates[2]) + adam_eps)
        + weight_decay * snapshot
    )
    left = lane_half((half, 128))
    for x in range(0, NX, 2):
        at = slice(x * 64, x * 64 + 128)
        a, b = shares[x, 0], shares[x + 1, 0]
        top = jnp.where(left, a, pltpu.roll(b, 64, 1))
        bottom = jnp.where(left, pltpu.roll(a, 64, 1), b)
        out[0, :half, at] = (mix_share * updated[:half, at] + (1.0 - mix_share) * top).astype(BF)
        out[0, half:, at] = (mix_share * updated[half:, at] + (1.0 - mix_share) * bottom).astype(BF)


def adam(pos, rates, normed, cots, cots_z, theirs, slot, first, second, shares, weights):
    rows, kv = theirs.shape
    wide = kv // NH
    column = pl.BlockSpec((rows, wide), lambda i, *_: (0, i))
    cot_block = pl.BlockSpec(cots.shape[:2] + (wide,), lambda i, *_: (0, 0, i))
    share_block = pl.BlockSpec((NX, 1) + shares.shape[2:], lambda i, *_: (0, i, 0, 0))
    return pl.pallas_call(
        adam_kernel,
        grid_spec=pltpu.PrefetchScalarGridSpec(
            num_scalar_prefetch=2,
            grid=(NH,),
            in_specs=[whole(normed.shape), cot_block, cot_block]
            + [column] * 4
            + [share_block, pl.BlockSpec(memory_space=pl.ANY)],
            out_specs=[
                pl.BlockSpec((1, rows, wide), lambda i, pos, rates: (pos[0], 0, i)),
                column,
                column,
            ],
        ),
        out_shape=[shape(weights.shape, BF), shape((rows, kv), F32), shape((rows, kv), F32)],
        input_output_aliases={10: 0},
        compiler_params=pltpu.CompilerParams(vmem_limit_bytes=LIMIT),
        cost_estimate=pl.CostEstimate(
            flops=rows * kv * 2048, bytes_accessed=rows * kv * 28, transcendentals=0
        ),
        name="adam",
    )(pos, rates, normed, cots, cots_z, theirs, slot, first, second, shares, weights)


def local(
    hidden,
    key_cotangent,
    norm_gain,
    weights,
    adam_first,
    adam_second,
    inner_step,
    outer_global,
    outer_momentum,
):
    tokens, width = hidden.shape
    rows, kv = weights.shape[2:]
    frag_index = inner_step % FRAGS
    replica = lax.axis_index("replica")
    place = lax.axis_index("fsdp")
    pos = jnp.stack(
        [frag_index, replica % NX, replica // NX, place // 4, (place // 2) % 2, place % 2]
    ).astype(jnp.int32)
    counter = inner_step.astype(F32)
    rates = jnp.stack(
        [
            inner_rate * jnp.minimum(F32(1.0), counter / warmup_steps),
            1.0 - jnp.power(F32(beta_first), counter),
            1.0 - jnp.power(F32(beta_second), counter),
        ]
    )
    gain = norm_gain[None]

    cots = fsdp_trade(jnp.broadcast_to(key_cotangent[None], (NY, tokens, kv)), False)
    slot, pieces = pick(pos, weights[0])
    w_z = fsdp_move(slot, 1, 0)
    w_c = fsdp_move(slot, 0, 1)
    w_zc = fsdp_move(w_z, 0, 1)
    pieces = replica_trade(pieces)
    normed, inv = call(
        norm_kernel,
        "norm",
        [shape((width, tokens), BF), shape((tokens, 128), F32)],
        (pos, hidden, gain),
    )
    normed = fsdp_trade(normed.reshape(2 * NY, 2 * rows, tokens), True)

    (backs,) = call(
        back_kernel,
        "back_product",
        [shape((NY, 4 * rows, tokens), F32)],
        (pos, slot, w_z, w_c, w_zc, cots),
        scratch=[pltpu.VMEM((kv, NY * tokens), BF)],
        flops=2 * 4 * rows * kv * NY * tokens,
    )
    backs = fsdp_trade(backs, False).reshape(width, tokens)
    (hidden_grad,) = call(
        hidden_kernel,
        "hidden_back",
        [shape(hidden.shape, BF)],
        (pos, hidden, gain, inv, backs),
        scratch=[pltpu.VMEM(hidden.shape, F32)],
    )

    packed = shape((rows // 2, 128), F32)
    parts = call(sum_x_kernel, "sum_x", [packed] * NH, (pos, pieces))
    parts = [parts[0]] + [replica_move(parts[d], d) for d in range(1, NH)]
    turned = [jnp.swapaxes(a, 1, 2) for a in (outer_global, outer_momentum)]
    new_global, new_momentum, share = call(
        outer_kernel,
        "outer",
        [shape(turned[0].shape, F32), shape(turned[0].shape, F32), packed],
        (pos, *parts, *turned),
    )
    shares = [share] + [replica_move(share, d) for d in range(1, NH)]
    (shares,) = call(stack_kernel, "stack", [shape((NX, NH) + packed.shape, F32)], (pos, *shares))
    shares = replica_trade(shares)

    cots_z = fsdp_move(cots, 1, 0)
    (theirs,) = call(
        other_kernel,
        "other_half",
        [shape((rows, kv), F32)],
        (pos, normed, cots, cots_z),
        flops=rows * kv * 2048,
    )
    theirs = fsdp_move(theirs, 0, 1)
    layers_out, first_next, second_next = adam(
        pos,
        rates,
        normed,
        cots,
        cots_z,
        theirs,
        slot,
        adam_first[0],
        adam_second[0],
        shares,
        keep(weights[0]),
    )
    return (
        layers_out[None],
        hidden_grad,
        first_next[None],
        second_next[None],
        jnp.swapaxes(new_global, 1, 2),
        jnp.swapaxes(new_momentum, 1, 2),
    )


def solution(mesh):
    in_specs = (
        P(("replica", "fsdp"), None),
        P(("replica", "fsdp"), None),
        P(),
        P("replica", None, "fsdp", None),
        P("replica", "fsdp", None),
        P("replica", "fsdp", None),
        P(),
        P(None, "fsdp", "replica"),
        P(None, "fsdp", "replica"),
    )
    out_specs = (
        P("replica", None, "fsdp", None),
        P(("replica", "fsdp"), None),
        P("replica", "fsdp", None),
        P("replica", "fsdp", None),
        P(None, "fsdp", "replica"),
        P(None, "fsdp", "replica"),
    )
    return jax.shard_map(local, mesh=mesh, in_specs=in_specs, out_specs=out_specs, check_vma=False)
```

time: 587 us -> 181 us (0.31)
  waiting for transfers between devices: 521 us -> 72 us
  starting transfers between devices: 0.2 us -> 42.8 us
  Pallas kernels: 0 us -> 40.7 us
  matrix products: 16 us -> 0 us
  other arithmetic: 14.3 us -> 0.6 us
  between operations: 14.7 us -> 1.49 us
  blocking collectives: 0 us -> 13.2 us
  local copies, waits for them, and re-layouts: 17.6 us -> 7.99 us
    reduce_scatter x1 -> x0, waiting for transfers between devices: 202 us -> none  [local(): lax.psum_scatter(lax.dot_general(normed, key_cotangent, (((0,), (0,)), ((...]
    psum x1 -> x0, waiting for transfers between devices: 163 us -> none  [local(): whole_sum = lax.psum(snapshot, 'replica')]
    all_gather x3 -> x0, waiting for transfers between devices: 155 us -> none  [the longest x1 59.4 us: local(): lax.all_gather(local_w, 'fsdp', axis=0, tiled=True)]
    ppermute x0 -> x11, waiting for transfers between devices: none -> 58.4 us  [the longest x5 50.3 us: fsdp_move(): lax.ppermute(array, 'fsdp', [(i, i ^ dz * 2 + dc) for i in range(4 * NY)])]
    pallas_call x0 -> x10, Pallas kernels: none -> 40.7 us  [the longest x7 26.6 us: call(): pl.pallas_call(kernel, grid_spec=pltpu.PrefetchScalarGridSpec(num_scalar_...]
    ppermute x0 -> x11, starting transfers between devices: none -> 21.7 us  [the longest x6 20.1 us: replica_move(): return lax.ppermute(array, 'replica', pairs)]
    all_to_all x0 -> x4, starting transfers between devices: none -> 21.1 us  [the longest x3 15.5 us: fsdp_trade(): lax.all_to_all(array, 'fsdp', 0, 0, axis_index_groups=groups, tiled=True)]
    dot_general x2 -> x0, matrix products: 16 us -> none  [the longest x1 8.27 us: local(): lax.dot_general(normed, key_cotangent, (((0,), (0,)), ((), ())), preferre...]
  transfers between devices with their start and end apart: 5 -> 15, of which waited for: 5 -> 9; matrix products, arithmetic and copies ran while one was open for 6% -> 1% of each run, Pallas kernels for 0% -> 17%
where the time goes in v2:
time: 181 us; the launch traced here: 179 us
  waiting for transfers between devices  72 us (40%)
  starting transfers between devices  42.8 us (24%)
  Pallas kernels  40.7 us (22%)
  blocking collectives  13.2 us (7%)
  local copies, waits for them, and re-layouts  7.99 us (4%)
    ppermute x5, waiting for transfers between devices, fsdp_move(): lax.ppermute(array, 'fsdp', [(i, i ^ dz * 2 + dc) for i in range(4 * NY)])  50.3 us
    pallas_call x7, Pallas kernels, call(): pl.pallas_call(kernel, grid_spec=pltpu.PrefetchScalarGridSpec(num_scalar_...  26.6 us
    ppermute x6, starting transfers between devices, replica_move(): return lax.ppermute(array, 'replica', pairs)  20.1 us
    all_to_all x3, starting transfers between devices, fsdp_trade(): lax.all_to_all(array, 'fsdp', 0, 0, axis_index_groups=groups, tiled=True)  15.5 us
    all_to_all x1, blocking collectives, replica_trade(): lax.all_to_all(array, 'replica', 0, 0, axis_index_groups=groups, tiled=True)  13.2 us
    all_to_all x3, waiting for transfers between devices, fsdp_trade(): lax.all_to_all(array, 'fsdp', 0, 0, axis_index_groups=groups, tiled=True)  8.31 us
    ppermute x6, waiting for transfers between devices, replica_move(): return lax.ppermute(array, 'replica', pairs)  8.15 us
    pallas_call x1, Pallas kernels, adam(): pl.pallas_call(adam_kernel, grid_spec=pltpu.PrefetchScalarGridSpec(num_sc...  7.17 us
  transfers between devices with their start and end apart: 15, of which 9 were waited for; matrix products, arithmetic and copies ran while one was open for 1% of the time, Pallas kernels for 17%

profile of v2, /device:TPU:14, one launch (start us, length us, event | category | flops | bytes accessed | tf_op | source)
XLA Modules:
  0.0 178.7 jit_solution(882669908276539765)
XLA Ops:
  1.9 3.0 %pick.1 = (bf16[288,1024]{1,0:T(8,128)(2,1)}, bf16[4,4,144,128]{3,2,1,0:T(8,128)(2,1)}) custom-call(s32[6]{0:T(128)} %stack.40.pos, bf16[4,288,1024]{2,1,0:T(8,128)(2,1)} %bitcast.21), custom_call_target="tpu_custom_call" | custom-call | bytes 1769472 | tf_op jit(solution)/shard_map/pick/pallas_call | solution.py:96
  4.9 13.2 %all_to_all.25.pieces = bf16[4,4,144,128]{3,2,1,0:T(8,128)(2,1)} all-to-all(bf16[4,4,144,128]{3,2,1,0:T(8,128)(2,1)} %get-tuple-element.22), channel_id=1, replica_groups={{0,16,32,48},{64,80,96,112},{128,144,160,176},{192,208,224,240},{1,17,3..., dimensions={0} | all-to-all | bytes 1179648 | tf_op jit(solution)/shard_map/all_to_all | solution.py:74
  19.2 5.0 %all-to-all-start.1 = ((bf16[4,128,1024]{2,1,0:T(8,128)(2,1)}), bf16[4,128,1024]{2,1,0:T(8,128)(2,1)S(1)}, u32[]{:S(2)}, u32[]{:S(2)}) async-start(bf16[4,128,1024]{2,1,0:T(8,128)(2,1)} %broadcast_in_dim.19), calls=%async_computation.1 | async-start | bytes 2097152 | tf_op jit(solution)/shard_map/all_to_all | solution.py:64
  24.9 3.6 %norm.1 = (bf16[4608,128]{1,0:T(8,128)(2,1)}, f32[128,128]{1,0:T(8,128)}) custom-call(s32[6]{0:T(128)} %stack.40.pos, bf16[128,4608]{1,0:T(8,128)(2,1)} %hidden.3, f32[1,4608]{1,0:T(1,128)} %broadcast_in_dim.18.gain), custom_call_target="tpu_custom_call" | custom-call | bytes 2443264 | tf_op jit(solution)/shard_map/norm/pallas_call | solution.py:39
  28.5 8.3 %all-to-all-done.1.cots = bf16[4,128,1024]{2,1,0:T(8,128)(2,1)S(1)} async-done(((bf16[4,128,1024]{2,1,0:T(8,128)(2,1)}), bf16[4,128,1024]{2,1,0:T(8,128)(2,1)S(1)}, u32[]{:S(2)}, u32[]{:S(2)}) %all-to-all-start.1) | async-done | bytes 1048608 | tf_op jit(solution)/shard_map/all_to_all | solution.py:64
  37.8 5.3 %all-to-all-start = ((bf16[8,576,128]{2,1,0:T(8,128)(2,1)}), bf16[8,576,128]{2,1,0:T(8,128)(2,1)S(1)}, u32[]{:S(2)}, u32[]{:S(2)}) async-start(bf16[8,576,128]{2,1,0:T(8,128)(2,1)} %bitcast.24), calls=%async_computation | async-start | bytes 2359296 | tf_op jit(solution)/shard_map/all_to_all | solution.py:64
  44.5 23.4 %collective-permute-done.8.wz = bf16[288,1024]{1,0:T(8,128)(2,1)S(1)} collective-permute-done((bf16[288,1024]{1,0:T(8,128)(2,1)S(1)}, bf16[288,1024]{1,0:T(8,128)(2,1)S(1)}, u32[]{:S(2)}, u32[]{:S(2)}) %collective-permute-start.8) | collective-permute-done | bytes 589856 | tf_op jit(solution)/shard_map/ppermute | solution.py:56
  70.0 5.5 %back_product.1 = f32[4,1152,128]{2,1,0:T(8,128)} custom-call(s32[6]{0:T(128)} %stack.40.pos, bf16[288,1024]{1,0:T(8,128)(2,1)} %get-tuple-element.21.slot.w0, bf16[288,1024]{1,0:T(8,128)(2,1)} %copy-done.7, bf16[288,1024]{1,0:T(8,128)(2,1)} %copy-done.8, bf16[288,1024]{1,0:T(8,128)(2,1)} %collective-permute-done.10.wzc, bf16[4,128,1024]{2,1,0:T(8,128)(2,1)} %copy-done), custom_call_target="tpu_custom_call" | custom-call | flops 1207959552 | bytes 5767168 | tf_op jit(solution)/shard_map/back_product/pallas_call | solution.py:39
  76.6 5.2 %all-to-all-start.4 = ((f32[4,1152,128]{2,1,0:T(8,128)}), f32[4,1152,128]{2,1,0:T(8,128)}, u32[]{:S(2)}, u32[]{:S(2)}) async-start(f32[4,1152,128]{2,1,0:T(8,128)} %back_product.1), calls=%async_computation.4 | async-start | bytes 4718592 | tf_op jit(solution)/shard_map/all_to_all | solution.py:64
  82.0 24.8 %collective-permute-done.cots_z = bf16[4,128,1024]{2,1,0:T(8,128)(2,1)S(1)} collective-permute-done((bf16[4,128,1024]{2,1,0:T(8,128)(2,1)S(1)}, bf16[4,128,1024]{2,1,0:T(8,128)(2,1)S(1)}, u32[]{:S(2)}, u32[]{:S(2)}) %collective-permute-start) | collective-permute-done | bytes 1048608 | tf_op jit(solution)/shard_map/ppermute | solution.py:56
  107.8 4.4 %other_half.1 = f32[288,1024]{1,0:T(8,128)} custom-call(s32[6]{0:T(128)} %stack.40.pos, bf16[8,576,128]{2,1,0:T(8,128)(2,1)} %copy-done.2, bf16[4,128,1024]{2,1,0:T(8,128)(2,1)} %copy-done, bf16[4,128,1024]{2,1,0:T(8,128)(2,1)} %copy-done.4), custom_call_target="tpu_custom_call" | custom-call | flops 603979776 | bytes 4456448 | tf_op jit(solution)/shard_map/other_half/pallas_call | solution.py:39
  114.6 3.3 %collective-permute-start.2 = (f32[144,128]{1,0:T(8,128)}, f32[144,128]{1,0:T(8,128)S(1)}, u32[]{:S(2)}, u32[]{:S(2)}) collective-permute-start(f32[144,128]{1,0:T(8,128)} %get-tuple-element.24), channel_id=1, source_target_pairs={{0,64},{16,80},{32,96},{48,112},{64,128},{80,144},{96,160},{112,17... | collective-permute-start | bytes 221192 | tf_op jit(solution)/shard_map/ppermute | solution.py:69
  117.8 5.2 %collective-permute-start.3 = (f32[144,128]{1,0:T(8,128)}, f32[144,128]{1,0:T(8,128)S(1)}, u32[]{:S(2)}, u32[]{:S(2)}) collective-permute-start(f32[144,128]{1,0:T(8,128)} %get-tuple-element.25), channel_id=1, source_target_pairs={{0,128},{16,144},{32,160},{48,176},{64,192},{80,208},{96,224},{112... | collective-permute-start | bytes 221192 | tf_op jit(solution)/shard_map/ppermute | solution.py:69
  123.1 2.7 %collective-permute-start.4 = (f32[144,128]{1,0:T(8,128)}, f32[144,128]{1,0:T(8,128)S(1)}, u32[]{:S(2)}, u32[]{:S(2)}) collective-permute-start(f32[144,128]{1,0:T(8,128)} %get-tuple-element.26), channel_id=1, source_target_pairs={{0,192},{16,208},{32,224},{48,240},{64,0},{80,16},{96,32},{112,48}... | collective-permute-start | bytes 221192 | tf_op jit(solution)/shard_map/ppermute | solution.py:69
  125.7 4.4 %collective-permute-done.3.c = f32[144,128]{1,0:T(8,128)S(1)} collective-permute-done((f32[144,128]{1,0:T(8,128)}, f32[144,128]{1,0:T(8,128)S(1)}, u32[]{:S(2)}, u32[]{:S(2)}) %collective-permute-start.3) | collective-permute-done | bytes 73760 | tf_op jit(solution)/shard_map/ppermute | solution.py:69
  131.1 3.0 %outer.1 = (f32[4,64,288]{2,1,0:T(8,128)}, f32[4,64,288]{2,1,0:T(8,128)}, f32[144,128]{1,0:T(8,128)}) custom-call(s32[6]{0:T(128)} %stack.40.pos, f32[144,128]{1,0:T(8,128)} %get-tuple-element.23.a, f32[144,128]{1,0:T(8,128)} %copy-done.10, f32[144,128]{1,0:T(8,128)} %copy-done.11, f32[144,128]{1,0:T(8,128)} %copy-done.12, f32[4,64,288]{2,1,0:T(8,128)} %bitcast.27, ...), custom_call_target="tpu_custom_call" | custom-call | bytes 1548288 | tf_op jit(solution)/shard_map/outer/pallas_call | solution.py:39
  136.3 3.8 %collective-permute-start.6 = (f32[144,128]{1,0:T(8,128)}, f32[144,128]{1,0:T(8,128)S(1)}, u32[]{:S(2)}, u32[]{:S(2)}) collective-permute-start(f32[144,128]{1,0:T(8,128)} %get-tuple-element.27.a), channel_id=1, source_target_pairs={{0,128},{16,144},{32,160},{48,176},{64,192},{80,208},{96,224},{112... | collective-permute-start | bytes 221192 | tf_op jit(solution)/shard_map/ppermute | solution.py:69
  140.1 2.9 %collective-permute-start.7 = (f32[144,128]{1,0:T(8,128)}, f32[144,128]{1,0:T(8,128)S(1)}, u32[]{:S(2)}, u32[]{:S(2)}) collective-permute-start(f32[144,128]{1,0:T(8,128)} %get-tuple-element.27.a), channel_id=1, source_target_pairs={{0,192},{16,208},{32,224},{48,240},{64,0},{80,16},{96,32},{112,48}... | collective-permute-start | bytes 221192 | tf_op jit(solution)/shard_map/ppermute | solution.py:69
  147.0 2.7 %stack.45 = f32[4,4,144,128]{3,2,1,0:T(8,128)} custom-call(s32[6]{0:T(128)} %stack.40.pos, f32[144,128]{1,0:T(8,128)} %get-tuple-element.27.a, f32[144,128]{1,0:T(8,128)} %copy-done.13, f32[144,128]{1,0:T(8,128)} %copy-done.14, f32[144,128]{1,0:T(8,128)} %copy-done.15), custom_call_target="tpu_custom_call" | custom-call | bytes 1474560 | tf_op jit(solution)/shard_map/stack/pallas_call | solution.py:39
  149.8 5.6 %all-to-all-start.3 = ((f32[4,4,144,128]{3,2,1,0:T(8,128)}), f32[4,4,144,128]{3,2,1,0:T(8,128)S(1)}, u32[]{:S(2)}, u32[]{:S(2)}) async-start(f32[4,4,144,128]{3,2,1,0:T(8,128)} %stack.45), calls=%async_computation.3 | async-start | bytes 2359296 | tf_op jit(solution)/shard_map/all_to_all | solution.py:74
  155.4 3.9 %keep.1._ = bf16[4,288,1024]{2,1,0:T(8,128)(2,1)} custom-call(bf16[4,288,1024]{2,1,0:T(8,128)(2,1)} %bitcast.22), custom_call_target="tpu_custom_call" | custom-call | bytes 4718592 | tf_op jit(solution)/shard_map/keep/pallas_call | solution.py:117
  159.9 4.9 %hidden_back.1 = bf16[128,4608]{1,0:T(8,128)(2,1)} custom-call(s32[6]{0:T(128)} %stack.40.pos, bf16[128,4608]{1,0:T(8,128)(2,1)} %hidden.3, f32[1,4608]{1,0:T(1,128)} %broadcast_in_dim.18.gain, f32[128,128]{1,0:T(8,128)} %get-tuple-element.29.inv, f32[4608,128]{1,0:T(8,128)} %bitcast.16.backs), custom_call_target="tpu_custom_call" | custom-call | bytes 4802560 | tf_op jit(solution)/shard_map/hidden_back/pallas_call | solution.py:39
  164.8 5.2 %all-to-all-done.3.shares = f32[4,4,144,128]{3,2,1,0:T(8,128)S(1)} async-done(((f32[4,4,144,128]{3,2,1,0:T(8,128)}), f32[4,4,144,128]{3,2,1,0:T(8,128)S(1)}, u32[]{:S(2)}, u32[]{:S(2)}) %all-to-all-start.3) | async-done | bytes 1179680 | tf_op jit(solution)/shard_map/all_to_all | solution.py:74
  171.5 7.2 %adam.1 = (bf16[4,288,1024]{2,1,0:T(8,128)(2,1)}, f32[288,1024]{1,0:T(8,128)}, f32[288,1024]{1,0:T(8,128)}) custom-call(s32[6]{0:T(128)} %stack.40.pos, f32[3]{0:T(128)} %pad_maximum_fusion.rates, bf16[8,576,128]{2,1,0:T(8,128)(2,1)} %copy-done.2, bf16[4,128,1024]{2,1,0:T(8,128)(2,1)} %copy-done, ...), custom_call_target="tpu_custom_call", output_to_operand_aliasing={{0}: (10, {})} | custom-call | flops 603979776 | bytes 8257536 | tf_op jit(solution)/shard_map/adam/pallas_call | solution.py:256
  (55 shorter events, 20.6 us)
Async XLA Ops:
  4.9 13.2 %copy-start.9 = (bf16[128,1024]{1,0:T(8,128)(2,1)S(1)}, bf16[128,1024]{1,0:T(8,128)(2,1)}, u32[]{:S(2)}) copy-start(bf16[128,1024]{1,0:T(8,128)(2,1)} %param.10) | copy-start | bytes 786436
  19.2 5.0 %copy-start.16 = (f32[4608]{0:T(1024)S(1)}, f32[4608]{0:T(1024)}, u32[]{:S(2)}) copy-start(f32[4608]{0:T(1024)} %param.11) | copy-start | bytes 55300
  19.2 17.6 %all-to-all-start.1 = ((bf16[4,128,1024]{2,1,0:T(8,128)(2,1)}), bf16[4,128,1024]{2,1,0:T(8,128)(2,1)S(1)}, u32[]{:S(2)}, u32[]{:S(2)}) async-start(bf16[4,128,1024]{2,1,0:T(8,128)(2,1)} %broadcast_in_dim.19), calls=%async_computation.1 | async-start | bytes 2097152 | tf_op jit(solution)/shard_map/all_to_all | solution.py:64
  36.8 6.2 %copy-start.5 = (bf16[288,1024]{1,0:T(8,128)(2,1)S(1)}, bf16[288,1024]{1,0:T(8,128)(2,1)}, u32[]{:S(2)}) copy-start(bf16[288,1024]{1,0:T(8,128)(2,1)} %get-tuple-element.21.slot.w0) | copy-start | bytes 1769476
  37.8 37.8 %all-to-all-start = ((bf16[8,576,128]{2,1,0:T(8,128)(2,1)}), bf16[8,576,128]{2,1,0:T(8,128)(2,1)S(1)}, u32[]{:S(2)}, u32[]{:S(2)}) async-start(bf16[8,576,128]{2,1,0:T(8,128)(2,1)} %bitcast.24), calls=%async_computation | async-start | bytes 2359296 | tf_op jit(solution)/shard_map/all_to_all | solution.py:64
  43.1 24.8 %collective-permute-start.8 = (bf16[288,1024]{1,0:T(8,128)(2,1)S(1)}, bf16[288,1024]{1,0:T(8,128)(2,1)S(1)}, u32[]{:S(2)}, u32[]{:S(2)}) collective-permute-start(bf16[288,1024]{1,0:T(8,128)(2,1)S(1)} %copy-done.5), channel_id=1, source_target_pairs={{0,2},{1,3},{2,0},{3,1},{4,6},{5,7},{6,4},{7,5},{8,10},{9,11},{10,... | collective-permute-start | bytes 1769480 | tf_op jit(solution)/shard_map/ppermute | solution.py:56
  44.5 23.4 %collective-permute-start.9 = (bf16[288,1024]{1,0:T(8,128)(2,1)S(1)}, bf16[288,1024]{1,0:T(8,128)(2,1)S(1)}, u32[]{:S(2)}, u32[]{:S(2)}) collective-permute-start(bf16[288,1024]{1,0:T(8,128)(2,1)S(1)} %copy-done.5), channel_id=1, source_target_pairs={{0,1},{1,0},{2,3},{3,2},{4,5},{5,4},{6,7},{7,6},{8,9},{9,8},{10,11... | collective-permute-start | bytes 1769480 | tf_op jit(solution)/shard_map/ppermute | solution.py:56
  67.9 2.1 %copy-start.7 = (bf16[288,1024]{1,0:T(8,128)(2,1)}, bf16[288,1024]{1,0:T(8,128)(2,1)S(1)}, u32[]{:S(2)}) copy-start(bf16[288,1024]{1,0:T(8,128)(2,1)S(1)} %collective-permute-done.8.wz) | copy-start | bytes 1769476
  67.9 2.1 %collective-permute-start.10 = (bf16[288,1024]{1,0:T(8,128)(2,1)S(1)}, bf16[288,1024]{1,0:T(8,128)(2,1)}, u32[]{:S(2)}, u32[]{:S(2)}) collective-permute-start(bf16[288,1024]{1,0:T(8,128)(2,1)S(1)} %collective-permute-done.8.wz), channel_id=1, source_target_pairs={{0,1},{1,0},{2,3},{3,2},{4,5},{5,4},{6,7},{7,6},{8,9},{9,8},{10,11... | collective-permute-start | bytes 1769480 | tf_op jit(solution)/shard_map/ppermute | solution.py:56
  67.9 2.1 %copy-start.8 = (bf16[288,1024]{1,0:T(8,128)(2,1)}, bf16[288,1024]{1,0:T(8,128)(2,1)S(1)}, u32[]{:S(2)}) copy-start(bf16[288,1024]{1,0:T(8,128)(2,1)S(1)} %collective-permute-done.9.wc) | copy-start | bytes 1769476
  75.6 6.2 %copy-start.1 = (bf16[4,128,1024]{2,1,0:T(8,128)(2,1)S(1)}, bf16[4,128,1024]{2,1,0:T(8,128)(2,1)}, u32[]{:S(2)}) copy-start(bf16[4,128,1024]{2,1,0:T(8,128)(2,1)} %copy-done) | copy-start | bytes 3145732
  76.6 73.2 %all-to-all-start.4 = ((f32[4,1152,128]{2,1,0:T(8,128)}), f32[4,1152,128]{2,1,0:T(8,128)}, u32[]{:S(2)}, u32[]{:S(2)}) async-start(f32[4,1152,128]{2,1,0:T(8,128)} %back_product.1), calls=%async_computation.4 | async-start | bytes 4718592 | tf_op jit(solution)/shard_map/all_to_all | solution.py:64
  81.8 24.9 %collective-permute-start = (bf16[4,128,1024]{2,1,0:T(8,128)(2,1)S(1)}, bf16[4,128,1024]{2,1,0:T(8,128)(2,1)S(1)}, u32[]{:S(2)}, u32[]{:S(2)}) collective-permute-start(bf16[4,128,1024]{2,1,0:T(8,128)(2,1)S(1)} %copy-done.1), channel_id=1, source_target_pairs={{0,2},{1,3},{2,0},{3,1},{4,6},{5,7},{6,4},{7,5},{8,10},{9,11},{10,... | collective-permute-start | bytes 3145736 | tf_op jit(solution)/shard_map/ppermute | solution.py:56
  112.1 58.0 %collective-permute-start.1 = (f32[288,1024]{1,0:T(8,128)}, f32[288,1024]{1,0:T(8,128)S(1)}, u32[]{:S(2)}, u32[]{:S(2)}) collective-permute-start(f32[288,1024]{1,0:T(8,128)} %other_half.1), channel_id=1, source_target_pairs={{0,1},{1,0},{2,3},{3,2},{4,5},{5,4},{6,7},{7,6},{8,9},{9,8},{10,11... | collective-permute-start | bytes 3538952 | tf_op jit(solution)/shard_map/ppermute | solution.py:56
  114.6 11.2 %collective-permute-start.2 = (f32[144,128]{1,0:T(8,128)}, f32[144,128]{1,0:T(8,128)S(1)}, u32[]{:S(2)}, u32[]{:S(2)}) collective-permute-start(f32[144,128]{1,0:T(8,128)} %get-tuple-element.24), channel_id=1, source_target_pairs={{0,64},{16,80},{32,96},{48,112},{64,128},{80,144},{96,160},{112,17... | collective-permute-start | bytes 221192 | tf_op jit(solution)/shard_map/ppermute | solution.py:69
  117.8 12.3 %collective-permute-start.3 = (f32[144,128]{1,0:T(8,128)}, f32[144,128]{1,0:T(8,128)S(1)}, u32[]{:S(2)}, u32[]{:S(2)}) collective-permute-start(f32[144,128]{1,0:T(8,128)} %get-tuple-element.25), channel_id=1, source_target_pairs={{0,128},{16,144},{32,160},{48,176},{64,192},{80,208},{96,224},{112... | collective-permute-start | bytes 221192 | tf_op jit(solution)/shard_map/ppermute | solution.py:69
  123.1 7.5 %collective-permute-start.4 = (f32[144,128]{1,0:T(8,128)}, f32[144,128]{1,0:T(8,128)S(1)}, u32[]{:S(2)}, u32[]{:S(2)}) collective-permute-start(f32[144,128]{1,0:T(8,128)} %get-tuple-element.26), channel_id=1, source_target_pairs={{0,192},{16,208},{32,224},{48,240},{64,0},{80,16},{96,32},{112,48}... | collective-permute-start | bytes 221192 | tf_op jit(solution)/shard_map/ppermute | solution.py:69
  125.7 4.8 %copy-start.10 = (f32[144,128]{1,0:T(8,128)}, f32[144,128]{1,0:T(8,128)S(1)}, u32[]{:S(2)}) copy-start(f32[144,128]{1,0:T(8,128)S(1)} %collective-permute-done.2.b) | copy-start | bytes 221188
  134.1 8.9 %collective-permute-start.5 = (f32[144,128]{1,0:T(8,128)}, f32[144,128]{1,0:T(8,128)S(1)}, u32[]{:S(2)}, u32[]{:S(2)}) collective-permute-start(f32[144,128]{1,0:T(8,128)} %get-tuple-element.27.a), channel_id=1, source_target_pairs={{0,64},{16,80},{32,96},{48,112},{64,128},{80,144},{96,160},{112,17... | collective-permute-start | bytes 221192 | tf_op jit(solution)/shard_map/ppermute | solution.py:69
  136.3 9.4 %collective-permute-start.6 = (f32[144,128]{1,0:T(8,128)}, f32[144,128]{1,0:T(8,128)S(1)}, u32[]{:S(2)}, u32[]{:S(2)}) collective-permute-start(f32[144,128]{1,0:T(8,128)} %get-tuple-element.27.a), channel_id=1, source_target_pairs={{0,128},{16,144},{32,160},{48,176},{64,192},{80,208},{96,224},{112... | collective-permute-start | bytes 221192 | tf_op jit(solution)/shard_map/ppermute | solution.py:69
  140.1 6.3 %collective-permute-start.7 = (f32[144,128]{1,0:T(8,128)}, f32[144,128]{1,0:T(8,128)S(1)}, u32[]{:S(2)}, u32[]{:S(2)}) collective-permute-start(f32[144,128]{1,0:T(8,128)} %get-tuple-element.27.a), channel_id=1, source_target_pairs={{0,192},{16,208},{32,224},{48,240},{64,0},{80,16},{96,32},{112,48}... | collective-permute-start | bytes 221192 | tf_op jit(solution)/shard_map/ppermute | solution.py:69
  143.0 3.4 %copy-start.13 = (f32[144,128]{1,0:T(8,128)}, f32[144,128]{1,0:T(8,128)S(1)}, u32[]{:S(2)}) copy-start(f32[144,128]{1,0:T(8,128)S(1)} %collective-permute-done.5.b) | copy-start | bytes 221188
  149.8 20.3 %all-to-all-start.3 = ((f32[4,4,144,128]{3,2,1,0:T(8,128)}), f32[4,4,144,128]{3,2,1,0:T(8,128)S(1)}, u32[]{:S(2)}, u32[]{:S(2)}) async-start(f32[4,4,144,128]{3,2,1,0:T(8,128)} %stack.45), calls=%async_computation.3 | async-start | bytes 2359296 | tf_op jit(solution)/shard_map/all_to_all | solution.py:74
  170.1 1.4 copy-start.6
  (8 other events, 6.7 us)

commit v3 on v2

v3 whole, which is shorter than its diff:
```python
import functools

import jax
import jax.numpy as jnp
from jax import lax
from jax.experimental import pallas as pl
from jax.experimental.pallas import tpu as pltpu
from jax.sharding import PartitionSpec as P

FRAGS = 4
NY = 4
NX = 4
NH = 4

beta_first = 0.9
beta_second = 0.95
inner_rate = 0.004
warmup_steps = 4096.0
weight_decay = 0.1
outer_rate = 0.7
outer_mom = 0.9
mix_share = 0.5
norm_eps = 1e-06
adam_eps = 1e-08

BF = jnp.bfloat16
F32 = jnp.float32
LIMIT = 20 * 1024 * 1024
MEAN_SHARE = outer_rate * (1.0 + outer_mom) / (NX * NH)


def shape(dims, dtype):
    return jax.ShapeDtypeStruct(dims, dtype)


def in_hbm(array):
    return pltpu.with_memory_space_constraint(array, pltpu.HBM)


def whole(dims):
    return pl.BlockSpec(dims, lambda *_: (0,) * len(dims))


def call(kernel, name, outs, operands, scratch=()):
    return pl.pallas_call(
        kernel,
        grid_spec=pltpu.PrefetchScalarGridSpec(
            num_scalar_prefetch=1,
            grid=(1,),
            in_specs=[whole(a.shape) for a in operands[1:]],
            out_specs=[whole(o.shape) for o in outs],
            scratch_shapes=list(scratch),
        ),
        out_shape=list(outs),
        compiler_params=pltpu.CompilerParams(vmem_limit_bytes=LIMIT),
        name=name,
    )(*operands)


def fsdp_move(array, dz, dc):
    return lax.ppermute(array, "fsdp", [(i, i ^ (dz * 2 + dc)) for i in range(4 * NY)])


def fsdp_trade(array):
    groups = [[y * 4 + i for y in range(NY)] for i in range(4)]
    return lax.all_to_all(array, "fsdp", 0, 0, axis_index_groups=groups, tiled=True)


def replica_turn(array, dx):
    pairs = [(i, i // NX * NX + (i % NX + dx) % NX) for i in range(NH * NX)]
    return lax.ppermute(array, "replica", pairs)


def replica_swap(array, step):
    pairs = []
    for replica in range(NH * NX):
        for place in range(4 * NY):
            flip = (1, 3)[(step + place) % 2]
            pairs.append((replica * 4 * NY + place, (replica ^ (flip * NX)) * 4 * NY + place))
    return lax.ppermute(array, ("replica", "fsdp"), pairs)


def after(pos, done):
    return lax.optimization_barrier((pos, done))


def lane_half(block_shape):
    return lax.broadcasted_iota(jnp.int32, block_shape, 1) < 64


def pick_kernel(pos, w_ref, slot_ref, *outs):
    outs, pieces = outs[:NX], outs[NX]
    slot_ref[...] = w_ref[0]
    half = w_ref.shape[1] // 2
    left = lane_half((half, 128))
    for q in range(w_ref.shape[2] // 128):
        block = w_ref[0, :, q * 128 : (q + 1) * 128].astype(F32)
        top, bottom = block[:half], block[half:]
        h, x = 2 * q // NX, 2 * q % NX
        pieces[x, h] = jnp.where(left, top, pltpu.roll(bottom, 64, 1)).astype(BF)
        pieces[x + 1, h] = jnp.where(left, pltpu.roll(top, 64, 1), bottom).astype(BF)
    for d in range(NX):
        outs[d][...] = pieces[lax.rem(pos[1] + d, NX)]


def pick(pos, weights):
    _, rows, kv = weights.shape
    piece = (NH, rows // 2, 128)
    return pl.pallas_call(
        pick_kernel,
        grid_spec=pltpu.PrefetchScalarGridSpec(
            num_scalar_prefetch=1,
            grid=(1,),
            in_specs=[pl.BlockSpec((1, rows, kv), lambda i, pos: (pos[0], 0, 0))],
            out_specs=[whole((rows, kv))] + [whole(piece)] * NX,
            scratch_shapes=[pltpu.VMEM((NX,) + piece, BF)],
        ),
        out_shape=[pltpu.HBM((rows, kv), BF)] + [shape(piece, BF)] * NX,
        compiler_params=pltpu.CompilerParams(vmem_limit_bytes=LIMIT),
        name="pick",
    )(pos, in_hbm(weights))


def keep_kernel(pos, w_ref, out):
    out[...] = w_ref[...]


def keep(pos, weights):
    block = pl.BlockSpec((1,) + weights.shape[1:], lambda i, pos: (i, 0, 0))
    return pl.pallas_call(
        keep_kernel,
        grid_spec=pltpu.PrefetchScalarGridSpec(
            num_scalar_prefetch=1,
            grid=(weights.shape[0],),
            in_specs=[block],
            out_specs=block,
        ),
        out_shape=shape(weights.shape, BF),
        compiler_params=pltpu.CompilerParams(vmem_limit_bytes=LIMIT),
        name="keep",
    )(pos, in_hbm(weights))


def stepped(slot, mom, mean):
    pseudo = slot - mean
    momentum = outer_mom * mom + pseudo
    return slot - outer_rate * (pseudo + outer_mom * momentum), momentum


def sum_x_kernel(pos, a, b, c, d, glob, mom, out):
    for h in range(NH):
        total = (a[h].astype(F32) + b[h].astype(F32)) + (c[h].astype(F32) + d[h].astype(F32))
        out[h] = MEAN_SHARE * total
    updated, _ = stepped(glob[pos[0]], mom[pos[0]], 0.0)
    half = updated.shape[1] // 2
    updated = jnp.concatenate([updated[:, :half], updated[:, half:]], axis=0).T
    out[pos[2]] = out[pos[2]] + updated


def pair_kernel(pos, a, b, out):
    out[...] = a[...] + b[...]


def outer_kernel(pos, totals, glob, mom, new_glob, new_mom):
    frag = pos[0]
    updated = totals[pos[2]].T
    updated = jnp.concatenate([updated[:64], updated[64:]], axis=1)
    new_glob[...] = glob[...]
    new_mom[...] = mom[...]
    new_glob[frag] = updated
    alone, _ = stepped(glob[frag], mom[frag], 0.0)
    mean = (updated - alone) / (outer_rate * (1.0 + outer_mom))
    new_mom[frag] = stepped(glob[frag], mom[frag], mean)[1]


def norm_kernel(pos, hidden, gain, cot, out, inv_out):
    tokens, width = hidden.shape
    chunk = width // NY
    total = jnp.zeros((tokens, 128), F32)
    for j in range(width // 128):
        block = hidden[:, j * 128 : (j + 1) * 128].astype(F32)
        total = total + block * block
    mean = jnp.sum(total, axis=1, keepdims=True) / width
    inverse = lax.rsqrt(mean + norm_eps)
    inv_out[...] = jnp.broadcast_to(inverse, inv_out.shape)
    for y in range(NY):
        for j in range(chunk // 128):
            at = slice(y * chunk + j * 128, y * chunk + (j + 1) * 128)
            block = hidden[:, at].astype(F32) * inverse * gain[at][None]
            out[y, j * 128 : (j + 1) * 128, :] = block.T.astype(BF)
        for j in range(cot.shape[1] // 128):
            at = slice(j * 128, (j + 1) * 128)
            out[y, chunk + j * tokens : chunk + (j + 1) * tokens, :] = cot[:, at]


def back_kernel(pos, w0, wz, wc, wzc, both, out, turned):
    rows, depth = w0.shape
    tokens = both.shape[2]
    for y in range(2):
        for j in range(depth // 128):
            cot = both[y, 4 * rows + j * tokens : 4 * rows + (j + 1) * tokens, :]
            turned[j * 128 : (j + 1) * 128, y * tokens : (y + 1) * tokens] = cot.T
    for dz, dc, w in ((0, 0, w0), (0, 1, wc), (1, 0, wz), (1, 1, wzc)):
        start = (jnp.bitwise_xor(pos[4], dz) * 2 + jnp.bitwise_xor(pos[5], dc)) * rows
        at = pl.ds(pl.multiple_of(start, 32), rows)
        product = jnp.dot(w[...], turned[...], preferred_element_type=F32)
        out[0, at, :] = product[:, :tokens]
        out[1, at, :] = product[:, tokens:]


def back_product(pos, weights, both):
    rows, kv = weights[0].shape
    tokens = both.shape[2]
    return pl.pallas_call(
        back_kernel,
        grid_spec=pltpu.PrefetchScalarGridSpec(
            num_scalar_prefetch=1,
            grid=(NY // 2,),
            in_specs=[whole((rows, kv))] * 4
            + [pl.BlockSpec((2,) + both.shape[1:], lambda i, pos: (i, 0, 0))],
            out_specs=pl.BlockSpec((2, 4 * rows, tokens), lambda i, pos: (i, 0, 0)),
            scratch_shapes=[pltpu.VMEM((kv, 2 * tokens), BF)],
        ),
        out_shape=pltpu.HBM((NY, 4 * rows, tokens), F32),
        compiler_params=pltpu.CompilerParams(vmem_limit_bytes=LIMIT),
        name="back_product",
    )(pos, *weights, both)


def grad_kernel(dz, pos, mine, theirs, out):
    rows, kv = out.shape
    tokens = mine.shape[2]
    start = (jnp.bitwise_xor(pos[4], dz) * 2 + pos[5]) * rows
    at = pl.ds(pl.multiple_of(start, 32), rows)
    left = jnp.concatenate([both[y, at, :] for both in (mine, theirs) for y in range(NY)], axis=1)
    for j in range(kv // 256):
        columns = []
        for b in (2 * j, 2 * j + 1):
            lines = slice(4 * rows + b * tokens, 4 * rows + (b + 1) * tokens)
            blocks = [both[y, lines, :] for both in (mine, theirs) for y in range(NY)]
            columns.append(jnp.concatenate(blocks, axis=0))
        out[:, j * 256 : (j + 1) * 256] = jnp.dot(
            left, jnp.concatenate(columns, axis=1), preferred_element_type=F32
        )


def hidden_kernel(pos, hidden, gain, inv, backs, out, scratch):
    width = hidden.shape[1]
    total = jnp.zeros((hidden.shape[0], 128), F32)
    for j in range(width // 128):
        at = slice(j * 128, (j + 1) * 128)
        scaled = gain[at][None] * backs[at, :].T
        total = total + scaled * hidden[:, at].astype(F32)
        scratch[:, at] = scaled
    project = jnp.sum(total, axis=1, keepdims=True) / width
    inverse = inv[...]
    factor = inverse * inverse * inverse * project
    for j in range(width // 128):
        at = slice(j * 128, (j + 1) * 128)
        out[:, at] = (inverse * scratch[:, at] - hidden[:, at].astype(F32) * factor).astype(BF)


def adam_kernel(pos, rates, own, far, slot, first, second, *refs):
    totals, (_, out, first_out, second_out, ordered) = refs[:NX], refs[NX:]
    for d in range(NX):
        ordered[lax.rem(pos[1] + NX - d, NX)] = totals[d][0]
    rows = own.shape[0]
    half = rows // 2
    grad = own[...] + far[...]
    first_next = beta_first * first[...] + (1.0 - beta_first) * grad
    second_next = beta_second * second[...] + (1.0 - beta_second) * grad * grad
    first_out[...] = first_next
    second_out[...] = second_next
    snapshot = slot[...].astype(F32)
    updated = snapshot - rates[0] * (
        (first_next / rates[1]) / (jnp.sqrt(second_next / rates[2]) + adam_eps)
        + weight_decay * snapshot
    )
    left = lane_half((half, 128))
    for x in range(0, NX, 2):
        at = slice(x * 64, x * 64 + 128)
        a, b = ordered[x], ordered[x + 1]
        top = jnp.where(left, a, pltpu.roll(b, 64, 1))
        bottom = jnp.where(left, pltpu.roll(a, 64, 1), b)
        out[0, :half, at] = (mix_share * updated[:half, at] + (1.0 - mix_share) * top).astype(BF)
        out[0, half:, at] = (mix_share * updated[half:, at] + (1.0 - mix_share) * bottom).astype(BF)


def adam(pos, rates, own, far, slot, first, second, totals, weights):
    rows, kv = own.shape
    wide = kv // NH
    column = pl.BlockSpec((rows, wide), lambda i, *_: (0, i))
    piece = totals[0].shape[1:]
    columns = [in_hbm(a) for a in (own, far, slot, first, second)]
    return pl.pallas_call(
        adam_kernel,
        grid_spec=pltpu.PrefetchScalarGridSpec(
            num_scalar_prefetch=2,
            grid=(NH,),
            in_specs=[column] * 5
            + [pl.BlockSpec((1,) + piece, lambda i, *_: (i, 0, 0))] * NX
            + [pl.BlockSpec(memory_space=pl.ANY)],
            out_specs=[
                pl.BlockSpec((1, rows, wide), lambda i, pos, rates: (pos[0], 0, i)),
                column,
                column,
            ],
            scratch_shapes=[pltpu.VMEM((NX,) + piece, F32)],
        ),
        out_shape=[shape(weights.shape, BF), shape((rows, kv), F32), shape((rows, kv), F32)],
        input_output_aliases={7 + NX: 0},
        compiler_params=pltpu.CompilerParams(vmem_limit_bytes=LIMIT),
        name="adam",
    )(pos, rates, *columns, *totals, weights)


def local(
    hidden,
    key_cotangent,
    norm_gain,
    weights,
    adam_first,
    adam_second,
    inner_step,
    outer_global,
    outer_momentum,
):
    tokens, width = hidden.shape
    rows, kv = weights.shape[2:]
    frag_index = inner_step % FRAGS
    replica = lax.axis_index("replica")
    place = lax.axis_index("fsdp")
    pos = jnp.stack(
        [frag_index, replica % NX, replica // NX, place // 4, (place // 2) % 2, place % 2]
    ).astype(jnp.int32)
    counter = inner_step.astype(F32)
    rates = jnp.stack(
        [
            inner_rate * jnp.minimum(F32(1.0), counter / warmup_steps),
            1.0 - jnp.power(F32(beta_first), counter),
            1.0 - jnp.power(F32(beta_second), counter),
        ]
    )
    gain = norm_gain

    both, inv = call(
        norm_kernel,
        "norm",
        [pltpu.HBM((NY, width // NY + kv, tokens), BF), pltpu.HBM((tokens, 128), F32)],
        (pos, hidden, gain, key_cotangent),
    )
    both = fsdp_trade(both)
    pos, inv = after(pos, inv)

    slot, *pieces = pick(pos, weights[0])
    w_z = fsdp_move(slot, 1, 0)
    pieces = [pieces[0]] + [replica_turn(pieces[d], d) for d in range(1, NX)]
    w_c = fsdp_move(slot, 0, 1)
    pos, slot = after(pos, slot)

    turned = [jnp.swapaxes(a, 1, 2) for a in (outer_global, outer_momentum)]
    packed = shape((NH, rows // 2, 128), F32)
    (totals,) = call(sum_x_kernel, "sum_x", [packed], (pos, *pieces, *turned))
    pos, totals = after(pos, totals)
    w_z, totals = after(w_z, totals)
    w_zc = fsdp_move(w_z, 0, 1)
    near_totals = replica_swap(totals, 0)
    (totals,) = call(pair_kernel, "sum_h", [packed], (pos, totals, near_totals))
    pos, totals = after(pos, totals)
    far_totals = replica_swap(totals, 1)
    pos, w_zc = after(pos, w_zc)

    both, totals = after(both, totals)
    both_c = fsdp_move(both, 0, 1)
    backs = back_product(pos, (slot, w_z, w_c, w_zc), both)
    pos, backs = after(pos, backs)
    backs = fsdp_trade(backs).reshape(width, tokens)

    (totals,) = call(pair_kernel, "sum_hh", [packed], (pos, totals, far_totals))
    pos, totals = after(pos, totals)
    all_totals = [totals] + [replica_turn(totals, d) for d in range(1, NX)]
    block = [pltpu.HBM((rows, kv), F32)]
    (far,) = call(functools.partial(grad_kernel, 1), "grad_far", block, (pos, both, both_c))
    pos, far = after(pos, far)
    far = fsdp_move(far, 1, 0)
    (own,) = call(functools.partial(grad_kernel, 0), "grad_near", block, (pos, both, both_c))
    pos, own = after(pos, own)

    new_global, new_momentum = call(
        outer_kernel, "outer", [shape(turned[0].shape, F32)] * 2, (pos, totals, *turned)
    )
    pos, new_global = after(pos, new_global)
    kept = keep(pos, weights[0])
    pos, kept = after(pos, kept)

    (hidden_grad,) = call(
        hidden_kernel,
        "hidden_back",
        [shape(hidden.shape, BF)],
        (pos, hidden, gain, inv, backs),
        scratch=[pltpu.VMEM(hidden.shape, F32)],
    )
    pos, hidden_grad = after(pos, hidden_grad)
    layers_out, first_next, second_next = adam(
        pos, rates, own, far, slot, adam_first[0], adam_second[0], all_totals, kept
    )
    return (
        layers_out[None],
        hidden_grad,
        first_next[None],
        second_next[None],
        jnp.swapaxes(new_global, 1, 2),
        jnp.swapaxes(new_momentum, 1, 2),
    )


def solution(mesh):
    in_specs = (
        P(("replica", "fsdp"), None),
        P(("replica", "fsdp"), None),
        P(),
        P("replica", None, "fsdp", None),
        P("replica", "fsdp", None),
        P("replica", "fsdp", None),
        P(),
        P(None, "fsdp", "replica"),
        P(None, "fsdp", "replica"),
    )
    out_specs = (
        P("replica", None, "fsdp", None),
        P(("replica", "fsdp"), None),
        P("replica", "fsdp", None),
        P("replica", "fsdp", None),
        P(None, "fsdp", "replica"),
        P(None, "fsdp", "replica"),
    )
    return jax.shard_map(local, mesh=mesh, in_specs=in_specs, out_specs=out_specs, check_vma=False)
```

time: 181 us -> 107 us (0.59)
  waiting for transfers between devices: 72 us -> 35 us
  blocking collectives: 13.2 us -> 0 us
  starting transfers between devices: 42.8 us -> 29.7 us
  Pallas kernels: 40.7 us -> 34.7 us
  local copies, waits for them, and re-layouts: 7.99 us -> 5.1 us
    ppermute x5, waiting for transfers between devices: 50.3 us -> 12.7 us  [fsdp_move(): lax.ppermute(array, 'fsdp', [(i, i ^ dz * 2 + dc) for i in range(4 * NY)])]
    ppermute x6 -> x8, waiting for transfers between devices: 8.15 us -> 22.3 us  [the longest x2 15.3 us: replica_swap(): return lax.ppermute(array, ('replica', 'fsdp'), pairs)]
    all_to_all x1 -> x0, blocking collectives: 13.2 us -> none  [replica_trade(): lax.all_to_all(array, 'replica', 0, 0, axis_index_groups=groups, tiled=True)]
    all_to_all x3 -> x2, waiting for transfers between devices: 8.31 us -> 0.01 us  [fsdp_trade(): lax.all_to_all(array, 'fsdp', 0, 0, axis_index_groups=groups, tiled=True)]
    pallas_call x7 -> x8, Pallas kernels: 26.6 us -> 18.5 us  [call(): pl.pallas_call(kernel, grid_spec=pltpu.PrefetchScalarGridSpec(num_scalar_...]
    all_to_all x3 -> x2, starting transfers between devices: 15.5 us -> 9.84 us  [fsdp_trade(): lax.all_to_all(array, 'fsdp', 0, 0, axis_index_groups=groups, tiled=True)]
    all_to_all x1 -> x0, starting transfers between devices: 5.57 us -> none  [replica_trade(): lax.all_to_all(array, 'replica', 0, 0, axis_index_groups=groups, tiled=True)]
    all_to_all x1 -> x0, waiting for transfers between devices: 5.24 us -> none  [replica_trade(): lax.all_to_all(array, 'replica', 0, 0, axis_index_groups=groups, tiled=True)]
  transfers between devices with their start and end apart: 15 -> 15, of which waited for: 9 -> 8; matrix products, arithmetic and copies ran while one was open for 1% -> 0% of each run, Pallas kernels for 17% -> 25%
where the time goes in v3:
time: 107 us; the launch traced here: 106 us
  waiting for transfers between devices  35 us (33%)
  Pallas kernels  34.7 us (32%)
  starting transfers between devices  29.7 us (28%)
  local copies, waits for them, and re-layouts  5.1 us (5%)
  between operations  1.55 us (1%)
    pallas_call x8, Pallas kernels, call(): pl.pallas_call(kernel, grid_spec=pltpu.PrefetchScalarGridSpec(num_scalar_...  18.5 us
    ppermute x2, waiting for transfers between devices, replica_swap(): return lax.ppermute(array, ('replica', 'fsdp'), pairs)  15.3 us
    ppermute x5, waiting for transfers between devices, fsdp_move(): lax.ppermute(array, 'fsdp', [(i, i ^ dz * 2 + dc) for i in range(4 * NY)])  12.7 us
    all_to_all x2, starting transfers between devices, fsdp_trade(): lax.all_to_all(array, 'fsdp', 0, 0, axis_index_groups=groups, tiled=True)  9.84 us
    ppermute x2, starting transfers between devices, replica_swap(): return lax.ppermute(array, ('replica', 'fsdp'), pairs)  8.48 us
    ppermute x6, waiting for transfers between devices, replica_turn(): return lax.ppermute(array, 'replica', pairs)  6.98 us
    ppermute x6, starting transfers between devices, replica_turn(): return lax.ppermute(array, 'replica', pairs)  6.93 us
    pallas_call x1, Pallas kernels, adam(): pl.pallas_call(adam_kernel, grid_spec=pltpu.PrefetchScalarGridSpec(num_sc...  5.7 us
  transfers between devices with their start and end apart: 15, of which 8 were waited for; matrix products, arithmetic and copies ran while one was open for 0% of the time, Pallas kernels for 25%

profile of v3, /device:TPU:14, one launch (start us, length us, event | category | flops | bytes accessed | tf_op | source)
XLA Modules:
  0.0 106.2 jit_solution(12026392235186799150)
XLA Ops:
  4.4 2.7 %norm.1 = (bf16[4,2176,128]{2,1,0:T(8,128)(2,1)}, f32[128,128]{1,0:T(8,128)}) custom-call(s32[6]{0:T(128)S(1)} %stack.39.pos, bf16[128,4608]{1,0:T(8,128)(2,1)S(1)} %copy-done, f32[4608]{0:T(1024)S(1)} %copy-done.11, bf16[128,1024]{1,0:T(8,128)(2,1)S(1)} %copy-done.10), custom_call_target="tpu_custom_call" | custom-call | tf_op jit(solution)/shard_map/norm/pallas_call | solution.py:45
  7.1 4.9 %all-to-all-start = ((bf16[4,2176,128]{2,1,0:T(8,128)(2,1)}), bf16[4,2176,128]{2,1,0:T(8,128)(2,1)S(1)}, u32[]{:S(2)}, u32[]{:S(2)}) async-start(bf16[4,2176,128]{2,1,0:T(8,128)(2,1)} %get-tuple-element.62), calls=%async_computation | async-start | bytes 4456448 | tf_op jit(solution)/shard_map/all_to_all | solution.py:66
  12.0 2.7 %pick.1 = (bf16[288,1024]{1,0:T(8,128)(2,1)}, bf16[4,144,128]{2,1,0:T(8,128)(2,1)S(1)}, bf16[4,144,128]{2,1,0:T(8,128)(2,1)S(1)}, bf16[4,144,128]{2,1,0:T(8,128)(2,1)S(1)}, bf16[4,144,128]{2,1,0:T(8,128)(2,1)S(1)}) custom-call(s32[6]{0:T(128)S(1)} %stack.39.pos, bf16[4,288,1024]{2,1,0:T(8,128)(2,1)} %bitcast.25), custom_call_target="tpu_custom_call" | custom-call | tf_op jit(solution)/shard_map/pick/pallas_call | solution.py:109
  14.7 1.9 %collective-permute-start.3 = (bf16[288,1024]{1,0:T(8,128)(2,1)}, bf16[288,1024]{1,0:T(8,128)(2,1)S(1)}, u32[]{:S(2)}, u32[]{:S(2)}) collective-permute-start(bf16[288,1024]{1,0:T(8,128)(2,1)} %get-tuple-element.60.w0.slot), channel_id=1, source_target_pairs={{0,2},{1,3},{2,0},{3,1},{4,6},{5,7},{6,4},{7,5},{8,10},{9,11},{10,... | collective-permute-start | bytes 1769480 | tf_op jit(solution)/shard_map/ppermute | solution.py:61
  17.1 2.4 %collective-permute-start.1 = (bf16[4,144,128]{2,1,0:T(8,128)(2,1)S(1)}, bf16[4,144,128]{2,1,0:T(8,128)(2,1)S(1)}, u32[]{:S(2)}, u32[]{:S(2)}) collective-permute-start(bf16[4,144,128]{2,1,0:T(8,128)(2,1)S(1)} %get-tuple-element.52), channel_id=1, source_target_pairs={{0,32},{16,48},{32,0},{48,16},{64,96},{80,112},{96,64},{112,80},{1... | collective-permute-start | bytes 442376 | tf_op jit(solution)/shard_map/ppermute | solution.py:71
  19.5 3.4 %collective-permute-done.b = bf16[4,144,128]{2,1,0:T(8,128)(2,1)S(1)} collective-permute-done((bf16[4,144,128]{2,1,0:T(8,128)(2,1)S(1)}, bf16[4,144,128]{2,1,0:T(8,128)(2,1)S(1)}, u32[]{:S(2)}, u32[]{:S(2)}) %collective-permute-start) | collective-permute-done | bytes 147488 | tf_op jit(solution)/shard_map/ppermute | solution.py:71
  23.0 2.0 %collective-permute-done.1.c = bf16[4,144,128]{2,1,0:T(8,128)(2,1)S(1)} collective-permute-done((bf16[4,144,128]{2,1,0:T(8,128)(2,1)S(1)}, bf16[4,144,128]{2,1,0:T(8,128)(2,1)S(1)}, u32[]{:S(2)}, u32[]{:S(2)}) %collective-permute-start.1) | collective-permute-done | bytes 147488 | tf_op jit(solution)/shard_map/ppermute | solution.py:71
  27.2 2.4 %collective-permute-done.3.wz = bf16[288,1024]{1,0:T(8,128)(2,1)S(1)} collective-permute-done((bf16[288,1024]{1,0:T(8,128)(2,1)}, bf16[288,1024]{1,0:T(8,128)(2,1)S(1)}, u32[]{:S(2)}, u32[]{:S(2)}) %collective-permute-start.3) | collective-permute-done | bytes 589856 | tf_op jit(solution)/shard_map/ppermute | solution.py:61
  29.6 3.3 %collective-permute-start.4 = (f32[4,144,128]{2,1,0:T(8,128)S(1)}, f32[4,144,128]{2,1,0:T(8,128)S(1)}, u32[]{:S(2)}, u32[]{:S(2)}) collective-permute-start(f32[4,144,128]{2,1,0:T(8,128)S(1)} %sum_x.1.a), channel_id=1, source_target_pairs={{0,64},{1,193},{2,66},{3,195},{4,68},{5,197},{6,70},{7,199},{8,72}... | collective-permute-start | bytes 884744 | tf_op jit(solution)/shard_map/ppermute | solution.py:80
  32.9 7.9 %collective-permute-done.4.b = f32[4,144,128]{2,1,0:T(8,128)S(1)} collective-permute-done((f32[4,144,128]{2,1,0:T(8,128)S(1)}, f32[4,144,128]{2,1,0:T(8,128)S(1)}, u32[]{:S(2)}, u32[]{:S(2)}) %collective-permute-start.4) | collective-permute-done | bytes 294944 | tf_op jit(solution)/shard_map/ppermute | solution.py:80
  42.1 5.3 %collective-permute-done.5.wzc = bf16[288,1024]{1,0:T(8,128)(2,1)S(1)} collective-permute-done((bf16[288,1024]{1,0:T(8,128)(2,1)}, bf16[288,1024]{1,0:T(8,128)(2,1)S(1)}, u32[]{:S(2)}, u32[]{:S(2)}) %collective-permute-start.5) | collective-permute-done | bytes 589856 | tf_op jit(solution)/shard_map/ppermute | solution.py:61
  48.4 3.4 %back_product.1 = f32[4,1152,128]{2,1,0:T(8,128)} custom-call(s32[6]{0:T(128)S(1)} %stack.39.pos, bf16[288,1024]{1,0:T(8,128)(2,1)S(1)} %copy-done.2, bf16[288,1024]{1,0:T(8,128)(2,1)S(1)} %copy-done.9, bf16[288,1024]{1,0:T(8,128)(2,1)S(1)} %collective-permute-done.6.wc, bf16[288,1024]{1,0:T(8,128)(2,1)S(1)} %collective-permute-done.5.wzc, ...), custom_call_target="tpu_custom_call" | custom-call | tf_op jit(solution)/shard_map/back_product/pallas_call | solution.py:214
  51.8 4.9 %all-to-all-start.1 = ((f32[4,1152,128]{2,1,0:T(8,128)}), f32[4,1152,128]{2,1,0:T(8,128)}, u32[]{:S(2)}, u32[]{:S(2)}) async-start(f32[4,1152,128]{2,1,0:T(8,128)} %back_product.1), calls=%async_computation.1 | async-start | bytes 4718592 | tf_op jit(solution)/shard_map/all_to_all | solution.py:66
  56.7 5.2 %collective-permute-start.7 = (f32[4,144,128]{2,1,0:T(8,128)S(1)}, f32[4,144,128]{2,1,0:T(8,128)S(1)}, u32[]{:S(2)}, u32[]{:S(2)}) collective-permute-start(f32[4,144,128]{2,1,0:T(8,128)S(1)} %sum_h.1.a), channel_id=1, source_target_pairs={{0,192},{1,65},{2,194},{3,67},{4,196},{5,69},{6,198},{7,71},{8,200... | collective-permute-start | bytes 884744 | tf_op jit(solution)/shard_map/ppermute | solution.py:80
  61.9 7.4 %collective-permute-done.7.b = f32[4,144,128]{2,1,0:T(8,128)S(1)} collective-permute-done((f32[4,144,128]{2,1,0:T(8,128)S(1)}, f32[4,144,128]{2,1,0:T(8,128)S(1)}, u32[]{:S(2)}, u32[]{:S(2)}) %collective-permute-start.7) | collective-permute-done | bytes 294944 | tf_op jit(solution)/shard_map/ppermute | solution.py:80
  70.9 4.0 %grad_far.1 = f32[288,1024]{1,0:T(8,128)} custom-call(s32[6]{0:T(128)S(1)} %stack.39.pos, bf16[4,2176,128]{2,1,0:T(8,128)(2,1)S(1)} %all-to-all-done.both.mine, bf16[4,2176,128]{2,1,0:T(8,128)(2,1)} %collective-permute-done.8.theirs), custom_call_target="tpu_custom_call" | custom-call | tf_op jit(solution)/shard_map/grad_far/pallas_call | solution.py:45
  74.9 1.8 %collective-permute-start.9 = (f32[288,1024]{1,0:T(8,128)}, f32[288,1024]{1,0:T(8,128)}, u32[]{:S(2)}, u32[]{:S(2)}) collective-permute-start(f32[288,1024]{1,0:T(8,128)} %grad_far.1), channel_id=1, source_target_pairs={{0,2},{1,3},{2,0},{3,1},{4,6},{5,7},{6,4},{7,5},{8,10},{9,11},{10,... | collective-permute-start | bytes 3538952 | tf_op jit(solution)/shard_map/ppermute | solution.py:61
  78.6 2.1 %collective-permute-start.10 = (f32[4,144,128]{2,1,0:T(8,128)S(1)}, f32[4,144,128]{2,1,0:T(8,128)}, u32[]{:S(2)}, u32[]{:S(2)}) collective-permute-start(f32[4,144,128]{2,1,0:T(8,128)S(1)} %sum_hh.1.totals.refs_0_), channel_id=1, source_target_pairs={{0,16},{16,32},{32,48},{48,0},{64,80},{80,96},{96,112},{112,64},{1... | collective-permute-start | bytes 884744 | tf_op jit(solution)/shard_map/ppermute | solution.py:71
  80.9 4.0 %grad_near.1.own = f32[288,1024]{1,0:T(8,128)} custom-call(s32[6]{0:T(128)S(1)} %stack.39.pos, bf16[4,2176,128]{2,1,0:T(8,128)(2,1)S(1)} %all-to-all-done.both.mine, bf16[4,2176,128]{2,1,0:T(8,128)(2,1)} %collective-permute-done.8.theirs), custom_call_target="tpu_custom_call" | custom-call | tf_op jit(solution)/shard_map/grad_near/pallas_call | solution.py:45
  84.9 1.6 %outer.1 = (f32[4,64,288]{2,1,0:T(8,128)}, f32[4,64,288]{2,1,0:T(8,128)}) custom-call(s32[6]{0:T(128)S(1)} %stack.39.pos, f32[4,144,128]{2,1,0:T(8,128)S(1)} %sum_hh.1.totals.refs_0_, f32[4,64,288]{2,1,0:T(8,128)S(1)} %bitcast.21, f32[4,64,288]{2,1,0:T(8,128)S(1)} %bitcast.23), custom_call_target="tpu_custom_call" | custom-call | tf_op jit(solution)/shard_map/outer/pallas_call | solution.py:45
  86.5 4.4 %keep.1.refs_4_ = bf16[4,288,1024]{2,1,0:T(8,128)(2,1)} custom-call(s32[6]{0:T(128)S(1)} %stack.39.pos, bf16[4,288,1024]{2,1,0:T(8,128)(2,1)} %bitcast.26), custom_call_target="tpu_custom_call" | custom-call | tf_op jit(solution)/shard_map/keep/pallas_call | solution.py:130
  90.9 4.4 %hidden_back.1 = bf16[128,4608]{1,0:T(8,128)(2,1)} custom-call(s32[6]{0:T(128)S(1)} %stack.39.pos, bf16[128,4608]{1,0:T(8,128)(2,1)S(1)} %copy-done.1, f32[4608]{0:T(1024)S(1)} %copy-done.12, f32[128,128]{1,0:T(8,128)S(1)} %copy-done.13, f32[4608,128]{1,0:T(8,128)} %bitcast.9.backs), custom_call_target="tpu_custom_call" | custom-call | tf_op jit(solution)/shard_map/hidden_back/pallas_call | solution.py:45
  95.4 5.1 %collective-permute-done.9.far = f32[288,1024]{1,0:T(8,128)} collective-permute-done((f32[288,1024]{1,0:T(8,128)}, f32[288,1024]{1,0:T(8,128)}, u32[]{:S(2)}, u32[]{:S(2)}) %collective-permute-start.9) | collective-permute-done | bytes 1179680 | tf_op jit(solution)/shard_map/ppermute | solution.py:61
  100.5 5.7 %adam.1 = (bf16[4,288,1024]{2,1,0:T(8,128)(2,1)}, f32[288,1024]{1,0:T(8,128)}, f32[288,1024]{1,0:T(8,128)}) custom-call(s32[6]{0:T(128)S(1)} %stack.39.pos, f32[3]{0:T(128)S(1)} %pad_maximum_fusion.rates, f32[288,1024]{1,0:T(8,128)} %grad_near.1.own, f32[288,1024]{1,0:T(8,128)} %collective-permute-done.9.far, ...), custom_call_target="tpu_custom_call", output_to_operand_aliasing={{0}: (11, {})} | custom-call | tf_op jit(solution)/shard_map/adam/pallas_call | solution.py:295
  (48 shorter events, 11.7 us)
Async XLA Ops:
  7.1 34.3 %all-to-all-start = ((bf16[4,2176,128]{2,1,0:T(8,128)(2,1)}), bf16[4,2176,128]{2,1,0:T(8,128)(2,1)S(1)}, u32[]{:S(2)}, u32[]{:S(2)}) async-start(bf16[4,2176,128]{2,1,0:T(8,128)(2,1)} %get-tuple-element.62), calls=%async_computation | async-start | bytes 4456448 | tf_op jit(solution)/shard_map/all_to_all | solution.py:66
  12.0 14.5 %copy-start.3 = (f32[4,288,64]{1,2,0:T(8,128)S(1)}, f32[4,288,64]{1,2,0:T(8,128)}, u32[]{:S(2)}) copy-start(f32[4,288,64]{1,2,0:T(8,128)} %param.16) | copy-start | bytes 884740
  12.0 14.5 %copy-start.4 = (f32[4,288,64]{1,2,0:T(8,128)S(1)}, f32[4,288,64]{1,2,0:T(8,128)}, u32[]{:S(2)}) copy-start(f32[4,288,64]{1,2,0:T(8,128)} %param.17) | copy-start | bytes 884740
  14.7 14.9 %collective-permute-start.3 = (bf16[288,1024]{1,0:T(8,128)(2,1)}, bf16[288,1024]{1,0:T(8,128)(2,1)S(1)}, u32[]{:S(2)}, u32[]{:S(2)}) collective-permute-start(bf16[288,1024]{1,0:T(8,128)(2,1)} %get-tuple-element.60.w0.slot), channel_id=1, source_target_pairs={{0,2},{1,3},{2,0},{3,1},{4,6},{5,7},{6,4},{7,5},{8,10},{9,11},{10,... | collective-permute-start | bytes 1769480 | tf_op jit(solution)/shard_map/ppermute | solution.py:61
  16.6 6.3 %collective-permute-start = (bf16[4,144,128]{2,1,0:T(8,128)(2,1)S(1)}, bf16[4,144,128]{2,1,0:T(8,128)(2,1)S(1)}, u32[]{:S(2)}, u32[]{:S(2)}) collective-permute-start(bf16[4,144,128]{2,1,0:T(8,128)(2,1)S(1)} %get-tuple-element.51), channel_id=1, source_target_pairs={{0,16},{16,32},{32,48},{48,0},{64,80},{80,96},{96,112},{112,64},{1... | collective-permute-start | bytes 442376 | tf_op jit(solution)/shard_map/ppermute | solution.py:71
  17.1 7.9 %collective-permute-start.1 = (bf16[4,144,128]{2,1,0:T(8,128)(2,1)S(1)}, bf16[4,144,128]{2,1,0:T(8,128)(2,1)S(1)}, u32[]{:S(2)}, u32[]{:S(2)}) collective-permute-start(bf16[4,144,128]{2,1,0:T(8,128)(2,1)S(1)} %get-tuple-element.52), channel_id=1, source_target_pairs={{0,32},{16,48},{32,0},{48,16},{64,96},{80,112},{96,64},{112,80},{1... | collective-permute-start | bytes 442376 | tf_op jit(solution)/shard_map/ppermute | solution.py:71
  19.5 7.0 %collective-permute-start.2 = (bf16[4,144,128]{2,1,0:T(8,128)(2,1)S(1)}, bf16[4,144,128]{2,1,0:T(8,128)(2,1)S(1)}, u32[]{:S(2)}, u32[]{:S(2)}) collective-permute-start(bf16[4,144,128]{2,1,0:T(8,128)(2,1)S(1)} %get-tuple-element.53), channel_id=1, source_target_pairs={{0,48},{16,0},{32,16},{48,32},{64,112},{80,64},{96,80},{112,96},{1... | collective-permute-start | bytes 442376 | tf_op jit(solution)/shard_map/ppermute | solution.py:71
  26.5 15.4 %copy-start.2 = (bf16[288,1024]{1,0:T(8,128)(2,1)S(1)}, bf16[288,1024]{1,0:T(8,128)(2,1)}, u32[]{:S(2)}) copy-start(bf16[288,1024]{1,0:T(8,128)(2,1)} %get-tuple-element.60.w0.slot) | copy-start | bytes 1769476
  29.6 11.1 %copy-start.8 = (bf16[288,1024]{1,0:T(8,128)(2,1)}, bf16[288,1024]{1,0:T(8,128)(2,1)S(1)}, u32[]{:S(2)}) copy-start(bf16[288,1024]{1,0:T(8,128)(2,1)S(1)} %collective-permute-done.3.wz) | copy-start | bytes 1769476
  29.6 11.1 %collective-permute-start.4 = (f32[4,144,128]{2,1,0:T(8,128)S(1)}, f32[4,144,128]{2,1,0:T(8,128)S(1)}, u32[]{:S(2)}, u32[]{:S(2)}) collective-permute-start(f32[4,144,128]{2,1,0:T(8,128)S(1)} %sum_x.1.a), channel_id=1, source_target_pairs={{0,64},{1,193},{2,66},{3,195},{4,68},{5,197},{6,70},{7,199},{8,72}... | collective-permute-start | bytes 884744 | tf_op jit(solution)/shard_map/ppermute | solution.py:80
  41.3 15.4 %copy-start.6 = (f32[4,144,128]{2,1,0:T(8,128)}, f32[4,144,128]{2,1,0:T(8,128)S(1)}, u32[]{:S(2)}) copy-start(f32[4,144,128]{2,1,0:T(8,128)S(1)} %sum_h.1.a) | copy-start | bytes 884740
  41.3 29.5 %collective-permute-start.8 = (bf16[4,2176,128]{2,1,0:T(8,128)(2,1)S(1)}, bf16[4,2176,128]{2,1,0:T(8,128)(2,1)}, u32[]{:S(2)}, u32[]{:S(2)}) collective-permute-start(bf16[4,2176,128]{2,1,0:T(8,128)(2,1)S(1)} %all-to-all-done.both.mine), channel_id=1, source_target_pairs={{0,1},{1,0},{2,3},{3,2},{4,5},{5,4},{6,7},{7,6},{8,9},{9,8},{10,11... | collective-permute-start | bytes 6684680 | tf_op jit(solution)/shard_map/ppermute | solution.py:61
  41.5 5.9 %collective-permute-start.5 = (bf16[288,1024]{1,0:T(8,128)(2,1)}, bf16[288,1024]{1,0:T(8,128)(2,1)S(1)}, u32[]{:S(2)}, u32[]{:S(2)}) collective-permute-start(bf16[288,1024]{1,0:T(8,128)(2,1)} %copy-done.8), channel_id=1, source_target_pairs={{0,1},{1,0},{2,3},{3,2},{4,5},{5,4},{6,7},{7,6},{8,9},{9,8},{10,11... | collective-permute-start | bytes 1769480 | tf_op jit(solution)/shard_map/ppermute | solution.py:61
  41.9 5.4 %collective-permute-start.6 = (bf16[288,1024]{1,0:T(8,128)(2,1)S(1)}, bf16[288,1024]{1,0:T(8,128)(2,1)S(1)}, u32[]{:S(2)}, u32[]{:S(2)}) collective-permute-start(bf16[288,1024]{1,0:T(8,128)(2,1)S(1)} %copy-done.2), channel_id=1, source_target_pairs={{0,1},{1,0},{2,3},{3,2},{4,5},{5,4},{6,7},{7,6},{8,9},{9,8},{10,11... | collective-permute-start | bytes 1769480 | tf_op jit(solution)/shard_map/ppermute | solution.py:61
  51.8 39.2 %all-to-all-start.1 = ((f32[4,1152,128]{2,1,0:T(8,128)}), f32[4,1152,128]{2,1,0:T(8,128)}, u32[]{:S(2)}, u32[]{:S(2)}) async-start(f32[4,1152,128]{2,1,0:T(8,128)} %back_product.1), calls=%async_computation.1 | async-start | bytes 4718592 | tf_op jit(solution)/shard_map/all_to_all | solution.py:66
  56.7 12.6 %collective-permute-start.7 = (f32[4,144,128]{2,1,0:T(8,128)S(1)}, f32[4,144,128]{2,1,0:T(8,128)S(1)}, u32[]{:S(2)}, u32[]{:S(2)}) collective-permute-start(f32[4,144,128]{2,1,0:T(8,128)S(1)} %sum_h.1.a), channel_id=1, source_target_pairs={{0,192},{1,65},{2,194},{3,67},{4,196},{5,69},{6,198},{7,71},{8,200... | collective-permute-start | bytes 884744 | tf_op jit(solution)/shard_map/ppermute | solution.py:80
  74.9 25.6 %collective-permute-start.9 = (f32[288,1024]{1,0:T(8,128)}, f32[288,1024]{1,0:T(8,128)}, u32[]{:S(2)}, u32[]{:S(2)}) collective-permute-start(f32[288,1024]{1,0:T(8,128)} %grad_far.1), channel_id=1, source_target_pairs={{0,2},{1,3},{2,0},{3,1},{4,6},{5,7},{6,4},{7,5},{8,10},{9,11},{10,... | collective-permute-start | bytes 3538952 | tf_op jit(solution)/shard_map/ppermute | solution.py:61
  76.7 18.7 %collective-permute-start.12 = (f32[4,144,128]{2,1,0:T(8,128)S(1)}, f32[4,144,128]{2,1,0:T(8,128)S(1)}, u32[]{:S(2)}, u32[]{:S(2)}) collective-permute-start(f32[4,144,128]{2,1,0:T(8,128)S(1)} %sum_hh.1.totals.refs_0_), channel_id=1, source_target_pairs={{0,48},{16,0},{32,16},{48,32},{64,112},{80,64},{96,80},{112,96},{1... | collective-permute-start | bytes 884744 | tf_op jit(solution)/shard_map/ppermute | solution.py:71
  77.5 17.9 %collective-permute-start.11 = (f32[4,144,128]{2,1,0:T(8,128)S(1)}, f32[4,144,128]{2,1,0:T(8,128)S(1)}, u32[]{:S(2)}, u32[]{:S(2)}) collective-permute-start(f32[4,144,128]{2,1,0:T(8,128)S(1)} %sum_hh.1.totals.refs_0_), channel_id=1, source_target_pairs={{0,32},{16,48},{32,0},{48,16},{64,96},{80,112},{96,64},{112,80},{1... | collective-permute-start | bytes 884744 | tf_op jit(solution)/shard_map/ppermute | solution.py:71
  78.6 16.7 %collective-permute-start.10 = (f32[4,144,128]{2,1,0:T(8,128)S(1)}, f32[4,144,128]{2,1,0:T(8,128)}, u32[]{:S(2)}, u32[]{:S(2)}) collective-permute-start(f32[4,144,128]{2,1,0:T(8,128)S(1)} %sum_hh.1.totals.refs_0_), channel_id=1, source_target_pairs={{0,16},{16,32},{32,48},{48,0},{64,80},{80,96},{96,112},{112,64},{1... | collective-permute-start | bytes 884744 | tf_op jit(solution)/shard_map/ppermute | solution.py:71
  80.9 4.0 %copy-start.5 = (f32[4,288,64]{1,2,0:T(8,128)S(1)}, f32[4,288,64]{1,2,0:T(8,128)}, u32[]{:S(2)}) copy-start(f32[4,288,64]{1,2,0:T(8,128)} %param.17) | copy-start | bytes 884740
  86.5 4.4 %copy-start.1 = (bf16[128,4608]{1,0:T(8,128)(2,1)S(1)}, bf16[128,4608]{1,0:T(8,128)(2,1)}, u32[]{:S(2)}) copy-start(bf16[128,4608]{1,0:T(8,128)(2,1)} %hidden.3) | copy-start | bytes 3538948
  86.5 4.4 %copy-start.12 = (f32[4608]{0:T(1024)S(1)}, f32[4608]{0:T(1024)}, u32[]{:S(2)}) copy-start(f32[4608]{0:T(1024)} %gain.3) | copy-start | bytes 55300
  86.5 4.4 %copy-start.13 = (f32[128,128]{1,0:T(8,128)S(1)}, f32[128,128]{1,0:T(8,128)}, u32[]{:S(2)}) copy-start(f32[128,128]{1,0:T(8,128)} %get-tuple-element.74.inv) | copy-start | bytes 196612
  (5 other events, 5.0 us)

commit v4 on v3

--- a/solution.py
+++ b/solution.py
@@ -31,6 +31,9 @@
 
 def shape(dims, dtype):
     return jax.ShapeDtypeStruct(dims, dtype)
+
+
+ANY = pl.BlockSpec(memory_space=pl.ANY)
 
 
 def in_hbm(array):
@@ -193,19 +196,31 @@
             out[y, chunk + j * tokens : chunk + (j + 1) * tokens, :] = cot[:, at]
 
 
-def back_kernel(pos, w0, wz, wc, wzc, both, out, turned):
+def back_kernel(pos, w0, wz, wc, wzc, both, out, w_v, turned, out_v, in_sem, out_sem):
     rows, depth = w0.shape
     tokens = both.shape[2]
-    for y in range(2):
+    loads = []
+    for k, w in enumerate((w0, wc, wz, wzc)):
+        loads.append(pltpu.make_async_copy(w, w_v.at[k], in_sem.at[k]))
+        loads[k].start()
+    for y in range(NY):
         for j in range(depth // 128):
             cot = both[y, 4 * rows + j * tokens : 4 * rows + (j + 1) * tokens, :]
             turned[j * 128 : (j + 1) * 128, y * tokens : (y + 1) * tokens] = cot.T
-    for dz, dc, w in ((0, 0, w0), (0, 1, wc), (1, 0, wz), (1, 1, wzc)):
+    stores = []
+    for k, (dz, dc) in enumerate(((0, 0), (0, 1), (1, 0), (1, 1))):
         start = (jnp.bitwise_xor(pos[4], dz) * 2 + jnp.bitwise_xor(pos[5], dc)) * rows
         at = pl.ds(pl.multiple_of(start, 32), rows)
-        product = jnp.dot(w[...], turned[...], preferred_element_type=F32)
-        out[0, at, :] = product[:, :tokens]
-        out[1, at, :] = product[:, tokens:]
+        loads[k].wait()
+        for pair in range(NY // 2):
+            cot = turned[:, 2 * pair * tokens : (2 * pair + 2) * tokens]
+            product = jnp.dot(w_v[k], cot, preferred_element_type=F32)
+            out_v[2 * pair, at, :] = product[:, :tokens]
+            out_v[2 * pair + 1, at, :] = product[:, tokens:]
+        stores.append(pltpu.make_async_copy(out_v.at[:, at, :], out.at[:, at, :], out_sem.at[k]))
+        stores[k].start()
+    for copy in stores:
+        copy.wait()
 
 
 def back_product(pos, weights, both):
@@ -215,33 +230,53 @@
         back_kernel,
         grid_spec=pltpu.PrefetchScalarGridSpec(
             num_scalar_prefetch=1,
-            grid=(NY // 2,),
-            in_specs=[whole((rows, kv))] * 4
-            + [pl.BlockSpec((2,) + both.shape[1:], lambda i, pos: (i, 0, 0))],
-            out_specs=pl.BlockSpec((2, 4 * rows, tokens), lambda i, pos: (i, 0, 0)),
-            scratch_shapes=[pltpu.VMEM((kv, 2 * tokens), BF)],
+            grid=(1,),
+            in_specs=[ANY] * 4 + [pl.BlockSpec(memory_space=pltpu.VMEM)],
+            out_specs=ANY,
+            scratch_shapes=[
+                pltpu.VMEM((4, rows, kv), BF),
+                pltpu.VMEM((kv, NY * tokens), BF),
+                pltpu.VMEM((NY, 4 * rows, tokens), F32),
+                pltpu.SemaphoreType.DMA((4,)),
+                pltpu.SemaphoreType.DMA((4,)),
+            ],
         ),
         out_shape=pltpu.HBM((NY, 4 * rows, tokens), F32),
         compiler_params=pltpu.CompilerParams(vmem_limit_bytes=LIMIT),
         name="back_product",
-    )(pos, *weights, both)
-
-
-def grad_kernel(dz, pos, mine, theirs, out):
-    rows, kv = out.shape
+    )(pos, *(in_hbm(w) for w in weights), both)
+
+
+def grad_kernel(dz, begin, pos, mine, theirs, out):
+    rows, wide = out.shape
     tokens = mine.shape[2]
     start = (jnp.bitwise_xor(pos[4], dz) * 2 + pos[5]) * rows
     at = pl.ds(pl.multiple_of(start, 32), rows)
     left = jnp.concatenate([both[y, at, :] for both in (mine, theirs) for y in range(NY)], axis=1)
-    for j in range(kv // 256):
+    for j in range(wide // 256):
         columns = []
-        for b in (2 * j, 2 * j + 1):
+        for b in (begin // 128 + 2 * j, begin // 128 + 2 * j + 1):
             lines = slice(4 * rows + b * tokens, 4 * rows + (b + 1) * tokens)
             blocks = [both[y, lines, :] for both in (mine, theirs) for y in range(NY)]
             columns.append(jnp.concatenate(blocks, axis=0))
         out[:, j * 256 : (j + 1) * 256] = jnp.dot(
             left, jnp.concatenate(columns, axis=1), preferred_element_type=F32
         )
+
+
+def grad_product(pos, both, both_c, dz, begin, shape_out, name):
+    return pl.pallas_call(
+        functools.partial(grad_kernel, dz, begin),
+        grid_spec=pltpu.PrefetchScalarGridSpec(
+            num_scalar_prefetch=1,
+            grid=(1,),
+            in_specs=[pl.BlockSpec(memory_space=pltpu.VMEM)] * 2,
+            out_specs=whole(shape_out),
+        ),
+        out_shape=pltpu.HBM(shape_out, F32),
+        compiler_params=pltpu.CompilerParams(vmem_limit_bytes=LIMIT),
+        name=name,
+    )(pos, both, both_c)
 
 
 def hidden_kernel(pos, hidden, gain, inv, backs, out, scratch):
@@ -261,7 +296,7 @@
 
 
 def adam_kernel(pos, rates, own, far, slot, first, second, *refs):
-    totals, (_, out, first_out, second_out, ordered) = refs[:NX], refs[NX:]
+    totals, (out, first_out, second_out, ordered) = refs[:NX], refs[-4:]
     for d in range(NX):
         ordered[lax.rem(pos[1] + NX - d, NX)] = totals[d][0]
     rows = own.shape[0]
@@ -273,7 +308,7 @@
     second_out[...] = second_next
     snapshot = slot[...].astype(F32)
     updated = snapshot - rates[0] * (
-        (first_next / rates[1]) / (jnp.sqrt(second_next / rates[2]) + adam_eps)
+        (first_next * rates[1]) / (jnp.sqrt(second_next * rates[2]) + adam_eps)
         + weight_decay * snapshot
     )
     left = lane_half((half, 128))
@@ -286,32 +321,33 @@
         out[0, half:, at] = (mix_share * updated[half:, at] + (1.0 - mix_share) * bottom).astype(BF)
 
 
-def adam(pos, rates, own, far, slot, first, second, totals, weights):
+def adam(pos, rates, own, far, slot, first, second, totals, held, part):
     rows, kv = own.shape
     wide = kv // NH
-    column = pl.BlockSpec((rows, wide), lambda i, *_: (0, i))
-    piece = totals[0].shape[1:]
+    steps = NH // 2
+    column = pl.BlockSpec((rows, wide), lambda i, *_: (0, steps * part + i))
+    share_block = pl.BlockSpec((1,) + totals[0].shape[1:], lambda i, *_: (steps * part + i, 0, 0))
     columns = [in_hbm(a) for a in (own, far, slot, first, second)]
+    in_specs = [column] * 5 + [share_block] * NX + [pl.BlockSpec(memory_space=pl.ANY)] * len(held)
+    in_specs[1] = pl.BlockSpec((rows, wide), lambda i, *_: (0, i))
     return pl.pallas_call(
         adam_kernel,
         grid_spec=pltpu.PrefetchScalarGridSpec(
             num_scalar_prefetch=2,
-            grid=(NH,),
-            in_specs=[column] * 5
-            + [pl.BlockSpec((1,) + piece, lambda i, *_: (i, 0, 0))] * NX
-            + [pl.BlockSpec(memory_space=pl.ANY)],
+            grid=(steps,),
+            in_specs=in_specs,
             out_specs=[
-                pl.BlockSpec((1, rows, wide), lambda i, pos, rates: (pos[0], 0, i)),
+                pl.BlockSpec((1, rows, wide), lambda i, pos, rates: (pos[0], 0, steps * part + i)),
                 column,
                 column,
             ],
-            scratch_shapes=[pltpu.VMEM((NX,) + piece, F32)],
-        ),
-        out_shape=[shape(weights.shape, BF), shape((rows, kv), F32), shape((rows, kv), F32)],
-        input_output_aliases={7 + NX: 0},
+            scratch_shapes=[pltpu.VMEM((NX,) + totals[0].shape[1:], F32)],
+        ),
+        out_shape=[shape(held[0].shape, BF), shape((rows, kv), F32), shape((rows, kv), F32)],
+        input_output_aliases={7 + NX + k: k for k in range(len(held))},
         compiler_params=pltpu.CompilerParams(vmem_limit_bytes=LIMIT),
         name="adam",
-    )(pos, rates, *columns, *totals, weights)
+    )(pos, rates, *columns, *totals, *held)
 
 
 def local(
@@ -337,8 +373,8 @@
     rates = jnp.stack(
         [
             inner_rate * jnp.minimum(F32(1.0), counter / warmup_steps),
-            1.0 - jnp.power(F32(beta_first), counter),
-            1.0 - jnp.power(F32(beta_second), counter),
+            1.0 / (1.0 - jnp.power(F32(beta_first), counter)),
+            1.0 / (1.0 - jnp.power(F32(beta_second), counter)),
         ]
     )
     gain = norm_gain
@@ -347,7 +383,7 @@
         norm_kernel,
         "norm",
         [pltpu.HBM((NY, width // NY + kv, tokens), BF), pltpu.HBM((tokens, 128), F32)],
-        (pos, hidden, gain, key_cotangent),
+        (pos, *(in_hbm(a) for a in (hidden, gain, key_cotangent))),
     )
     both = fsdp_trade(both)
     pos, inv = after(pos, inv)
@@ -362,47 +398,52 @@
     packed = shape((NH, rows // 2, 128), F32)
     (totals,) = call(sum_x_kernel, "sum_x", [packed], (pos, *pieces, *turned))
     pos, totals = after(pos, totals)
+    near_totals = replica_swap(totals, 0)
     w_z, totals = after(w_z, totals)
     w_zc = fsdp_move(w_z, 0, 1)
-    near_totals = replica_swap(totals, 0)
+    pos, w_c, w_zc = lax.optimization_barrier((pos, w_c, w_zc))
+    kept = keep(pos, weights[0])
+    pos, kept = after(pos, kept)
     (totals,) = call(pair_kernel, "sum_h", [packed], (pos, totals, near_totals))
     pos, totals = after(pos, totals)
     far_totals = replica_swap(totals, 1)
-    pos, w_zc = after(pos, w_zc)
 
     both, totals = after(both, totals)
     both_c = fsdp_move(both, 0, 1)
     backs = back_product(pos, (slot, w_z, w_c, w_zc), both)
     pos, backs = after(pos, backs)
-    backs = fsdp_trade(backs).reshape(width, tokens)
-
-    (totals,) = call(pair_kernel, "sum_hh", [packed], (pos, totals, far_totals))
-    pos, totals = after(pos, totals)
+
+    far = []
+    for part in range(2):
+        sums = grad_product(pos, both, both_c, 1, part * kv // 2, (rows, kv // 2), "grad_far")
+        pos, sums = after(pos, sums)
+        if part == 0:
+            (totals,) = call(pair_kernel, "sum_hh", [packed], (pos, totals, far_totals))
+            pos, totals, backs = lax.optimization_barrier((pos, totals, backs))
+            backs = fsdp_trade(backs).reshape(width, tokens)
+        sums, totals = after(sums, totals)
+        far.append(fsdp_move(sums, 1, 0))
     all_totals = [totals] + [replica_turn(totals, d) for d in range(1, NX)]
-    block = [pltpu.HBM((rows, kv), F32)]
-    (far,) = call(functools.partial(grad_kernel, 1), "grad_far", block, (pos, both, both_c))
-    pos, far = after(pos, far)
-    far = fsdp_move(far, 1, 0)
-    (own,) = call(functools.partial(grad_kernel, 0), "grad_near", block, (pos, both, both_c))
+    own = grad_product(pos, both, both_c, 0, 0, (rows, kv), "grad_near")
     pos, own = after(pos, own)
 
     new_global, new_momentum = call(
         outer_kernel, "outer", [shape(turned[0].shape, F32)] * 2, (pos, totals, *turned)
     )
     pos, new_global = after(pos, new_global)
-    kept = keep(pos, weights[0])
-    pos, kept = after(pos, kept)
-
+    held = (kept,)
+    for part in range(2):
+        held = adam(
+            pos, rates, own, far[part], slot, adam_first[0], adam_second[0], all_totals, held, part
+        )
+    layers_out, first_next, second_next = held
+    pos, first_next = after(pos, first_next)
     (hidden_grad,) = call(
         hidden_kernel,
         "hidden_back",
         [shape(hidden.shape, BF)],
         (pos, hidden, gain, inv, backs),
         scratch=[pltpu.VMEM(hidden.shape, F32)],
-    )
-    pos, hidden_grad = after(pos, hidden_grad)
-    layers_out, first_next, second_next = adam(
-        pos, rates, own, far, slot, adam_first[0], adam_second[0], all_totals, kept
     )
     return (
         layers_out[None],

time: 107 us -> 94.2 us (0.88)
  waiting for transfers between devices: 35 us -> 21.4 us
  Pallas kernels: 34.7 us -> 36.6 us
  local copies, waits for them, and re-layouts: 5.1 us -> 3.38 us
    ppermute x2, waiting for transfers between devices: 15.3 us -> 4.56 us  [replica_swap(): return lax.ppermute(array, ('replica', 'fsdp'), pairs)]
    ppermute x5 -> x6, waiting for transfers between devices: 12.7 us -> 4.82 us  [fsdp_move(): lax.ppermute(array, 'fsdp', [(i, i ^ dz * 2 + dc) for i in range(4 * NY)])]
    pallas_call x8 -> x6, Pallas kernels: 18.5 us -> 11.9 us  [call(): pl.pallas_call(kernel, grid_spec=pltpu.PrefetchScalarGridSpec(num_scalar_...]
    pallas_call x0 -> x3, Pallas kernels: none -> 6.04 us  [grad_product(): pl.pallas_call(functools.partial(grad_kernel, dz, begin), grid_spec=pltpu...]
    ppermute x6, waiting for transfers between devices: 6.98 us -> 12 us  [replica_turn(): return lax.ppermute(array, 'replica', pairs)]
    unnamed x28 -> x24, local copies, waits for them, and re-layouts: 5.01 us -> 3.3 us
    ppermute x5 -> x6, starting transfers between devices: 4.42 us -> 5.99 us  [fsdp_move(): lax.ppermute(array, 'fsdp', [(i, i ^ dz * 2 + dc) for i in range(4 * NY)])]
    pallas_call x1 -> x2, Pallas kernels: 5.7 us -> 7.14 us  [adam(): pl.pallas_call(adam_kernel, grid_spec=pltpu.PrefetchScalarGridSpec(num_sc...]
  transfers between devices with their start and end apart: 15 -> 16, of which waited for: 8 -> 9; matrix products, arithmetic and copies ran while one was open for 0% -> 0% of each run, Pallas kernels for 25% -> 30%
where the time goes in v4:
time: 94.2 us; the launch traced here: 93.4 us
  Pallas kernels  36.6 us (39%)
  starting transfers between devices  30.2 us (32%)
  waiting for transfers between devices  21.4 us (23%)
  local copies, waits for them, and re-layouts  3.38 us (4%)
  between operations  1.67 us (2%)
    ppermute x6, waiting for transfers between devices, replica_turn(): return lax.ppermute(array, 'replica', pairs)  12 us
    pallas_call x6, Pallas kernels, call(): pl.pallas_call(kernel, grid_spec=pltpu.PrefetchScalarGridSpec(num_scalar_...  11.9 us
    all_to_all x2, starting transfers between devices, fsdp_trade(): lax.all_to_all(array, 'fsdp', 0, 0, axis_index_groups=groups, tiled=True)  9.72 us
    ppermute x2, starting transfers between devices, replica_swap(): return lax.ppermute(array, ('replica', 'fsdp'), pairs)  7.57 us
    pallas_call x2, Pallas kernels, adam(): pl.pallas_call(adam_kernel, grid_spec=pltpu.PrefetchScalarGridSpec(num_sc...  7.14 us
    ppermute x6, starting transfers between devices, replica_turn(): return lax.ppermute(array, 'replica', pairs)  6.94 us
    pallas_call x3, Pallas kernels, grad_product(): pl.pallas_call(functools.partial(grad_kernel, dz, begin), grid_spec=pltpu...  6.04 us
    ppermute x6, starting transfers between devices, fsdp_move(): lax.ppermute(array, 'fsdp', [(i, i ^ dz * 2 + dc) for i in range(4 * NY)])  5.99 us
  transfers between devices with their start and end apart: 16, of which 9 were waited for; matrix products, arithmetic and copies ran while one was open for 0% of the time, Pallas kernels for 30%

profile of v4, /device:TPU:14, one launch (start us, length us, event | category | flops | bytes accessed | tf_op | source)
XLA Modules:
  0.0 93.4 jit_solution(16254755349805232798)
XLA Ops:
  1.4 4.0 %norm.1 = (bf16[4,2176,128]{2,1,0:T(8,128)(2,1)}, f32[128,128]{1,0:T(8,128)}) custom-call(s32[6]{0:T(128)S(1)} %stack.39.pos, bf16[128,4608]{1,0:T(8,128)(2,1)} %hidden.3, f32[4608]{0:T(1024)} %gain.3, bf16[128,1024]{1,0:T(8,128)(2,1)} %cot.1), custom_call_target="tpu_custom_call" | custom-call | tf_op jit(solution)/shard_map/norm/pallas_call | solution.py:48
  5.5 4.9 %all-to-all-start = ((bf16[4,2176,128]{2,1,0:T(8,128)(2,1)}), bf16[4,2176,128]{2,1,0:T(8,128)(2,1)S(1)}, u32[]{:S(2)}, u32[]{:S(2)}) async-start(bf16[4,2176,128]{2,1,0:T(8,128)(2,1)} %get-tuple-element.75), calls=%async_computation | async-start | bytes 4456448 | tf_op jit(solution)/shard_map/all_to_all | solution.py:69
  10.4 2.7 %pick.1 = (bf16[288,1024]{1,0:T(8,128)(2,1)}, bf16[4,144,128]{2,1,0:T(8,128)(2,1)S(1)}, bf16[4,144,128]{2,1,0:T(8,128)(2,1)S(1)}, bf16[4,144,128]{2,1,0:T(8,128)(2,1)S(1)}, bf16[4,144,128]{2,1,0:T(8,128)(2,1)S(1)}) custom-call(s32[6]{0:T(128)S(1)} %stack.39.pos, bf16[4,288,1024]{2,1,0:T(8,128)(2,1)} %bitcast.25), custom_call_target="tpu_custom_call" | custom-call | tf_op jit(solution)/shard_map/pick/pallas_call | solution.py:112
  13.1 1.9 %collective-permute-start.4 = (bf16[288,1024]{1,0:T(8,128)(2,1)}, bf16[288,1024]{1,0:T(8,128)(2,1)S(1)}, u32[]{:S(2)}, u32[]{:S(2)}) collective-permute-start(bf16[288,1024]{1,0:T(8,128)(2,1)} %get-tuple-element.72.w0.slot), channel_id=1, source_target_pairs={{0,2},{1,3},{2,0},{3,1},{4,6},{5,7},{6,4},{7,5},{8,10},{9,11},{10,... | collective-permute-start | bytes 1769480 | tf_op jit(solution)/shard_map/ppermute | solution.py:64
  15.5 2.4 %collective-permute-start.1 = (bf16[4,144,128]{2,1,0:T(8,128)(2,1)S(1)}, bf16[4,144,128]{2,1,0:T(8,128)(2,1)S(1)}, u32[]{:S(2)}, u32[]{:S(2)}) collective-permute-start(bf16[4,144,128]{2,1,0:T(8,128)(2,1)S(1)} %get-tuple-element.63), channel_id=1, source_target_pairs={{0,32},{16,48},{32,0},{48,16},{64,96},{80,112},{96,64},{112,80},{1... | collective-permute-start | bytes 442376 | tf_op jit(solution)/shard_map/ppermute | solution.py:74
  17.9 3.4 %collective-permute-done.b = bf16[4,144,128]{2,1,0:T(8,128)(2,1)S(1)} collective-permute-done((bf16[4,144,128]{2,1,0:T(8,128)(2,1)S(1)}, bf16[4,144,128]{2,1,0:T(8,128)(2,1)S(1)}, u32[]{:S(2)}, u32[]{:S(2)}) %collective-permute-start) | collective-permute-done | bytes 147488 | tf_op jit(solution)/shard_map/ppermute | solution.py:74
  21.4 2.0 %collective-permute-done.1.c = bf16[4,144,128]{2,1,0:T(8,128)(2,1)S(1)} collective-permute-done((bf16[4,144,128]{2,1,0:T(8,128)(2,1)S(1)}, bf16[4,144,128]{2,1,0:T(8,128)(2,1)S(1)}, u32[]{:S(2)}, u32[]{:S(2)}) %collective-permute-start.1) | collective-permute-done | bytes 147488 | tf_op jit(solution)/shard_map/ppermute | solution.py:74
  25.6 2.4 %collective-permute-done.4.wz = bf16[288,1024]{1,0:T(8,128)(2,1)S(1)} collective-permute-done((bf16[288,1024]{1,0:T(8,128)(2,1)}, bf16[288,1024]{1,0:T(8,128)(2,1)S(1)}, u32[]{:S(2)}, u32[]{:S(2)}) %collective-permute-start.4) | collective-permute-done | bytes 589856 | tf_op jit(solution)/shard_map/ppermute | solution.py:64
  28.0 3.3 %collective-permute-start.6 = (f32[4,144,128]{2,1,0:T(8,128)S(1)}, f32[4,144,128]{2,1,0:T(8,128)S(1)}, u32[]{:S(2)}, u32[]{:S(2)}) collective-permute-start(f32[4,144,128]{2,1,0:T(8,128)S(1)} %sum_x.1.a), channel_id=1, source_target_pairs={{0,64},{1,193},{2,66},{3,195},{4,68},{5,197},{6,70},{7,199},{8,72}... | collective-permute-start | bytes 884744 | tf_op jit(solution)/shard_map/ppermute | solution.py:83
  31.3 4.4 %keep.1.refs_4_ = bf16[4,288,1024]{2,1,0:T(8,128)(2,1)} custom-call(s32[6]{0:T(128)S(1)} %stack.39.pos, bf16[4,288,1024]{2,1,0:T(8,128)(2,1)} %bitcast.26), custom_call_target="tpu_custom_call" | custom-call | tf_op jit(solution)/shard_map/keep/pallas_call | solution.py:133
  35.7 3.5 %collective-permute-done.6.b = f32[4,144,128]{2,1,0:T(8,128)S(1)} collective-permute-done((f32[4,144,128]{2,1,0:T(8,128)S(1)}, f32[4,144,128]{2,1,0:T(8,128)S(1)}, u32[]{:S(2)}, u32[]{:S(2)}) %collective-permute-start.6) | collective-permute-done | bytes 294944 | tf_op jit(solution)/shard_map/ppermute | solution.py:83
  39.9 2.0 %collective-permute-start.7 = (bf16[4,2176,128]{2,1,0:T(8,128)(2,1)S(1)}, bf16[4,2176,128]{2,1,0:T(8,128)(2,1)S(1)}, u32[]{:S(2)}, u32[]{:S(2)}) collective-permute-start(bf16[4,2176,128]{2,1,0:T(8,128)(2,1)S(1)} %all-to-all-done.both.mine), channel_id=1, source_target_pairs={{0,1},{1,0},{2,3},{3,2},{4,5},{5,4},{6,7},{7,6},{8,9},{9,8},{10,11... | collective-permute-start | bytes 6684680 | tf_op jit(solution)/shard_map/ppermute | solution.py:64
  41.9 4.3 %collective-permute-start.8 = (f32[4,144,128]{2,1,0:T(8,128)S(1)}, f32[4,144,128]{2,1,0:T(8,128)S(1)}, u32[]{:S(2)}, u32[]{:S(2)}) collective-permute-start(f32[4,144,128]{2,1,0:T(8,128)S(1)} %sum_h.1.a), channel_id=1, source_target_pairs={{0,192},{1,65},{2,194},{3,67},{4,196},{5,69},{6,198},{7,71},{8,200... | collective-permute-start | bytes 884744 | tf_op jit(solution)/shard_map/ppermute | solution.py:83
  46.2 4.4 %back_product.1 = f32[4,1152,128]{2,1,0:T(8,128)} custom-call(s32[6]{0:T(128)S(1)} %stack.39.pos, bf16[288,1024]{1,0:T(8,128)(2,1)} %get-tuple-element.72.w0.slot, bf16[288,1024]{1,0:T(8,128)(2,1)} %copy-done.10, bf16[288,1024]{1,0:T(8,128)(2,1)} %copy-done.11, bf16[288,1024]{1,0:T(8,128)(2,1)} %collective-permute-done.5.wzc, ...), custom_call_target="tpu_custom_call" | custom-call | tf_op jit(solution)/shard_map/back_product/pallas_call | solution.py:229
  54.1 4.8 %all-to-all-start.1 = ((f32[4,1152,128]{2,1,0:T(8,128)}), f32[4,1152,128]{2,1,0:T(8,128)}, u32[]{:S(2)}, u32[]{:S(2)}) async-start(f32[4,1152,128]{2,1,0:T(8,128)} %back_product.1), calls=%async_computation.1 | async-start | bytes 4718592 | tf_op jit(solution)/shard_map/all_to_all | solution.py:69
  58.9 1.9 %collective-permute-start.13 = (f32[288,512]{1,0:T(8,128)}, f32[288,512]{1,0:T(8,128)}, u32[]{:S(2)}, u32[]{:S(2)}) collective-permute-start(f32[288,512]{1,0:T(8,128)} %grad_far.2), channel_id=1, source_target_pairs={{0,2},{1,3},{2,0},{3,1},{4,6},{5,7},{6,4},{7,5},{8,10},{9,11},{10,... | collective-permute-start | bytes 1769480 | tf_op jit(solution)/shard_map/ppermute | solution.py:64
  62.4 1.9 %grad_far.3 = f32[288,512]{1,0:T(8,128)} custom-call(s32[6]{0:T(128)S(1)} %stack.39.pos, bf16[4,2176,128]{2,1,0:T(8,128)(2,1)S(1)} %all-to-all-done.both.mine, bf16[4,2176,128]{2,1,0:T(8,128)(2,1)S(1)} %copy-done.1), custom_call_target="tpu_custom_call" | custom-call | tf_op jit(solution)/shard_map/grad_far/pallas_call | solution.py:268
  66.4 2.1 %collective-permute-start.10 = (f32[4,144,128]{2,1,0:T(8,128)S(1)}, f32[4,144,128]{2,1,0:T(8,128)}, u32[]{:S(2)}, u32[]{:S(2)}) collective-permute-start(f32[4,144,128]{2,1,0:T(8,128)S(1)} %sum_hh.1.totals.refs_0_), channel_id=1, source_target_pairs={{0,16},{16,32},{32,48},{48,0},{64,80},{80,96},{96,112},{112,64},{1... | collective-permute-start | bytes 884744 | tf_op jit(solution)/shard_map/ppermute | solution.py:74
  70.3 2.3 %grad_near.1.own = f32[288,1024]{1,0:T(8,128)} custom-call(s32[6]{0:T(128)S(1)} %stack.39.pos, bf16[4,2176,128]{2,1,0:T(8,128)(2,1)S(1)} %all-to-all-done.both.mine, bf16[4,2176,128]{2,1,0:T(8,128)(2,1)S(1)} %copy-done.2), custom_call_target="tpu_custom_call" | custom-call | tf_op jit(solution)/shard_map/grad_near/pallas_call | solution.py:268
  74.3 4.4 %collective-permute-done.12.refs_3_ = f32[4,144,128]{2,1,0:T(8,128)} collective-permute-done((f32[4,144,128]{2,1,0:T(8,128)S(1)}, f32[4,144,128]{2,1,0:T(8,128)}, u32[]{:S(2)}, u32[]{:S(2)}) %collective-permute-start.12) | collective-permute-done | bytes 294944 | tf_op jit(solution)/shard_map/ppermute | solution.py:74
  79.3 3.6 %adam.2 = (bf16[4,288,1024]{2,1,0:T(8,128)(2,1)}, f32[288,1024]{1,0:T(8,128)}, f32[288,1024]{1,0:T(8,128)}) custom-call(s32[6]{0:T(128)S(1)} %stack.39.pos, f32[3]{0:T(128)S(1)} %pad_maximum_fusion.rates, f32[288,1024]{1,0:T(8,128)} %grad_near.1.own, f32[288,512]{1,0:T(8,128)} %collective-permute-done.13.far, ...), custom_call_target="tpu_custom_call", output_to_operand_aliasing={{0}: (11, {})} | custom-call | tf_op jit(solution)/shard_map/adam/pallas_call | solution.py:333
  82.9 2.4 %collective-permute-done.9.far = f32[288,512]{1,0:T(8,128)} collective-permute-done((f32[288,512]{1,0:T(8,128)}, f32[288,512]{1,0:T(8,128)}, u32[]{:S(2)}, u32[]{:S(2)}) %collective-permute-start.9) | collective-permute-done | bytes 589856 | tf_op jit(solution)/shard_map/ppermute | solution.py:64
  85.3 3.6 %adam.3 = (bf16[4,288,1024]{2,1,0:T(8,128)(2,1)}, f32[288,1024]{1,0:T(8,128)}, f32[288,1024]{1,0:T(8,128)}) custom-call(s32[6]{0:T(128)S(1)} %stack.39.pos, f32[3]{0:T(128)S(1)} %pad_maximum_fusion.rates, f32[288,1024]{1,0:T(8,128)} %grad_near.1.own, ...), custom_call_target="tpu_custom_call", output_to_operand_aliasing={{0}: (11, {}), {1}: (12, {}), {2}: (13, {})} | custom-call | tf_op jit(solution)/shard_map/adam/pallas_call | solution.py:333
  89.0 4.4 %hidden_back.1 = bf16[128,4608]{1,0:T(8,128)(2,1)} custom-call(s32[6]{0:T(128)S(1)} %stack.39.pos, bf16[128,4608]{1,0:T(8,128)(2,1)S(1)} %copy-done.3, f32[4608]{0:T(1024)S(1)} %copy-done.8, f32[128,128]{1,0:T(8,128)S(1)} %copy-done.9, f32[4608,128]{1,0:T(8,128)} %bitcast.15.backs), custom_call_target="tpu_custom_call" | custom-call | tf_op jit(solution)/shard_map/hidden_back/pallas_call | solution.py:48
  (48 shorter events, 14.5 us)
Async XLA Ops:
  5.5 34.4 %all-to-all-start = ((bf16[4,2176,128]{2,1,0:T(8,128)(2,1)}), bf16[4,2176,128]{2,1,0:T(8,128)(2,1)S(1)}, u32[]{:S(2)}, u32[]{:S(2)}) async-start(bf16[4,2176,128]{2,1,0:T(8,128)(2,1)} %get-tuple-element.75), calls=%async_computation | async-start | bytes 4456448 | tf_op jit(solution)/shard_map/all_to_all | solution.py:69
  10.4 14.5 %copy-start.4 = (f32[4,288,64]{1,2,0:T(8,128)S(1)}, f32[4,288,64]{1,2,0:T(8,128)}, u32[]{:S(2)}) copy-start(f32[4,288,64]{1,2,0:T(8,128)} %param.16) | copy-start | bytes 884740
  10.4 14.5 %copy-start.5 = (f32[4,288,64]{1,2,0:T(8,128)S(1)}, f32[4,288,64]{1,2,0:T(8,128)}, u32[]{:S(2)}) copy-start(f32[4,288,64]{1,2,0:T(8,128)} %param.17) | copy-start | bytes 884740
  13.1 14.9 %collective-permute-start.4 = (bf16[288,1024]{1,0:T(8,128)(2,1)}, bf16[288,1024]{1,0:T(8,128)(2,1)S(1)}, u32[]{:S(2)}, u32[]{:S(2)}) collective-permute-start(bf16[288,1024]{1,0:T(8,128)(2,1)} %get-tuple-element.72.w0.slot), channel_id=1, source_target_pairs={{0,2},{1,3},{2,0},{3,1},{4,6},{5,7},{6,4},{7,5},{8,10},{9,11},{10,... | collective-permute-start | bytes 1769480 | tf_op jit(solution)/shard_map/ppermute | solution.py:64
  15.0 6.3 %collective-permute-start = (bf16[4,144,128]{2,1,0:T(8,128)(2,1)S(1)}, bf16[4,144,128]{2,1,0:T(8,128)(2,1)S(1)}, u32[]{:S(2)}, u32[]{:S(2)}) collective-permute-start(bf16[4,144,128]{2,1,0:T(8,128)(2,1)S(1)} %get-tuple-element.62), channel_id=1, source_target_pairs={{0,16},{16,32},{32,48},{48,0},{64,80},{80,96},{96,112},{112,64},{1... | collective-permute-start | bytes 442376 | tf_op jit(solution)/shard_map/ppermute | solution.py:74
  15.5 7.9 %collective-permute-start.1 = (bf16[4,144,128]{2,1,0:T(8,128)(2,1)S(1)}, bf16[4,144,128]{2,1,0:T(8,128)(2,1)S(1)}, u32[]{:S(2)}, u32[]{:S(2)}) collective-permute-start(bf16[4,144,128]{2,1,0:T(8,128)(2,1)S(1)} %get-tuple-element.63), channel_id=1, source_target_pairs={{0,32},{16,48},{32,0},{48,16},{64,96},{80,112},{96,64},{112,80},{1... | collective-permute-start | bytes 442376 | tf_op jit(solution)/shard_map/ppermute | solution.py:74
  17.9 7.0 %collective-permute-start.2 = (bf16[4,144,128]{2,1,0:T(8,128)(2,1)S(1)}, bf16[4,144,128]{2,1,0:T(8,128)(2,1)S(1)}, u32[]{:S(2)}, u32[]{:S(2)}) collective-permute-start(bf16[4,144,128]{2,1,0:T(8,128)(2,1)S(1)} %get-tuple-element.64), channel_id=1, source_target_pairs={{0,48},{16,0},{32,16},{48,32},{64,112},{80,64},{96,80},{112,96},{1... | collective-permute-start | bytes 442376 | tf_op jit(solution)/shard_map/ppermute | solution.py:74
  17.9 13.4 %collective-permute-start.3 = (bf16[288,1024]{1,0:T(8,128)(2,1)}, bf16[288,1024]{1,0:T(8,128)(2,1)S(1)}, u32[]{:S(2)}, u32[]{:S(2)}) collective-permute-start(bf16[288,1024]{1,0:T(8,128)(2,1)} %get-tuple-element.72.w0.slot), channel_id=1, source_target_pairs={{0,1},{1,0},{2,3},{3,2},{4,5},{5,4},{6,7},{7,6},{8,9},{9,8},{10,11... | collective-permute-start | bytes 1769480 | tf_op jit(solution)/shard_map/ppermute | solution.py:64
  28.0 7.7 %copy-start.10 = (bf16[288,1024]{1,0:T(8,128)(2,1)}, bf16[288,1024]{1,0:T(8,128)(2,1)S(1)}, u32[]{:S(2)}) copy-start(bf16[288,1024]{1,0:T(8,128)(2,1)S(1)} %collective-permute-done.4.wz) | copy-start | bytes 1769476
  28.0 3.3 %collective-permute-start.5 = (bf16[288,1024]{1,0:T(8,128)(2,1)S(1)}, bf16[288,1024]{1,0:T(8,128)(2,1)}, u32[]{:S(2)}, u32[]{:S(2)}) collective-permute-start(bf16[288,1024]{1,0:T(8,128)(2,1)S(1)} %collective-permute-done.4.wz), channel_id=1, source_target_pairs={{0,1},{1,0},{2,3},{3,2},{4,5},{5,4},{6,7},{7,6},{8,9},{9,8},{10,11... | collective-permute-start | bytes 1769480 | tf_op jit(solution)/shard_map/ppermute | solution.py:64
  28.0 11.2 %collective-permute-start.6 = (f32[4,144,128]{2,1,0:T(8,128)S(1)}, f32[4,144,128]{2,1,0:T(8,128)S(1)}, u32[]{:S(2)}, u32[]{:S(2)}) collective-permute-start(f32[4,144,128]{2,1,0:T(8,128)S(1)} %sum_x.1.a), channel_id=1, source_target_pairs={{0,64},{1,193},{2,66},{3,195},{4,68},{5,197},{6,70},{7,199},{8,72}... | collective-permute-start | bytes 884744 | tf_op jit(solution)/shard_map/ppermute | solution.py:83
  31.3 4.4 %copy-start.11 = (bf16[288,1024]{1,0:T(8,128)(2,1)}, bf16[288,1024]{1,0:T(8,128)(2,1)S(1)}, u32[]{:S(2)}) copy-start(bf16[288,1024]{1,0:T(8,128)(2,1)S(1)} %collective-permute-done.3.wc) | copy-start | bytes 1769476
  39.8 10.7 %copy-start.6 = (f32[4,144,128]{2,1,0:T(8,128)}, f32[4,144,128]{2,1,0:T(8,128)S(1)}, u32[]{:S(2)}) copy-start(f32[4,144,128]{2,1,0:T(8,128)S(1)} %sum_h.1.a) | copy-start | bytes 884740
  39.9 10.7 %collective-permute-start.7 = (bf16[4,2176,128]{2,1,0:T(8,128)(2,1)S(1)}, bf16[4,2176,128]{2,1,0:T(8,128)(2,1)S(1)}, u32[]{:S(2)}, u32[]{:S(2)}) collective-permute-start(bf16[4,2176,128]{2,1,0:T(8,128)(2,1)S(1)} %all-to-all-done.both.mine), channel_id=1, source_target_pairs={{0,1},{1,0},{2,3},{3,2},{4,5},{5,4},{6,7},{7,6},{8,9},{9,8},{10,11... | collective-permute-start | bytes 6684680 | tf_op jit(solution)/shard_map/ppermute | solution.py:64
  41.9 11.6 %collective-permute-start.8 = (f32[4,144,128]{2,1,0:T(8,128)S(1)}, f32[4,144,128]{2,1,0:T(8,128)S(1)}, u32[]{:S(2)}, u32[]{:S(2)}) collective-permute-start(f32[4,144,128]{2,1,0:T(8,128)S(1)} %sum_h.1.a), channel_id=1, source_target_pairs={{0,192},{1,65},{2,194},{3,67},{4,196},{5,69},{6,198},{7,71},{8,200... | collective-permute-start | bytes 884744 | tf_op jit(solution)/shard_map/ppermute | solution.py:83
  54.1 34.9 %all-to-all-start.1 = ((f32[4,1152,128]{2,1,0:T(8,128)}), f32[4,1152,128]{2,1,0:T(8,128)}, u32[]{:S(2)}, u32[]{:S(2)}) async-start(f32[4,1152,128]{2,1,0:T(8,128)} %back_product.1), calls=%async_computation.1 | async-start | bytes 4718592 | tf_op jit(solution)/shard_map/all_to_all | solution.py:69
  58.9 20.5 %collective-permute-start.13 = (f32[288,512]{1,0:T(8,128)}, f32[288,512]{1,0:T(8,128)}, u32[]{:S(2)}, u32[]{:S(2)}) collective-permute-start(f32[288,512]{1,0:T(8,128)} %grad_far.2), channel_id=1, source_target_pairs={{0,2},{1,3},{2,0},{3,1},{4,6},{5,7},{6,4},{7,5},{8,10},{9,11},{10,... | collective-permute-start | bytes 1769480 | tf_op jit(solution)/shard_map/ppermute | solution.py:64
  64.3 21.1 %collective-permute-start.9 = (f32[288,512]{1,0:T(8,128)}, f32[288,512]{1,0:T(8,128)}, u32[]{:S(2)}, u32[]{:S(2)}) collective-permute-start(f32[288,512]{1,0:T(8,128)} %grad_far.3), channel_id=1, source_target_pairs={{0,2},{1,3},{2,0},{3,1},{4,6},{5,7},{6,4},{7,5},{8,10},{9,11},{10,... | collective-permute-start | bytes 1769480 | tf_op jit(solution)/shard_map/ppermute | solution.py:64
  64.4 14.3 %collective-permute-start.12 = (f32[4,144,128]{2,1,0:T(8,128)S(1)}, f32[4,144,128]{2,1,0:T(8,128)}, u32[]{:S(2)}, u32[]{:S(2)}) collective-permute-start(f32[4,144,128]{2,1,0:T(8,128)S(1)} %sum_hh.1.totals.refs_0_), channel_id=1, source_target_pairs={{0,48},{16,0},{32,16},{48,32},{64,112},{80,64},{96,80},{112,96},{1... | collective-permute-start | bytes 884744 | tf_op jit(solution)/shard_map/ppermute | solution.py:74
  65.2 13.5 %collective-permute-start.11 = (f32[4,144,128]{2,1,0:T(8,128)S(1)}, f32[4,144,128]{2,1,0:T(8,128)}, u32[]{:S(2)}, u32[]{:S(2)}) collective-permute-start(f32[4,144,128]{2,1,0:T(8,128)S(1)} %sum_hh.1.totals.refs_0_), channel_id=1, source_target_pairs={{0,32},{16,48},{32,0},{48,16},{64,96},{80,112},{96,64},{112,80},{1... | collective-permute-start | bytes 884744 | tf_op jit(solution)/shard_map/ppermute | solution.py:74
  66.4 13.0 %collective-permute-start.10 = (f32[4,144,128]{2,1,0:T(8,128)S(1)}, f32[4,144,128]{2,1,0:T(8,128)}, u32[]{:S(2)}, u32[]{:S(2)}) collective-permute-start(f32[4,144,128]{2,1,0:T(8,128)S(1)} %sum_hh.1.totals.refs_0_), channel_id=1, source_target_pairs={{0,16},{16,32},{32,48},{48,0},{64,80},{80,96},{96,112},{112,64},{1... | collective-permute-start | bytes 884744 | tf_op jit(solution)/shard_map/ppermute | solution.py:74
  85.3 3.6 %copy-start.3 = (bf16[128,4608]{1,0:T(8,128)(2,1)S(1)}, bf16[128,4608]{1,0:T(8,128)(2,1)}, u32[]{:S(2)}) copy-start(bf16[128,4608]{1,0:T(8,128)(2,1)} %hidden.3) | copy-start | bytes 3538948
  85.3 3.6 %copy-start.8 = (f32[4608]{0:T(1024)S(1)}, f32[4608]{0:T(1024)}, u32[]{:S(2)}) copy-start(f32[4608]{0:T(1024)} %gain.3) | copy-start | bytes 55300
  85.3 3.6 %copy-start.9 = (f32[128,128]{1,0:T(8,128)S(1)}, f32[128,128]{1,0:T(8,128)}, u32[]{:S(2)}) copy-start(f32[128,128]{1,0:T(8,128)} %get-tuple-element.102.inv) | copy-start | bytes 196612
  (4 other events, 8.0 us)

commit v5 on v4

--- a/solution.py
+++ b/solution.py
@@ -247,33 +247,36 @@
     )(pos, *(in_hbm(w) for w in weights), both)
 
 
-def grad_kernel(dz, begin, pos, mine, theirs, out):
-    rows, wide = out.shape
+def grad_kernel(dz, pos, mine, theirs, *outs):
+    rows = outs[0].shape[0]
     tokens = mine.shape[2]
     start = (jnp.bitwise_xor(pos[4], dz) * 2 + pos[5]) * rows
     at = pl.ds(pl.multiple_of(start, 32), rows)
     left = jnp.concatenate([both[y, at, :] for both in (mine, theirs) for y in range(NY)], axis=1)
-    for j in range(wide // 256):
-        columns = []
-        for b in (begin // 128 + 2 * j, begin // 128 + 2 * j + 1):
-            lines = slice(4 * rows + b * tokens, 4 * rows + (b + 1) * tokens)
-            blocks = [both[y, lines, :] for both in (mine, theirs) for y in range(NY)]
-            columns.append(jnp.concatenate(blocks, axis=0))
-        out[:, j * 256 : (j + 1) * 256] = jnp.dot(
-            left, jnp.concatenate(columns, axis=1), preferred_element_type=F32
-        )
-
-
-def grad_product(pos, both, both_c, dz, begin, shape_out, name):
-    return pl.pallas_call(
-        functools.partial(grad_kernel, dz, begin),
+    b = 0
+    for out in outs:
+        for j in range(out.shape[1] // 256):
+            columns = []
+            for _ in range(2):
+                lines = slice(4 * rows + b * tokens, 4 * rows + (b + 1) * tokens)
+                blocks = [both[y, lines, :] for both in (mine, theirs) for y in range(NY)]
+                columns.append(jnp.concatenate(blocks, axis=0))
+                b += 1
+            out[:, j * 256 : (j + 1) * 256] = jnp.dot(
+                left, jnp.concatenate(columns, axis=1), preferred_element_type=F32
+            )
+
+
+def grad_product(pos, both, both_c, dz, rows, widths, name):
+    return pl.pallas_call(
+        functools.partial(grad_kernel, dz),
         grid_spec=pltpu.PrefetchScalarGridSpec(
             num_scalar_prefetch=1,
             grid=(1,),
             in_specs=[pl.BlockSpec(memory_space=pltpu.VMEM)] * 2,
-            out_specs=whole(shape_out),
-        ),
-        out_shape=pltpu.HBM(shape_out, F32),
+            out_specs=[whole((rows, wide)) for wide in widths],
+        ),
+        out_shape=[pltpu.HBM((rows, wide), F32) for wide in widths],
         compiler_params=pltpu.CompilerParams(vmem_limit_bytes=LIMIT),
         name=name,
     )(pos, both, both_c)
@@ -321,12 +324,13 @@
         out[0, half:, at] = (mix_share * updated[half:, at] + (1.0 - mix_share) * bottom).astype(BF)
 
 
-def adam(pos, rates, own, far, slot, first, second, totals, held, part):
+def adam(pos, rates, own, far, slot, first, second, totals, held, begin):
     rows, kv = own.shape
     wide = kv // NH
-    steps = NH // 2
-    column = pl.BlockSpec((rows, wide), lambda i, *_: (0, steps * part + i))
-    share_block = pl.BlockSpec((1,) + totals[0].shape[1:], lambda i, *_: (steps * part + i, 0, 0))
+    steps = far.shape[1] // wide
+    skip = begin // wide
+    column = pl.BlockSpec((rows, wide), lambda i, *_: (0, skip + i))
+    share_block = pl.BlockSpec((1,) + totals[0].shape[1:], lambda i, *_: (skip + i, 0, 0))
     columns = [in_hbm(a) for a in (own, far, slot, first, second)]
     in_specs = [column] * 5 + [share_block] * NX + [pl.BlockSpec(memory_space=pl.ANY)] * len(held)
     in_specs[1] = pl.BlockSpec((rows, wide), lambda i, *_: (0, i))
@@ -337,7 +341,7 @@
             grid=(steps,),
             in_specs=in_specs,
             out_specs=[
-                pl.BlockSpec((1, rows, wide), lambda i, pos, rates: (pos[0], 0, steps * part + i)),
+                pl.BlockSpec((1, rows, wide), lambda i, pos, rates: (pos[0], 0, skip + i)),
                 column,
                 column,
             ],
@@ -348,6 +352,60 @@
         compiler_params=pltpu.CompilerParams(vmem_limit_bytes=LIMIT),
         name="adam",
     )(pos, rates, *columns, *totals, *held)
+
+
+def last_kernel(pos, rates, hidden, gain, inv, backs, own, far, slot, first, second, *refs):
+    totals, (hidden_out, out, first_out, second_out, scratch, ordered) = refs[:NX], refs[-6:]
+    hidden_kernel(pos, hidden, gain, inv, backs, hidden_out, scratch)
+    wide = 64 * NX
+    for k in range(own.shape[1] // wide):
+        at = slice(k * wide, (k + 1) * wide)
+        adam_kernel(
+            pos,
+            rates,
+            *(a.at[:, at] for a in (own, far, slot, first, second)),
+            *(t.at[k : k + 1] for t in totals),
+            out.at[:, :, at],
+            first_out.at[:, at],
+            second_out.at[:, at],
+            ordered,
+        )
+
+
+def last(pos, rates, hidden, gain, inv, backs, own, far, slot, first, second, totals, held):
+    rows, kv = own.shape
+    wide = far.shape[1]
+    end = kv // wide - 1
+    column = pl.BlockSpec((rows, wide), lambda *_: (0, end))
+    share_block = pl.BlockSpec((NH * wide // kv,) + totals[0].shape[1:], lambda *_: (end, 0, 0))
+    tokens = [in_hbm(a) for a in (hidden, gain, inv, backs)]
+    columns = [in_hbm(a) for a in (own, far, slot, first, second)]
+    return pl.pallas_call(
+        last_kernel,
+        grid_spec=pltpu.PrefetchScalarGridSpec(
+            num_scalar_prefetch=2,
+            grid=(1,),
+            in_specs=[whole(a.shape) for a in tokens]
+            + [column, whole(far.shape)]
+            + [column] * 3
+            + [share_block] * NX
+            + [ANY] * 3,
+            out_specs=[
+                whole(hidden.shape),
+                pl.BlockSpec((1, rows, wide), lambda i, pos, rates: (pos[0], 0, end)),
+                column,
+                column,
+            ],
+            scratch_shapes=[
+                pltpu.VMEM(hidden.shape, F32),
+                pltpu.VMEM((NX,) + totals[0].shape[1:], F32),
+            ],
+        ),
+        out_shape=[shape(hidden.shape, BF)] + [shape(a.shape, a.dtype) for a in held],
+        input_output_aliases={11 + NX + k: 1 + k for k in range(3)},
+        compiler_params=pltpu.CompilerParams(vmem_limit_bytes=2 * LIMIT),
+        name="last",
+    )(pos, rates, *tokens, *columns, *totals, *held)
 
 
 def local(
@@ -364,6 +422,7 @@
     tokens, width = hidden.shape
     rows, kv = weights.shape[2:]
     frag_index = inner_step % FRAGS
+    widths = [kv // 2, kv // 4, kv // 4]
     replica = lax.axis_index("replica")
     place = lax.axis_index("fsdp")
     pos = jnp.stack(
@@ -413,37 +472,40 @@
     backs = back_product(pos, (slot, w_z, w_c, w_zc), both)
     pos, backs = after(pos, backs)
 
-    far = []
-    for part in range(2):
-        sums = grad_product(pos, both, both_c, 1, part * kv // 2, (rows, kv // 2), "grad_far")
-        pos, sums = after(pos, sums)
-        if part == 0:
-            (totals,) = call(pair_kernel, "sum_hh", [packed], (pos, totals, far_totals))
-            pos, totals, backs = lax.optimization_barrier((pos, totals, backs))
-            backs = fsdp_trade(backs).reshape(width, tokens)
-        sums, totals = after(sums, totals)
-        far.append(fsdp_move(sums, 1, 0))
+    sums = grad_product(pos, both, both_c, 1, rows, widths, "grad_far")
+    pos, *sums = lax.optimization_barrier((pos, *sums))
+    (totals,) = call(pair_kernel, "sum_hh", [packed], (pos, totals, far_totals))
+    pos, totals, backs, *sums = lax.optimization_barrier((pos, totals, backs, *sums))
+    backs = fsdp_trade(backs).reshape(width, tokens)
+    far = [fsdp_move(part, 1, 0) for part in sums]
     all_totals = [totals] + [replica_turn(totals, d) for d in range(1, NX)]
-    own = grad_product(pos, both, both_c, 0, 0, (rows, kv), "grad_near")
+    (own,) = grad_product(pos, both, both_c, 0, rows, [kv], "grad_near")
     pos, own = after(pos, own)
 
     new_global, new_momentum = call(
         outer_kernel, "outer", [shape(turned[0].shape, F32)] * 2, (pos, totals, *turned)
     )
     pos, new_global = after(pos, new_global)
-    held = (kept,)
-    for part in range(2):
+    held, begin = (kept,), 0
+    for part in far[:-1]:
         held = adam(
-            pos, rates, own, far[part], slot, adam_first[0], adam_second[0], all_totals, held, part
+            pos, rates, own, part, slot, adam_first[0], adam_second[0], all_totals, held, begin
         )
-    layers_out, first_next, second_next = held
-    pos, first_next = after(pos, first_next)
-    (hidden_grad,) = call(
-        hidden_kernel,
-        "hidden_back",
-        [shape(hidden.shape, BF)],
-        (pos, hidden, gain, inv, backs),
-        scratch=[pltpu.VMEM(hidden.shape, F32)],
+        begin += part.shape[1]
+    hidden_grad, layers_out, first_next, second_next = last(
+        pos,
+        rates,
+        hidden,
+        gain,
+        inv,
+        backs,
+        own,
+        far[-1],
+        slot,
+        adam_first[0],
+        adam_second[0],
+        all_totals,
+        held,
     )
     return (
         layers_out[None],

time: 94.2 us -> 93.5 us (level)
  starting transfers between devices: 30.2 us -> 31.9 us
  local copies, waits for them, and re-layouts: 3.38 us -> 1.74 us
  Pallas kernels: 36.6 us -> 35.3 us
    pallas_call x6 -> x5, Pallas kernels: 11.9 us -> 7.49 us  [call(): pl.pallas_call(kernel, grid_spec=pltpu.PrefetchScalarGridSpec(num_scalar_...]
    pallas_call x3, Pallas kernels: 6.04 us -> 9.89 us  [the longest x1 5.35 us: last(): pl.pallas_call(last_kernel, grid_spec=pltpu.PrefetchScalarGridSpec(num_sc...]
    ppermute x6, waiting for transfers between devices: 12 us -> 15.7 us  [replica_turn(): return lax.ppermute(array, 'replica', pairs)]
    ppermute x6 -> x7, waiting for transfers between devices: 4.82 us -> 2.4 us  [fsdp_move(): lax.ppermute(array, 'fsdp', [(i, i ^ dz * 2 + dc) for i in range(4 * NY)])]
    ppermute x6 -> x7, starting transfers between devices: 5.99 us -> 7.64 us  [fsdp_move(): lax.ppermute(array, 'fsdp', [(i, i ^ dz * 2 + dc) for i in range(4 * NY)])]
    unnamed x24 -> x16, local copies, waits for them, and re-layouts: 3.3 us -> 1.66 us
  transfers between devices with their start and end apart: 16 -> 17, of which waited for: 9 -> 7; matrix products, arithmetic and copies ran while one was open for 0% -> 0% of each run, Pallas kernels for 30% -> 27%
where the time goes in v5:
time: 93.5 us; the launch traced here: 93 us
  Pallas kernels  35.3 us (38%)
  starting transfers between devices  31.9 us (34%)
  waiting for transfers between devices  22.3 us (24%)
  local copies, waits for them, and re-layouts  1.74 us (2%)
  between operations  1.61 us (2%)
    ppermute x6, waiting for transfers between devices, replica_turn(): return lax.ppermute(array, 'replica', pairs)  15.7 us
    all_to_all x2, starting transfers between devices, fsdp_trade(): lax.all_to_all(array, 'fsdp', 0, 0, axis_index_groups=groups, tiled=True)  9.72 us
    ppermute x7, starting transfers between devices, fsdp_move(): lax.ppermute(array, 'fsdp', [(i, i ^ dz * 2 + dc) for i in range(4 * NY)])  7.64 us
    ppermute x2, starting transfers between devices, replica_swap(): return lax.ppermute(array, ('replica', 'fsdp'), pairs)  7.57 us
    pallas_call x5, Pallas kernels, call(): pl.pallas_call(kernel, grid_spec=pltpu.PrefetchScalarGridSpec(num_scalar_...  7.49 us
    ppermute x6, starting transfers between devices, replica_turn(): return lax.ppermute(array, 'replica', pairs)  6.94 us
    pallas_call x2, Pallas kernels, adam(): pl.pallas_call(adam_kernel, grid_spec=pltpu.PrefetchScalarGridSpec(num_sc...  6.45 us
    pallas_call x1, Pallas kernels, last(): pl.pallas_call(last_kernel, grid_spec=pltpu.PrefetchScalarGridSpec(num_sc...  5.35 us
  transfers between devices with their start and end apart: 17, of which 7 were waited for; matrix products, arithmetic and copies ran while one was open for 0% of the time, Pallas kernels for 27%

profile of v5, /device:TPU:14, one launch (start us, length us, event | category | flops | bytes accessed | tf_op | source)
XLA Modules:
  0.0 93.0 jit_solution(4535194353171813005)
XLA Ops:
  1.4 4.0 %norm.1 = (bf16[4,2176,128]{2,1,0:T(8,128)(2,1)}, f32[128,128]{1,0:T(8,128)}) custom-call(s32[6]{0:T(128)S(1)} %stack.39.pos, bf16[128,4608]{1,0:T(8,128)(2,1)} %hidden.3, f32[4608]{0:T(1024)} %gain.3, bf16[128,1024]{1,0:T(8,128)(2,1)} %cot.1), custom_call_target="tpu_custom_call" | custom-call | tf_op jit(solution)/shard_map/norm/pallas_call | solution.py:48
  5.5 4.9 %all-to-all-start = ((bf16[4,2176,128]{2,1,0:T(8,128)(2,1)}), bf16[4,2176,128]{2,1,0:T(8,128)(2,1)S(1)}, u32[]{:S(2)}, u32[]{:S(2)}) async-start(bf16[4,2176,128]{2,1,0:T(8,128)(2,1)} %get-tuple-element.79), calls=%async_computation | async-start | bytes 4456448 | tf_op jit(solution)/shard_map/all_to_all | solution.py:69
  10.4 2.7 %pick.1 = (bf16[288,1024]{1,0:T(8,128)(2,1)}, bf16[4,144,128]{2,1,0:T(8,128)(2,1)S(1)}, bf16[4,144,128]{2,1,0:T(8,128)(2,1)S(1)}, bf16[4,144,128]{2,1,0:T(8,128)(2,1)S(1)}, bf16[4,144,128]{2,1,0:T(8,128)(2,1)S(1)}) custom-call(s32[6]{0:T(128)S(1)} %stack.39.pos, bf16[4,288,1024]{2,1,0:T(8,128)(2,1)} %bitcast.31), custom_call_target="tpu_custom_call" | custom-call | tf_op jit(solution)/shard_map/pick/pallas_call | solution.py:112
  13.1 1.9 %collective-permute-start.4 = (bf16[288,1024]{1,0:T(8,128)(2,1)}, bf16[288,1024]{1,0:T(8,128)(2,1)S(1)}, u32[]{:S(2)}, u32[]{:S(2)}) collective-permute-start(bf16[288,1024]{1,0:T(8,128)(2,1)} %get-tuple-element.76.w0.slot), channel_id=1, source_target_pairs={{0,2},{1,3},{2,0},{3,1},{4,6},{5,7},{6,4},{7,5},{8,10},{9,11},{10,... | collective-permute-start | bytes 1769480 | tf_op jit(solution)/shard_map/ppermute | solution.py:64
  15.5 2.4 %collective-permute-start.1 = (bf16[4,144,128]{2,1,0:T(8,128)(2,1)S(1)}, bf16[4,144,128]{2,1,0:T(8,128)(2,1)S(1)}, u32[]{:S(2)}, u32[]{:S(2)}) collective-permute-start(bf16[4,144,128]{2,1,0:T(8,128)(2,1)S(1)} %get-tuple-element.67), channel_id=1, source_target_pairs={{0,32},{16,48},{32,0},{48,16},{64,96},{80,112},{96,64},{112,80},{1... | collective-permute-start | bytes 442376 | tf_op jit(solution)/shard_map/ppermute | solution.py:74
  17.9 3.4 %collective-permute-done.b = bf16[4,144,128]{2,1,0:T(8,128)(2,1)S(1)} collective-permute-done((bf16[4,144,128]{2,1,0:T(8,128)(2,1)S(1)}, bf16[4,144,128]{2,1,0:T(8,128)(2,1)S(1)}, u32[]{:S(2)}, u32[]{:S(2)}) %collective-permute-start) | collective-permute-done | bytes 147488 | tf_op jit(solution)/shard_map/ppermute | solution.py:74
  21.3 2.0 %collective-permute-done.1.c = bf16[4,144,128]{2,1,0:T(8,128)(2,1)S(1)} collective-permute-done((bf16[4,144,128]{2,1,0:T(8,128)(2,1)S(1)}, bf16[4,144,128]{2,1,0:T(8,128)(2,1)S(1)}, u32[]{:S(2)}, u32[]{:S(2)}) %collective-permute-start.1) | collective-permute-done | bytes 147488 | tf_op jit(solution)/shard_map/ppermute | solution.py:74
  25.6 2.4 %collective-permute-done.4.wz = bf16[288,1024]{1,0:T(8,128)(2,1)S(1)} collective-permute-done((bf16[288,1024]{1,0:T(8,128)(2,1)}, bf16[288,1024]{1,0:T(8,128)(2,1)S(1)}, u32[]{:S(2)}, u32[]{:S(2)}) %collective-permute-start.4) | collective-permute-done | bytes 589856 | tf_op jit(solution)/shard_map/ppermute | solution.py:64
  28.0 3.3 %collective-permute-start.6 = (f32[4,144,128]{2,1,0:T(8,128)S(1)}, f32[4,144,128]{2,1,0:T(8,128)S(1)}, u32[]{:S(2)}, u32[]{:S(2)}) collective-permute-start(f32[4,144,128]{2,1,0:T(8,128)S(1)} %sum_x.1.a), channel_id=1, source_target_pairs={{0,64},{1,193},{2,66},{3,195},{4,68},{5,197},{6,70},{7,199},{8,72}... | collective-permute-start | bytes 884744 | tf_op jit(solution)/shard_map/ppermute | solution.py:83
  31.3 4.4 %keep.1.refs_4_ = bf16[4,288,1024]{2,1,0:T(8,128)(2,1)} custom-call(s32[6]{0:T(128)S(1)} %stack.39.pos, bf16[4,288,1024]{2,1,0:T(8,128)(2,1)} %bitcast.32), custom_call_target="tpu_custom_call" | custom-call | tf_op jit(solution)/shard_map/keep/pallas_call | solution.py:133
  35.7 3.5 %collective-permute-done.6.b = f32[4,144,128]{2,1,0:T(8,128)S(1)} collective-permute-done((f32[4,144,128]{2,1,0:T(8,128)S(1)}, f32[4,144,128]{2,1,0:T(8,128)S(1)}, u32[]{:S(2)}, u32[]{:S(2)}) %collective-permute-start.6) | collective-permute-done | bytes 294944 | tf_op jit(solution)/shard_map/ppermute | solution.py:83
  39.8 2.0 %collective-permute-start.7 = (bf16[4,2176,128]{2,1,0:T(8,128)(2,1)S(1)}, bf16[4,2176,128]{2,1,0:T(8,128)(2,1)S(1)}, u32[]{:S(2)}, u32[]{:S(2)}) collective-permute-start(bf16[4,2176,128]{2,1,0:T(8,128)(2,1)S(1)} %all-to-all-done.both.mine), channel_id=1, source_target_pairs={{0,1},{1,0},{2,3},{3,2},{4,5},{5,4},{6,7},{7,6},{8,9},{9,8},{10,11... | collective-permute-start | bytes 6684680 | tf_op jit(solution)/shard_map/ppermute | solution.py:64
  41.9 4.3 %collective-permute-start.8 = (f32[4,144,128]{2,1,0:T(8,128)S(1)}, f32[4,144,128]{2,1,0:T(8,128)S(1)}, u32[]{:S(2)}, u32[]{:S(2)}) collective-permute-start(f32[4,144,128]{2,1,0:T(8,128)S(1)} %sum_h.1.a), channel_id=1, source_target_pairs={{0,192},{1,65},{2,194},{3,67},{4,196},{5,69},{6,198},{7,71},{8,200... | collective-permute-start | bytes 884744 | tf_op jit(solution)/shard_map/ppermute | solution.py:83
  46.2 4.4 %back_product.1 = f32[4,1152,128]{2,1,0:T(8,128)} custom-call(s32[6]{0:T(128)S(1)} %stack.39.pos, bf16[288,1024]{1,0:T(8,128)(2,1)} %get-tuple-element.76.w0.slot, bf16[288,1024]{1,0:T(8,128)(2,1)} %copy-done.6, bf16[288,1024]{1,0:T(8,128)(2,1)} %copy-done.7, bf16[288,1024]{1,0:T(8,128)(2,1)} %collective-permute-done.5.wzc, ...), custom_call_target="tpu_custom_call" | custom-call | tf_op jit(solution)/shard_map/back_product/pallas_call | solution.py:229
  50.6 2.2 %grad_far.1 = (f32[288,512]{1,0:T(8,128)}, f32[288,256]{1,0:T(8,128)}, f32[288,256]{1,0:T(8,128)}) custom-call(s32[6]{0:T(128)S(1)} %stack.39.pos, bf16[4,2176,128]{2,1,0:T(8,128)(2,1)S(1)} %all-to-all-done.both.mine, bf16[4,2176,128]{2,1,0:T(8,128)(2,1)S(1)} %collective-permute-done.7.theirs), custom_call_target="tpu_custom_call" | custom-call | tf_op jit(solution)/shard_map/grad_far/pallas_call | solution.py:271
  54.0 4.8 %all-to-all-start.1 = ((f32[4,1152,128]{2,1,0:T(8,128)}), f32[4,1152,128]{2,1,0:T(8,128)}, u32[]{:S(2)}, u32[]{:S(2)}) async-start(f32[4,1152,128]{2,1,0:T(8,128)} %back_product.1), calls=%async_computation.1 | async-start | bytes 4718592 | tf_op jit(solution)/shard_map/all_to_all | solution.py:69
  58.8 1.9 %collective-permute-start.14 = (f32[288,512]{1,0:T(8,128)}, f32[288,512]{1,0:T(8,128)}, u32[]{:S(2)}, u32[]{:S(2)}) collective-permute-start(f32[288,512]{1,0:T(8,128)} %get-tuple-element.102), channel_id=1, source_target_pairs={{0,2},{1,3},{2,0},{3,1},{4,6},{5,7},{6,4},{7,5},{8,10},{9,11},{10,... | collective-permute-start | bytes 1769480 | tf_op jit(solution)/shard_map/ppermute | solution.py:64
  62.6 2.1 %collective-permute-start.10 = (f32[4,144,128]{2,1,0:T(8,128)S(1)}, f32[4,144,128]{2,1,0:T(8,128)S(1)}, u32[]{:S(2)}, u32[]{:S(2)}) collective-permute-start(f32[4,144,128]{2,1,0:T(8,128)S(1)} %sum_hh.1.totals.refs_0_), channel_id=1, source_target_pairs={{0,16},{16,32},{32,48},{48,0},{64,80},{80,96},{96,112},{112,64},{1... | collective-permute-start | bytes 884744 | tf_op jit(solution)/shard_map/ppermute | solution.py:74
  64.9 8.7 %collective-permute-done.12.refs_3_ = f32[4,144,128]{2,1,0:T(8,128)S(1)} collective-permute-done((f32[4,144,128]{2,1,0:T(8,128)S(1)}, f32[4,144,128]{2,1,0:T(8,128)S(1)}, u32[]{:S(2)}, u32[]{:S(2)}) %collective-permute-start.12) | collective-permute-done | bytes 294944 | tf_op jit(solution)/shard_map/ppermute | solution.py:74
  73.6 1.7 %collective-permute-start.9 = (f32[288,256]{1,0:T(8,128)}, f32[288,256]{1,0:T(8,128)}, u32[]{:S(2)}, u32[]{:S(2)}) collective-permute-start(f32[288,256]{1,0:T(8,128)} %get-tuple-element.100), channel_id=1, source_target_pairs={{0,2},{1,3},{2,0},{3,1},{4,6},{5,7},{6,4},{7,5},{8,10},{9,11},{10,... | collective-permute-start | bytes 884744 | tf_op jit(solution)/shard_map/ppermute | solution.py:64
  77.2 2.4 %grad_near.1.own = f32[288,1024]{1,0:T(8,128)} custom-call(s32[6]{0:T(128)S(1)} %stack.39.pos, bf16[4,2176,128]{2,1,0:T(8,128)(2,1)S(1)} %all-to-all-done.both.mine, bf16[4,2176,128]{2,1,0:T(8,128)(2,1)S(1)} %copy-done.1), custom_call_target="tpu_custom_call" | custom-call | tf_op jit(solution)/shard_map/grad_near/pallas_call | solution.py:271
  81.1 3.4 %adam.2 = (bf16[4,288,1024]{2,1,0:T(8,128)(2,1)}, f32[288,1024]{1,0:T(8,128)}, f32[288,1024]{1,0:T(8,128)}) custom-call(s32[6]{0:T(128)S(1)} %stack.39.pos, f32[3]{0:T(128)S(1)} %pad_maximum_fusion.rates, f32[288,1024]{1,0:T(8,128)} %grad_near.1.own, f32[288,512]{1,0:T(8,128)} %collective-permute-done.14.far, ...), custom_call_target="tpu_custom_call", output_to_operand_aliasing={{0}: (11, {})} | custom-call | tf_op jit(solution)/shard_map/adam/pallas_call | solution.py:337
  84.6 3.0 %adam.3 = (bf16[4,288,1024]{2,1,0:T(8,128)(2,1)}, f32[288,1024]{1,0:T(8,128)}, f32[288,1024]{1,0:T(8,128)}) custom-call(s32[6]{0:T(128)S(1)} %stack.39.pos, f32[3]{0:T(128)S(1)} %pad_maximum_fusion.rates, f32[288,1024]{1,0:T(8,128)} %grad_near.1.own, ...), custom_call_target="tpu_custom_call", output_to_operand_aliasing={{0}: (11, {}), {1}: (12, {}), {2}: (13, {})} | custom-call | tf_op jit(solution)/shard_map/adam/pallas_call | solution.py:337
  87.6 5.4 %last.1 = (bf16[128,4608]{1,0:T(8,128)(2,1)}, bf16[4,288,1024]{2,1,0:T(8,128)(2,1)}, f32[288,1024]{1,0:T(8,128)}, f32[288,1024]{1,0:T(8,128)}) custom-call(s32[6]{0:T(128)S(1)} %stack.39.pos, f32[3]{0:T(128)S(1)} %pad_maximum_fusion.rates, bf16[128,4608]{1,0:T(8,128)(2,1)} %hidden.3, ...), custom_call_target="tpu_custom_call", output_to_operand_aliasing={{1}: (15, {}), {2}: (16, {}), {3}: (17, {})} | custom-call | tf_op jit(solution)/shard_map/last/pallas_call | solution.py:383
  (41 shorter events, 10.1 us)
Async XLA Ops:
  5.5 34.3 %all-to-all-start = ((bf16[4,2176,128]{2,1,0:T(8,128)(2,1)}), bf16[4,2176,128]{2,1,0:T(8,128)(2,1)S(1)}, u32[]{:S(2)}, u32[]{:S(2)}) async-start(bf16[4,2176,128]{2,1,0:T(8,128)(2,1)} %get-tuple-element.79), calls=%async_computation | async-start | bytes 4456448 | tf_op jit(solution)/shard_map/all_to_all | solution.py:69
  10.4 14.5 %copy-start.2 = (f32[4,288,64]{1,2,0:T(8,128)S(1)}, f32[4,288,64]{1,2,0:T(8,128)}, u32[]{:S(2)}) copy-start(f32[4,288,64]{1,2,0:T(8,128)} %param.16) | copy-start | bytes 884740
  10.4 14.5 %copy-start.4 = (f32[4,288,64]{1,2,0:T(8,128)S(1)}, f32[4,288,64]{1,2,0:T(8,128)}, u32[]{:S(2)}) copy-start(f32[4,288,64]{1,2,0:T(8,128)} %param.17) | copy-start | bytes 884740
  13.1 14.9 %collective-permute-start.4 = (bf16[288,1024]{1,0:T(8,128)(2,1)}, bf16[288,1024]{1,0:T(8,128)(2,1)S(1)}, u32[]{:S(2)}, u32[]{:S(2)}) collective-permute-start(bf16[288,1024]{1,0:T(8,128)(2,1)} %get-tuple-element.76.w0.slot), channel_id=1, source_target_pairs={{0,2},{1,3},{2,0},{3,1},{4,6},{5,7},{6,4},{7,5},{8,10},{9,11},{10,... | collective-permute-start | bytes 1769480 | tf_op jit(solution)/shard_map/ppermute | solution.py:64
  15.0 6.3 %collective-permute-start = (bf16[4,144,128]{2,1,0:T(8,128)(2,1)S(1)}, bf16[4,144,128]{2,1,0:T(8,128)(2,1)S(1)}, u32[]{:S(2)}, u32[]{:S(2)}) collective-permute-start(bf16[4,144,128]{2,1,0:T(8,128)(2,1)S(1)} %get-tuple-element.66), channel_id=1, source_target_pairs={{0,16},{16,32},{32,48},{48,0},{64,80},{80,96},{96,112},{112,64},{1... | collective-permute-start | bytes 442376 | tf_op jit(solution)/shard_map/ppermute | solution.py:74
  15.5 7.9 %collective-permute-start.1 = (bf16[4,144,128]{2,1,0:T(8,128)(2,1)S(1)}, bf16[4,144,128]{2,1,0:T(8,128)(2,1)S(1)}, u32[]{:S(2)}, u32[]{:S(2)}) collective-permute-start(bf16[4,144,128]{2,1,0:T(8,128)(2,1)S(1)} %get-tuple-element.67), channel_id=1, source_target_pairs={{0,32},{16,48},{32,0},{48,16},{64,96},{80,112},{96,64},{112,80},{1... | collective-permute-start | bytes 442376 | tf_op jit(solution)/shard_map/ppermute | solution.py:74
  17.9 7.0 %collective-permute-start.2 = (bf16[4,144,128]{2,1,0:T(8,128)(2,1)S(1)}, bf16[4,144,128]{2,1,0:T(8,128)(2,1)S(1)}, u32[]{:S(2)}, u32[]{:S(2)}) collective-permute-start(bf16[4,144,128]{2,1,0:T(8,128)(2,1)S(1)} %get-tuple-element.68), channel_id=1, source_target_pairs={{0,48},{16,0},{32,16},{48,32},{64,112},{80,64},{96,80},{112,96},{1... | collective-permute-start | bytes 442376 | tf_op jit(solution)/shard_map/ppermute | solution.py:74
  17.9 13.4 %collective-permute-start.3 = (bf16[288,1024]{1,0:T(8,128)(2,1)}, bf16[288,1024]{1,0:T(8,128)(2,1)S(1)}, u32[]{:S(2)}, u32[]{:S(2)}) collective-permute-start(bf16[288,1024]{1,0:T(8,128)(2,1)} %get-tuple-element.76.w0.slot), channel_id=1, source_target_pairs={{0,1},{1,0},{2,3},{3,2},{4,5},{5,4},{6,7},{7,6},{8,9},{9,8},{10,11... | collective-permute-start | bytes 1769480 | tf_op jit(solution)/shard_map/ppermute | solution.py:64
  28.0 7.7 %copy-start.6 = (bf16[288,1024]{1,0:T(8,128)(2,1)}, bf16[288,1024]{1,0:T(8,128)(2,1)S(1)}, u32[]{:S(2)}) copy-start(bf16[288,1024]{1,0:T(8,128)(2,1)S(1)} %collective-permute-done.4.wz) | copy-start | bytes 1769476
  28.0 3.3 %collective-permute-start.5 = (bf16[288,1024]{1,0:T(8,128)(2,1)S(1)}, bf16[288,1024]{1,0:T(8,128)(2,1)}, u32[]{:S(2)}, u32[]{:S(2)}) collective-permute-start(bf16[288,1024]{1,0:T(8,128)(2,1)S(1)} %collective-permute-done.4.wz), channel_id=1, source_target_pairs={{0,1},{1,0},{2,3},{3,2},{4,5},{5,4},{6,7},{7,6},{8,9},{9,8},{10,11... | collective-permute-start | bytes 1769480 | tf_op jit(solution)/shard_map/ppermute | solution.py:64
  28.0 11.2 %collective-permute-start.6 = (f32[4,144,128]{2,1,0:T(8,128)S(1)}, f32[4,144,128]{2,1,0:T(8,128)S(1)}, u32[]{:S(2)}, u32[]{:S(2)}) collective-permute-start(f32[4,144,128]{2,1,0:T(8,128)S(1)} %sum_x.1.a), channel_id=1, source_target_pairs={{0,64},{1,193},{2,66},{3,195},{4,68},{5,197},{6,70},{7,199},{8,72}... | collective-permute-start | bytes 884744 | tf_op jit(solution)/shard_map/ppermute | solution.py:83
  31.3 4.4 %copy-start.7 = (bf16[288,1024]{1,0:T(8,128)(2,1)}, bf16[288,1024]{1,0:T(8,128)(2,1)S(1)}, u32[]{:S(2)}) copy-start(bf16[288,1024]{1,0:T(8,128)(2,1)S(1)} %collective-permute-done.3.wc) | copy-start | bytes 1769476
  39.8 10.7 %collective-permute-start.7 = (bf16[4,2176,128]{2,1,0:T(8,128)(2,1)S(1)}, bf16[4,2176,128]{2,1,0:T(8,128)(2,1)S(1)}, u32[]{:S(2)}, u32[]{:S(2)}) collective-permute-start(bf16[4,2176,128]{2,1,0:T(8,128)(2,1)S(1)} %all-to-all-done.both.mine), channel_id=1, source_target_pairs={{0,1},{1,0},{2,3},{3,2},{4,5},{5,4},{6,7},{7,6},{8,9},{9,8},{10,11... | collective-permute-start | bytes 6684680 | tf_op jit(solution)/shard_map/ppermute | solution.py:64
  41.9 11.6 %collective-permute-start.8 = (f32[4,144,128]{2,1,0:T(8,128)S(1)}, f32[4,144,128]{2,1,0:T(8,128)S(1)}, u32[]{:S(2)}, u32[]{:S(2)}) collective-permute-start(f32[4,144,128]{2,1,0:T(8,128)S(1)} %sum_h.1.a), channel_id=1, source_target_pairs={{0,192},{1,65},{2,194},{3,67},{4,196},{5,69},{6,198},{7,71},{8,200... | collective-permute-start | bytes 884744 | tf_op jit(solution)/shard_map/ppermute | solution.py:83
  50.6 2.2 %copy-start = (bf16[4,2176,128]{2,1,0:T(8,128)(2,1)}, bf16[4,2176,128]{2,1,0:T(8,128)(2,1)S(1)}, u32[]{:S(2)}) copy-start(bf16[4,2176,128]{2,1,0:T(8,128)(2,1)S(1)} %collective-permute-done.7.theirs) | copy-start | bytes 6684676
  54.0 33.6 %all-to-all-start.1 = ((f32[4,1152,128]{2,1,0:T(8,128)}), f32[4,1152,128]{2,1,0:T(8,128)}, u32[]{:S(2)}, u32[]{:S(2)}) async-start(f32[4,1152,128]{2,1,0:T(8,128)} %back_product.1), calls=%async_computation.1 | async-start | bytes 4718592 | tf_op jit(solution)/shard_map/all_to_all | solution.py:69
  58.8 22.3 %collective-permute-start.14 = (f32[288,512]{1,0:T(8,128)}, f32[288,512]{1,0:T(8,128)}, u32[]{:S(2)}, u32[]{:S(2)}) collective-permute-start(f32[288,512]{1,0:T(8,128)} %get-tuple-element.102), channel_id=1, source_target_pairs={{0,2},{1,3},{2,0},{3,1},{4,6},{5,7},{6,4},{7,5},{8,10},{9,11},{10,... | collective-permute-start | bytes 1769480 | tf_op jit(solution)/shard_map/ppermute | solution.py:64
  60.7 12.9 %collective-permute-start.12 = (f32[4,144,128]{2,1,0:T(8,128)S(1)}, f32[4,144,128]{2,1,0:T(8,128)S(1)}, u32[]{:S(2)}, u32[]{:S(2)}) collective-permute-start(f32[4,144,128]{2,1,0:T(8,128)S(1)} %sum_hh.1.totals.refs_0_), channel_id=1, source_target_pairs={{0,48},{16,0},{32,16},{48,32},{64,112},{80,64},{96,80},{112,96},{1... | collective-permute-start | bytes 884744 | tf_op jit(solution)/shard_map/ppermute | solution.py:74
  61.5 19.6 %collective-permute-start.11 = (f32[4,144,128]{2,1,0:T(8,128)S(1)}, f32[4,144,128]{2,1,0:T(8,128)S(1)}, u32[]{:S(2)}, u32[]{:S(2)}) collective-permute-start(f32[4,144,128]{2,1,0:T(8,128)S(1)} %sum_hh.1.totals.refs_0_), channel_id=1, source_target_pairs={{0,32},{16,48},{32,0},{48,16},{64,96},{80,112},{96,64},{112,80},{1... | collective-permute-start | bytes 884744 | tf_op jit(solution)/shard_map/ppermute | solution.py:74
  62.6 18.5 %collective-permute-start.10 = (f32[4,144,128]{2,1,0:T(8,128)S(1)}, f32[4,144,128]{2,1,0:T(8,128)S(1)}, u32[]{:S(2)}, u32[]{:S(2)}) collective-permute-start(f32[4,144,128]{2,1,0:T(8,128)S(1)} %sum_hh.1.totals.refs_0_), channel_id=1, source_target_pairs={{0,16},{16,32},{32,48},{48,0},{64,80},{80,96},{96,112},{112,64},{1... | collective-permute-start | bytes 884744 | tf_op jit(solution)/shard_map/ppermute | solution.py:74
  64.7 19.8 %collective-permute-start.13 = (f32[288,256]{1,0:T(8,128)}, f32[288,256]{1,0:T(8,128)}, u32[]{:S(2)}, u32[]{:S(2)}) collective-permute-start(f32[288,256]{1,0:T(8,128)} %get-tuple-element.101), channel_id=1, source_target_pairs={{0,2},{1,3},{2,0},{3,1},{4,6},{5,7},{6,4},{7,5},{8,10},{9,11},{10,... | collective-permute-start | bytes 884744 | tf_op jit(solution)/shard_map/ppermute | solution.py:64
  73.6 14.0 %collective-permute-start.9 = (f32[288,256]{1,0:T(8,128)}, f32[288,256]{1,0:T(8,128)}, u32[]{:S(2)}, u32[]{:S(2)}) collective-permute-start(f32[288,256]{1,0:T(8,128)} %get-tuple-element.100), channel_id=1, source_target_pairs={{0,2},{1,3},{2,0},{3,1},{4,6},{5,7},{6,4},{7,5},{8,10},{9,11},{10,... | collective-permute-start | bytes 884744 | tf_op jit(solution)/shard_map/ppermute | solution.py:64
  77.2 2.4 %copy-start.3 = (f32[4,288,64]{1,2,0:T(8,128)S(1)}, f32[4,288,64]{1,2,0:T(8,128)}, u32[]{:S(2)}) copy-start(f32[4,288,64]{1,2,0:T(8,128)} %param.16) | copy-start | bytes 884740
  77.2 2.4 %copy-start.5 = (f32[4,288,64]{1,2,0:T(8,128)S(1)}, f32[4,288,64]{1,2,0:T(8,128)}, u32[]{:S(2)}) copy-start(f32[4,288,64]{1,2,0:T(8,128)} %param.17) | copy-start | bytes 884740
  (1 other events, 1.6 us)

commit v6 on v5

--- a/solution.py
+++ b/solution.py
@@ -118,7 +118,7 @@
             out_specs=[whole((rows, kv))] + [whole(piece)] * NX,
             scratch_shapes=[pltpu.VMEM((NX,) + piece, BF)],
         ),
-        out_shape=[pltpu.HBM((rows, kv), BF)] + [shape(piece, BF)] * NX,
+        out_shape=[shape((rows, kv), BF)] + [shape(piece, BF)] * NX,
         compiler_params=pltpu.CompilerParams(vmem_limit_bytes=LIMIT),
         name="pick",
     )(pos, in_hbm(weights))

time: 93.5 us -> 92.6 us (level)
  no operation moved by 1% of the time
where the time goes in v6:
time: 92.6 us; the launch traced here: 92.1 us
  Pallas kernels  34.6 us (37%)
  starting transfers between devices  31.9 us (34%)
  waiting for transfers between devices  22.1 us (24%)
  local copies, waits for them, and re-layouts  1.75 us (2%)
  between operations  1.63 us (2%)
    ppermute x6, waiting for transfers between devices, replica_turn(): return lax.ppermute(array, 'replica', pairs)  15.7 us
    all_to_all x2, starting transfers between devices, fsdp_trade(): lax.all_to_all(array, 'fsdp', 0, 0, axis_index_groups=groups, tiled=True)  9.72 us
    ppermute x7, starting transfers between devices, fsdp_move(): lax.ppermute(array, 'fsdp', [(i, i ^ dz * 2 + dc) for i in range(4 * NY)])  7.72 us
    ppermute x2, starting transfers between devices, replica_swap(): return lax.ppermute(array, ('replica', 'fsdp'), pairs)  7.57 us
    pallas_call x5, Pallas kernels, call(): pl.pallas_call(kernel, grid_spec=pltpu.PrefetchScalarGridSpec(num_scalar_...  7.49 us
    ppermute x6, starting transfers between devices, replica_turn(): return lax.ppermute(array, 'replica', pairs)  6.93 us
    pallas_call x2, Pallas kernels, adam(): pl.pallas_call(adam_kernel, grid_spec=pltpu.PrefetchScalarGridSpec(num_sc...  6.45 us
    pallas_call x1, Pallas kernels, last(): pl.pallas_call(last_kernel, grid_spec=pltpu.PrefetchScalarGridSpec(num_sc...  5.35 us
  transfers between devices with their start and end apart: 17, of which 7 were waited for; matrix products, arithmetic and copies ran while one was open for 0% of the time, Pallas kernels for 27%

profile of v6, /device:TPU:14, one launch (start us, length us, event | category | flops | bytes accessed | tf_op | source)
XLA Modules:
  0.0 92.1 jit_solution(18119642906712897908)
XLA Ops:
  1.4 4.0 %norm.1 = (bf16[4,2176,128]{2,1,0:T(8,128)(2,1)}, f32[128,128]{1,0:T(8,128)}) custom-call(s32[6]{0:T(128)S(1)} %stack.39.pos, bf16[128,4608]{1,0:T(8,128)(2,1)} %hidden.3, f32[4608]{0:T(1024)} %gain.3, bf16[128,1024]{1,0:T(8,128)(2,1)} %cot.1), custom_call_target="tpu_custom_call" | custom-call | tf_op jit(solution)/shard_map/norm/pallas_call | solution.py:48
  5.5 4.9 %all-to-all-start = ((bf16[4,2176,128]{2,1,0:T(8,128)(2,1)}), bf16[4,2176,128]{2,1,0:T(8,128)(2,1)S(1)}, u32[]{:S(2)}, u32[]{:S(2)}) async-start(bf16[4,2176,128]{2,1,0:T(8,128)(2,1)} %get-tuple-element.79), calls=%async_computation | async-start | bytes 4456448 | tf_op jit(solution)/shard_map/all_to_all | solution.py:69
  10.4 2.0 %pick.1 = (bf16[288,1024]{1,0:T(8,128)(2,1)S(1)}, bf16[4,144,128]{2,1,0:T(8,128)(2,1)S(1)}, bf16[4,144,128]{2,1,0:T(8,128)(2,1)S(1)}, bf16[4,144,128]{2,1,0:T(8,128)(2,1)S(1)}, bf16[4,144,128]{2,1,0:T(8,128)(2,1)S(1)}) custom-call(s32[6]{0:T(128)S(1)} %stack.39.pos, bf16[4,288,1024]{2,1,0:T(8,128)(2,1)} %bitcast.31), custom_call_target="tpu_custom_call" | custom-call | tf_op jit(solution)/shard_map/pick/pallas_call | solution.py:112
  12.4 2.0 %collective-permute-start.4 = (bf16[288,1024]{1,0:T(8,128)(2,1)S(1)}, bf16[288,1024]{1,0:T(8,128)(2,1)S(1)}, u32[]{:S(2)}, u32[]{:S(2)}) collective-permute-start(bf16[288,1024]{1,0:T(8,128)(2,1)S(1)} %get-tuple-element.76.w0.slot), channel_id=1, source_target_pairs={{0,2},{1,3},{2,0},{3,1},{4,6},{5,7},{6,4},{7,5},{8,10},{9,11},{10,... | collective-permute-start | bytes 1769480 | tf_op jit(solution)/shard_map/ppermute | solution.py:64
  14.9 2.4 %collective-permute-start.1 = (bf16[4,144,128]{2,1,0:T(8,128)(2,1)S(1)}, bf16[4,144,128]{2,1,0:T(8,128)(2,1)S(1)}, u32[]{:S(2)}, u32[]{:S(2)}) collective-permute-start(bf16[4,144,128]{2,1,0:T(8,128)(2,1)S(1)} %get-tuple-element.67), channel_id=1, source_target_pairs={{0,32},{16,48},{32,0},{48,16},{64,96},{80,112},{96,64},{112,80},{1... | collective-permute-start | bytes 442376 | tf_op jit(solution)/shard_map/ppermute | solution.py:74
  17.3 3.4 %collective-permute-done.b = bf16[4,144,128]{2,1,0:T(8,128)(2,1)S(1)} collective-permute-done((bf16[4,144,128]{2,1,0:T(8,128)(2,1)S(1)}, bf16[4,144,128]{2,1,0:T(8,128)(2,1)S(1)}, u32[]{:S(2)}, u32[]{:S(2)}) %collective-permute-start) | collective-permute-done | bytes 147488 | tf_op jit(solution)/shard_map/ppermute | solution.py:74
  20.7 2.0 %collective-permute-done.1.c = bf16[4,144,128]{2,1,0:T(8,128)(2,1)S(1)} collective-permute-done((bf16[4,144,128]{2,1,0:T(8,128)(2,1)S(1)}, bf16[4,144,128]{2,1,0:T(8,128)(2,1)S(1)}, u32[]{:S(2)}, u32[]{:S(2)}) %collective-permute-start.1) | collective-permute-done | bytes 147488 | tf_op jit(solution)/shard_map/ppermute | solution.py:74
  25.0 2.2 %collective-permute-done.4.wz = bf16[288,1024]{1,0:T(8,128)(2,1)S(1)} collective-permute-done((bf16[288,1024]{1,0:T(8,128)(2,1)S(1)}, bf16[288,1024]{1,0:T(8,128)(2,1)S(1)}, u32[]{:S(2)}, u32[]{:S(2)}) %collective-permute-start.4) | collective-permute-done | bytes 589856 | tf_op jit(solution)/shard_map/ppermute | solution.py:64
  27.2 3.3 %collective-permute-start.6 = (f32[4,144,128]{2,1,0:T(8,128)S(1)}, f32[4,144,128]{2,1,0:T(8,128)S(1)}, u32[]{:S(2)}, u32[]{:S(2)}) collective-permute-start(f32[4,144,128]{2,1,0:T(8,128)S(1)} %sum_x.1.a), channel_id=1, source_target_pairs={{0,64},{1,193},{2,66},{3,195},{4,68},{5,197},{6,70},{7,199},{8,72}... | collective-permute-start | bytes 884744 | tf_op jit(solution)/shard_map/ppermute | solution.py:83
  30.5 4.4 %keep.1.refs_4_ = bf16[4,288,1024]{2,1,0:T(8,128)(2,1)} custom-call(s32[6]{0:T(128)S(1)} %stack.39.pos, bf16[4,288,1024]{2,1,0:T(8,128)(2,1)} %bitcast.32), custom_call_target="tpu_custom_call" | custom-call | tf_op jit(solution)/shard_map/keep/pallas_call | solution.py:133
  34.9 3.5 %collective-permute-done.6.b = f32[4,144,128]{2,1,0:T(8,128)S(1)} collective-permute-done((f32[4,144,128]{2,1,0:T(8,128)S(1)}, f32[4,144,128]{2,1,0:T(8,128)S(1)}, u32[]{:S(2)}, u32[]{:S(2)}) %collective-permute-start.6) | collective-permute-done | bytes 294944 | tf_op jit(solution)/shard_map/ppermute | solution.py:83
  39.0 2.0 %collective-permute-start.7 = (bf16[4,2176,128]{2,1,0:T(8,128)(2,1)S(1)}, bf16[4,2176,128]{2,1,0:T(8,128)(2,1)S(1)}, u32[]{:S(2)}, u32[]{:S(2)}) collective-permute-start(bf16[4,2176,128]{2,1,0:T(8,128)(2,1)S(1)} %all-to-all-done.both.mine), channel_id=1, source_target_pairs={{0,1},{1,0},{2,3},{3,2},{4,5},{5,4},{6,7},{7,6},{8,9},{9,8},{10,11... | collective-permute-start | bytes 6684680 | tf_op jit(solution)/shard_map/ppermute | solution.py:64
  41.0 4.3 %collective-permute-start.8 = (f32[4,144,128]{2,1,0:T(8,128)S(1)}, f32[4,144,128]{2,1,0:T(8,128)S(1)}, u32[]{:S(2)}, u32[]{:S(2)}) collective-permute-start(f32[4,144,128]{2,1,0:T(8,128)S(1)} %sum_h.1.a), channel_id=1, source_target_pairs={{0,192},{1,65},{2,194},{3,67},{4,196},{5,69},{6,198},{7,71},{8,200... | collective-permute-start | bytes 884744 | tf_op jit(solution)/shard_map/ppermute | solution.py:83
  45.3 4.4 %back_product.1 = f32[4,1152,128]{2,1,0:T(8,128)} custom-call(s32[6]{0:T(128)S(1)} %stack.39.pos, bf16[288,1024]{1,0:T(8,128)(2,1)} %copy-done, bf16[288,1024]{1,0:T(8,128)(2,1)} %copy-done.7, bf16[288,1024]{1,0:T(8,128)(2,1)} %copy-done.8, bf16[288,1024]{1,0:T(8,128)(2,1)} %copy-done.9, bf16[4,2176,128]{2,1,0:T(8,128)(2,1)S(1)} %all-to-all-done.both.mine), custom_call_target="tpu_custom_call" | custom-call | tf_op jit(solution)/shard_map/back_product/pallas_call | solution.py:229
  49.7 2.2 %grad_far.1 = (f32[288,512]{1,0:T(8,128)}, f32[288,256]{1,0:T(8,128)}, f32[288,256]{1,0:T(8,128)}) custom-call(s32[6]{0:T(128)S(1)} %stack.39.pos, bf16[4,2176,128]{2,1,0:T(8,128)(2,1)S(1)} %all-to-all-done.both.mine, bf16[4,2176,128]{2,1,0:T(8,128)(2,1)S(1)} %collective-permute-done.7.theirs), custom_call_target="tpu_custom_call" | custom-call | tf_op jit(solution)/shard_map/grad_far/pallas_call | solution.py:271
  53.2 4.8 %all-to-all-start.1 = ((f32[4,1152,128]{2,1,0:T(8,128)}), f32[4,1152,128]{2,1,0:T(8,128)}, u32[]{:S(2)}, u32[]{:S(2)}) async-start(f32[4,1152,128]{2,1,0:T(8,128)} %back_product.1), calls=%async_computation.1 | async-start | bytes 4718592 | tf_op jit(solution)/shard_map/all_to_all | solution.py:69
  58.0 1.9 %collective-permute-start.14 = (f32[288,512]{1,0:T(8,128)}, f32[288,512]{1,0:T(8,128)}, u32[]{:S(2)}, u32[]{:S(2)}) collective-permute-start(f32[288,512]{1,0:T(8,128)} %get-tuple-element.102), channel_id=1, source_target_pairs={{0,2},{1,3},{2,0},{3,1},{4,6},{5,7},{6,4},{7,5},{8,10},{9,11},{10,... | collective-permute-start | bytes 1769480 | tf_op jit(solution)/shard_map/ppermute | solution.py:64
  61.8 2.1 %collective-permute-start.10 = (f32[4,144,128]{2,1,0:T(8,128)S(1)}, f32[4,144,128]{2,1,0:T(8,128)S(1)}, u32[]{:S(2)}, u32[]{:S(2)}) collective-permute-start(f32[4,144,128]{2,1,0:T(8,128)S(1)} %sum_hh.1.totals.refs_0_), channel_id=1, source_target_pairs={{0,16},{16,32},{32,48},{48,0},{64,80},{80,96},{96,112},{112,64},{1... | collective-permute-start | bytes 884744 | tf_op jit(solution)/shard_map/ppermute | solution.py:74
  64.1 8.7 %collective-permute-done.12.refs_3_ = f32[4,144,128]{2,1,0:T(8,128)S(1)} collective-permute-done((f32[4,144,128]{2,1,0:T(8,128)S(1)}, f32[4,144,128]{2,1,0:T(8,128)S(1)}, u32[]{:S(2)}, u32[]{:S(2)}) %collective-permute-start.12) | collective-permute-done | bytes 294944 | tf_op jit(solution)/shard_map/ppermute | solution.py:74
  72.8 1.7 %collective-permute-start.9 = (f32[288,256]{1,0:T(8,128)}, f32[288,256]{1,0:T(8,128)}, u32[]{:S(2)}, u32[]{:S(2)}) collective-permute-start(f32[288,256]{1,0:T(8,128)} %get-tuple-element.100), channel_id=1, source_target_pairs={{0,2},{1,3},{2,0},{3,1},{4,6},{5,7},{6,4},{7,5},{8,10},{9,11},{10,... | collective-permute-start | bytes 884744 | tf_op jit(solution)/shard_map/ppermute | solution.py:64
  76.3 2.4 %grad_near.1.own = f32[288,1024]{1,0:T(8,128)} custom-call(s32[6]{0:T(128)S(1)} %stack.39.pos, bf16[4,2176,128]{2,1,0:T(8,128)(2,1)S(1)} %all-to-all-done.both.mine, bf16[4,2176,128]{2,1,0:T(8,128)(2,1)S(1)} %copy-done.2), custom_call_target="tpu_custom_call" | custom-call | tf_op jit(solution)/shard_map/grad_near/pallas_call | solution.py:271
  80.3 3.4 %adam.2 = (bf16[4,288,1024]{2,1,0:T(8,128)(2,1)}, f32[288,1024]{1,0:T(8,128)}, f32[288,1024]{1,0:T(8,128)}) custom-call(s32[6]{0:T(128)S(1)} %stack.39.pos, f32[3]{0:T(128)S(1)} %pad_maximum_fusion.rates, f32[288,1024]{1,0:T(8,128)} %grad_near.1.own, f32[288,512]{1,0:T(8,128)} %collective-permute-done.14.far, ...), custom_call_target="tpu_custom_call", output_to_operand_aliasing={{0}: (11, {})} | custom-call | tf_op jit(solution)/shard_map/adam/pallas_call | solution.py:337
  83.7 3.0 %adam.3 = (bf16[4,288,1024]{2,1,0:T(8,128)(2,1)}, f32[288,1024]{1,0:T(8,128)}, f32[288,1024]{1,0:T(8,128)}) custom-call(s32[6]{0:T(128)S(1)} %stack.39.pos, f32[3]{0:T(128)S(1)} %pad_maximum_fusion.rates, f32[288,1024]{1,0:T(8,128)} %grad_near.1.own, ...), custom_call_target="tpu_custom_call", output_to_operand_aliasing={{0}: (11, {}), {1}: (12, {}), {2}: (13, {})} | custom-call | tf_op jit(solution)/shard_map/adam/pallas_call | solution.py:337
  86.8 5.4 %last.1 = (bf16[128,4608]{1,0:T(8,128)(2,1)}, bf16[4,288,1024]{2,1,0:T(8,128)(2,1)}, f32[288,1024]{1,0:T(8,128)}, f32[288,1024]{1,0:T(8,128)}) custom-call(s32[6]{0:T(128)S(1)} %stack.39.pos, f32[3]{0:T(128)S(1)} %pad_maximum_fusion.rates, bf16[128,4608]{1,0:T(8,128)(2,1)} %hidden.3, ...), custom_call_target="tpu_custom_call", output_to_operand_aliasing={{1}: (15, {}), {2}: (16, {}), {3}: (17, {})} | custom-call | tf_op jit(solution)/shard_map/last/pallas_call | solution.py:383
  (45 shorter events, 10.1 us)
Async XLA Ops:
  5.5 33.5 %all-to-all-start = ((bf16[4,2176,128]{2,1,0:T(8,128)(2,1)}), bf16[4,2176,128]{2,1,0:T(8,128)(2,1)S(1)}, u32[]{:S(2)}, u32[]{:S(2)}) async-start(bf16[4,2176,128]{2,1,0:T(8,128)(2,1)} %get-tuple-element.79), calls=%async_computation | async-start | bytes 4456448 | tf_op jit(solution)/shard_map/all_to_all | solution.py:69
  10.4 13.9 %copy-start.3 = (f32[4,288,64]{1,2,0:T(8,128)S(1)}, f32[4,288,64]{1,2,0:T(8,128)}, u32[]{:S(2)}) copy-start(f32[4,288,64]{1,2,0:T(8,128)} %param.16) | copy-start | bytes 884740
  10.4 13.9 %copy-start.5 = (f32[4,288,64]{1,2,0:T(8,128)S(1)}, f32[4,288,64]{1,2,0:T(8,128)}, u32[]{:S(2)}) copy-start(f32[4,288,64]{1,2,0:T(8,128)} %param.17) | copy-start | bytes 884740
  12.4 22.5 %copy-start = (bf16[288,1024]{1,0:T(8,128)(2,1)}, bf16[288,1024]{1,0:T(8,128)(2,1)S(1)}, u32[]{:S(2)}) copy-start(bf16[288,1024]{1,0:T(8,128)(2,1)S(1)} %get-tuple-element.76.w0.slot) | copy-start | bytes 1769476
  12.4 14.8 %collective-permute-start.4 = (bf16[288,1024]{1,0:T(8,128)(2,1)S(1)}, bf16[288,1024]{1,0:T(8,128)(2,1)S(1)}, u32[]{:S(2)}, u32[]{:S(2)}) collective-permute-start(bf16[288,1024]{1,0:T(8,128)(2,1)S(1)} %get-tuple-element.76.w0.slot), channel_id=1, source_target_pairs={{0,2},{1,3},{2,0},{3,1},{4,6},{5,7},{6,4},{7,5},{8,10},{9,11},{10,... | collective-permute-start | bytes 1769480 | tf_op jit(solution)/shard_map/ppermute | solution.py:64
  14.4 6.3 %collective-permute-start = (bf16[4,144,128]{2,1,0:T(8,128)(2,1)S(1)}, bf16[4,144,128]{2,1,0:T(8,128)(2,1)S(1)}, u32[]{:S(2)}, u32[]{:S(2)}) collective-permute-start(bf16[4,144,128]{2,1,0:T(8,128)(2,1)S(1)} %get-tuple-element.66), channel_id=1, source_target_pairs={{0,16},{16,32},{32,48},{48,0},{64,80},{80,96},{96,112},{112,64},{1... | collective-permute-start | bytes 442376 | tf_op jit(solution)/shard_map/ppermute | solution.py:74
  14.9 7.9 %collective-permute-start.1 = (bf16[4,144,128]{2,1,0:T(8,128)(2,1)S(1)}, bf16[4,144,128]{2,1,0:T(8,128)(2,1)S(1)}, u32[]{:S(2)}, u32[]{:S(2)}) collective-permute-start(bf16[4,144,128]{2,1,0:T(8,128)(2,1)S(1)} %get-tuple-element.67), channel_id=1, source_target_pairs={{0,32},{16,48},{32,0},{48,16},{64,96},{80,112},{96,64},{112,80},{1... | collective-permute-start | bytes 442376 | tf_op jit(solution)/shard_map/ppermute | solution.py:74
  17.3 7.0 %collective-permute-start.2 = (bf16[4,144,128]{2,1,0:T(8,128)(2,1)S(1)}, bf16[4,144,128]{2,1,0:T(8,128)(2,1)S(1)}, u32[]{:S(2)}, u32[]{:S(2)}) collective-permute-start(bf16[4,144,128]{2,1,0:T(8,128)(2,1)S(1)} %get-tuple-element.68), channel_id=1, source_target_pairs={{0,48},{16,0},{32,16},{48,32},{64,112},{80,64},{96,80},{112,96},{1... | collective-permute-start | bytes 442376 | tf_op jit(solution)/shard_map/ppermute | solution.py:74
  17.3 13.1 %collective-permute-start.3 = (bf16[288,1024]{1,0:T(8,128)(2,1)S(1)}, bf16[288,1024]{1,0:T(8,128)(2,1)S(1)}, u32[]{:S(2)}, u32[]{:S(2)}) collective-permute-start(bf16[288,1024]{1,0:T(8,128)(2,1)S(1)} %get-tuple-element.76.w0.slot), channel_id=1, source_target_pairs={{0,1},{1,0},{2,3},{3,2},{4,5},{5,4},{6,7},{7,6},{8,9},{9,8},{10,11... | collective-permute-start | bytes 1769480 | tf_op jit(solution)/shard_map/ppermute | solution.py:64
  27.2 7.7 %copy-start.7 = (bf16[288,1024]{1,0:T(8,128)(2,1)}, bf16[288,1024]{1,0:T(8,128)(2,1)S(1)}, u32[]{:S(2)}) copy-start(bf16[288,1024]{1,0:T(8,128)(2,1)S(1)} %collective-permute-done.4.wz) | copy-start | bytes 1769476
  27.2 3.3 %collective-permute-start.5 = (bf16[288,1024]{1,0:T(8,128)(2,1)S(1)}, bf16[288,1024]{1,0:T(8,128)(2,1)S(1)}, u32[]{:S(2)}, u32[]{:S(2)}) collective-permute-start(bf16[288,1024]{1,0:T(8,128)(2,1)S(1)} %collective-permute-done.4.wz), channel_id=1, source_target_pairs={{0,1},{1,0},{2,3},{3,2},{4,5},{5,4},{6,7},{7,6},{8,9},{9,8},{10,11... | collective-permute-start | bytes 1769480 | tf_op jit(solution)/shard_map/ppermute | solution.py:64
  27.2 11.2 %collective-permute-start.6 = (f32[4,144,128]{2,1,0:T(8,128)S(1)}, f32[4,144,128]{2,1,0:T(8,128)S(1)}, u32[]{:S(2)}, u32[]{:S(2)}) collective-permute-start(f32[4,144,128]{2,1,0:T(8,128)S(1)} %sum_x.1.a), channel_id=1, source_target_pairs={{0,64},{1,193},{2,66},{3,195},{4,68},{5,197},{6,70},{7,199},{8,72}... | collective-permute-start | bytes 884744 | tf_op jit(solution)/shard_map/ppermute | solution.py:83
  30.4 4.5 %copy-start.8 = (bf16[288,1024]{1,0:T(8,128)(2,1)}, bf16[288,1024]{1,0:T(8,128)(2,1)S(1)}, u32[]{:S(2)}) copy-start(bf16[288,1024]{1,0:T(8,128)(2,1)S(1)} %collective-permute-done.3.wc) | copy-start | bytes 1769476
  30.4 4.5 %copy-start.9 = (bf16[288,1024]{1,0:T(8,128)(2,1)}, bf16[288,1024]{1,0:T(8,128)(2,1)S(1)}, u32[]{:S(2)}) copy-start(bf16[288,1024]{1,0:T(8,128)(2,1)S(1)} %collective-permute-done.5.wzc) | copy-start | bytes 1769476
  39.0 10.7 %collective-permute-start.7 = (bf16[4,2176,128]{2,1,0:T(8,128)(2,1)S(1)}, bf16[4,2176,128]{2,1,0:T(8,128)(2,1)S(1)}, u32[]{:S(2)}, u32[]{:S(2)}) collective-permute-start(bf16[4,2176,128]{2,1,0:T(8,128)(2,1)S(1)} %all-to-all-done.both.mine), channel_id=1, source_target_pairs={{0,1},{1,0},{2,3},{3,2},{4,5},{5,4},{6,7},{7,6},{8,9},{9,8},{10,11... | collective-permute-start | bytes 6684680 | tf_op jit(solution)/shard_map/ppermute | solution.py:64
  41.0 11.6 %collective-permute-start.8 = (f32[4,144,128]{2,1,0:T(8,128)S(1)}, f32[4,144,128]{2,1,0:T(8,128)S(1)}, u32[]{:S(2)}, u32[]{:S(2)}) collective-permute-start(f32[4,144,128]{2,1,0:T(8,128)S(1)} %sum_h.1.a), channel_id=1, source_target_pairs={{0,192},{1,65},{2,194},{3,67},{4,196},{5,69},{6,198},{7,71},{8,200... | collective-permute-start | bytes 884744 | tf_op jit(solution)/shard_map/ppermute | solution.py:83
  53.2 33.6 %all-to-all-start.1 = ((f32[4,1152,128]{2,1,0:T(8,128)}), f32[4,1152,128]{2,1,0:T(8,128)}, u32[]{:S(2)}, u32[]{:S(2)}) async-start(f32[4,1152,128]{2,1,0:T(8,128)} %back_product.1), calls=%async_computation.1 | async-start | bytes 4718592 | tf_op jit(solution)/shard_map/all_to_all | solution.py:69
  58.0 22.3 %collective-permute-start.14 = (f32[288,512]{1,0:T(8,128)}, f32[288,512]{1,0:T(8,128)}, u32[]{:S(2)}, u32[]{:S(2)}) collective-permute-start(f32[288,512]{1,0:T(8,128)} %get-tuple-element.102), channel_id=1, source_target_pairs={{0,2},{1,3},{2,0},{3,1},{4,6},{5,7},{6,4},{7,5},{8,10},{9,11},{10,... | collective-permute-start | bytes 1769480 | tf_op jit(solution)/shard_map/ppermute | solution.py:64
  59.9 12.9 %collective-permute-start.12 = (f32[4,144,128]{2,1,0:T(8,128)S(1)}, f32[4,144,128]{2,1,0:T(8,128)S(1)}, u32[]{:S(2)}, u32[]{:S(2)}) collective-permute-start(f32[4,144,128]{2,1,0:T(8,128)S(1)} %sum_hh.1.totals.refs_0_), channel_id=1, source_target_pairs={{0,48},{16,0},{32,16},{48,32},{64,112},{80,64},{96,80},{112,96},{1... | collective-permute-start | bytes 884744 | tf_op jit(solution)/shard_map/ppermute | solution.py:74
  60.7 19.6 %collective-permute-start.11 = (f32[4,144,128]{2,1,0:T(8,128)S(1)}, f32[4,144,128]{2,1,0:T(8,128)S(1)}, u32[]{:S(2)}, u32[]{:S(2)}) collective-permute-start(f32[4,144,128]{2,1,0:T(8,128)S(1)} %sum_hh.1.totals.refs_0_), channel_id=1, source_target_pairs={{0,32},{16,48},{32,0},{48,16},{64,96},{80,112},{96,64},{112,80},{1... | collective-permute-start | bytes 884744 | tf_op jit(solution)/shard_map/ppermute | solution.py:74
  61.8 18.5 %collective-permute-start.10 = (f32[4,144,128]{2,1,0:T(8,128)S(1)}, f32[4,144,128]{2,1,0:T(8,128)S(1)}, u32[]{:S(2)}, u32[]{:S(2)}) collective-permute-start(f32[4,144,128]{2,1,0:T(8,128)S(1)} %sum_hh.1.totals.refs_0_), channel_id=1, source_target_pairs={{0,16},{16,32},{32,48},{48,0},{64,80},{80,96},{96,112},{112,64},{1... | collective-permute-start | bytes 884744 | tf_op jit(solution)/shard_map/ppermute | solution.py:74
  63.9 19.8 %collective-permute-start.13 = (f32[288,256]{1,0:T(8,128)}, f32[288,256]{1,0:T(8,128)}, u32[]{:S(2)}, u32[]{:S(2)}) collective-permute-start(f32[288,256]{1,0:T(8,128)} %get-tuple-element.101), channel_id=1, source_target_pairs={{0,2},{1,3},{2,0},{3,1},{4,6},{5,7},{6,4},{7,5},{8,10},{9,11},{10,... | collective-permute-start | bytes 884744 | tf_op jit(solution)/shard_map/ppermute | solution.py:64
  72.8 14.0 %collective-permute-start.9 = (f32[288,256]{1,0:T(8,128)}, f32[288,256]{1,0:T(8,128)}, u32[]{:S(2)}, u32[]{:S(2)}) collective-permute-start(f32[288,256]{1,0:T(8,128)} %get-tuple-element.100), channel_id=1, source_target_pairs={{0,2},{1,3},{2,0},{3,1},{4,6},{5,7},{6,4},{7,5},{8,10},{9,11},{10,... | collective-permute-start | bytes 884744 | tf_op jit(solution)/shard_map/ppermute | solution.py:64
  76.3 2.4 %copy-start.6 = (f32[4,288,64]{1,2,0:T(8,128)S(1)}, f32[4,288,64]{1,2,0:T(8,128)}, u32[]{:S(2)}) copy-start(f32[4,288,64]{1,2,0:T(8,128)} %param.17) | copy-start | bytes 884740
  (3 other events, 6.2 us)

commit v7 on v6

--- a/solution.py
+++ b/solution.py
@@ -473,14 +473,15 @@
     pos, backs = after(pos, backs)
 
     sums = grad_product(pos, both, both_c, 1, rows, widths, "grad_far")
-    pos, *sums = lax.optimization_barrier((pos, *sums))
+    pos, far_totals, backs, *sums = lax.optimization_barrier((pos, far_totals, backs, *sums))
+    backs = fsdp_trade(backs).reshape(width, tokens)
     (totals,) = call(pair_kernel, "sum_hh", [packed], (pos, totals, far_totals))
-    pos, totals, backs, *sums = lax.optimization_barrier((pos, totals, backs, *sums))
-    backs = fsdp_trade(backs).reshape(width, tokens)
-    far = [fsdp_move(part, 1, 0) for part in sums]
+    pos, totals, *sums = lax.optimization_barrier((pos, totals, *sums))
+    far = [fsdp_move(part, 1, 0) for part in sums[:-1]]
     all_totals = [totals] + [replica_turn(totals, d) for d in range(1, NX)]
     (own,) = grad_product(pos, both, both_c, 0, rows, [kv], "grad_near")
-    pos, own = after(pos, own)
+    pos, own, sums[-1] = lax.optimization_barrier((pos, own, sums[-1]))
+    far.append(fsdp_move(sums[-1], 1, 0))
 
     new_global, new_momentum = call(
         outer_kernel, "outer", [shape(turned[0].shape, F32)] * 2, (pos, totals, *turned)

time: 92.6 us -> 91.4 us (0.987)
  waiting for transfers between devices: 22.1 us -> 18 us
  local copies, waits for them, and re-layouts: 1.75 us -> 4.43 us
    ppermute x6, waiting for transfers between devices: 15.7 us -> 11.7 us  [replica_turn(): return lax.ppermute(array, 'replica', pairs)]
    unnamed x20 -> x22, local copies, waits for them, and re-layouts: 1.67 us -> 4.35 us
  transfers between devices with their start and end apart: 17 -> 17, of which waited for: 7 -> 7; matrix products, arithmetic and copies ran while one was open for 0% -> 0% of each run, Pallas kernels for 27% -> 28%
where the time goes in v7:
time: 91.4 us; the launch traced here: 90.8 us
  Pallas kernels  34.6 us (38%)
  starting transfers between devices  32 us (35%)
  waiting for transfers between devices  18 us (20%)
  local copies, waits for them, and re-layouts  4.43 us (5%)
  between operations  1.64 us (2%)
    ppermute x6, waiting for transfers between devices, replica_turn(): return lax.ppermute(array, 'replica', pairs)  11.7 us
    all_to_all x2, starting transfers between devices, fsdp_trade(): lax.all_to_all(array, 'fsdp', 0, 0, axis_index_groups=groups, tiled=True)  9.71 us
    ppermute x7, starting transfers between devices, fsdp_move(): lax.ppermute(array, 'fsdp', [(i, i ^ dz * 2 + dc) for i in range(4 * NY)])  7.81 us
    ppermute x2, starting transfers between devices, replica_swap(): return lax.ppermute(array, ('replica', 'fsdp'), pairs)  7.57 us
    pallas_call x5, Pallas kernels, call(): pl.pallas_call(kernel, grid_spec=pltpu.PrefetchScalarGridSpec(num_scalar_...  7.49 us
    ppermute x6, starting transfers between devices, replica_turn(): return lax.ppermute(array, 'replica', pairs)  6.93 us
    pallas_call x2, Pallas kernels, adam(): pl.pallas_call(adam_kernel, grid_spec=pltpu.PrefetchScalarGridSpec(num_sc...  6.45 us
    pallas_call x1, Pallas kernels, last(): pl.pallas_call(last_kernel, grid_spec=pltpu.PrefetchScalarGridSpec(num_sc...  5.34 us
  transfers between devices with their start and end apart: 17, of which 7 were waited for; matrix products, arithmetic and copies ran while one was open for 0% of the time, Pallas kernels for 28%

profile of v7, /device:TPU:14, one launch (start us, length us, event | category | flops | bytes accessed | tf_op | source)
XLA Modules:
  0.0 90.8 jit_solution(17342256639331983140)
XLA Ops:
  1.4 4.0 %norm.1 = (bf16[4,2176,128]{2,1,0:T(8,128)(2,1)}, f32[128,128]{1,0:T(8,128)}) custom-call(s32[6]{0:T(128)S(1)} %stack.39.pos, bf16[128,4608]{1,0:T(8,128)(2,1)} %hidden.3, f32[4608]{0:T(1024)} %gain.3, bf16[128,1024]{1,0:T(8,128)(2,1)} %cot.1), custom_call_target="tpu_custom_call" | custom-call | tf_op jit(solution)/shard_map/norm/pallas_call | solution.py:48
  5.5 4.9 %all-to-all-start = ((bf16[4,2176,128]{2,1,0:T(8,128)(2,1)}), bf16[4,2176,128]{2,1,0:T(8,128)(2,1)S(1)}, u32[]{:S(2)}, u32[]{:S(2)}) async-start(bf16[4,2176,128]{2,1,0:T(8,128)(2,1)} %get-tuple-element.81), calls=%async_computation | async-start | bytes 4456448 | tf_op jit(solution)/shard_map/all_to_all | solution.py:69
  10.4 2.0 %pick.1 = (bf16[288,1024]{1,0:T(8,128)(2,1)S(1)}, bf16[4,144,128]{2,1,0:T(8,128)(2,1)S(1)}, bf16[4,144,128]{2,1,0:T(8,128)(2,1)S(1)}, bf16[4,144,128]{2,1,0:T(8,128)(2,1)S(1)}, bf16[4,144,128]{2,1,0:T(8,128)(2,1)S(1)}) custom-call(s32[6]{0:T(128)S(1)} %stack.39.pos, bf16[4,288,1024]{2,1,0:T(8,128)(2,1)} %bitcast.31), custom_call_target="tpu_custom_call" | custom-call | tf_op jit(solution)/shard_map/pick/pallas_call | solution.py:112
  12.4 2.0 %collective-permute-start.4 = (bf16[288,1024]{1,0:T(8,128)(2,1)S(1)}, bf16[288,1024]{1,0:T(8,128)(2,1)S(1)}, u32[]{:S(2)}, u32[]{:S(2)}) collective-permute-start(bf16[288,1024]{1,0:T(8,128)(2,1)S(1)} %get-tuple-element.78.w0.slot), channel_id=1, source_target_pairs={{0,2},{1,3},{2,0},{3,1},{4,6},{5,7},{6,4},{7,5},{8,10},{9,11},{10,... | collective-permute-start | bytes 1769480 | tf_op jit(solution)/shard_map/ppermute | solution.py:64
  14.9 2.4 %collective-permute-start.1 = (bf16[4,144,128]{2,1,0:T(8,128)(2,1)S(1)}, bf16[4,144,128]{2,1,0:T(8,128)(2,1)S(1)}, u32[]{:S(2)}, u32[]{:S(2)}) collective-permute-start(bf16[4,144,128]{2,1,0:T(8,128)(2,1)S(1)} %get-tuple-element.69), channel_id=1, source_target_pairs={{0,32},{16,48},{32,0},{48,16},{64,96},{80,112},{96,64},{112,80},{1... | collective-permute-start | bytes 442376 | tf_op jit(solution)/shard_map/ppermute | solution.py:74
  17.3 3.4 %collective-permute-done.b = bf16[4,144,128]{2,1,0:T(8,128)(2,1)S(1)} collective-permute-done((bf16[4,144,128]{2,1,0:T(8,128)(2,1)S(1)}, bf16[4,144,128]{2,1,0:T(8,128)(2,1)S(1)}, u32[]{:S(2)}, u32[]{:S(2)}) %collective-permute-start) | collective-permute-done | bytes 147488 | tf_op jit(solution)/shard_map/ppermute | solution.py:74
  20.7 2.0 %collective-permute-done.1.c = bf16[4,144,128]{2,1,0:T(8,128)(2,1)S(1)} collective-permute-done((bf16[4,144,128]{2,1,0:T(8,128)(2,1)S(1)}, bf16[4,144,128]{2,1,0:T(8,128)(2,1)S(1)}, u32[]{:S(2)}, u32[]{:S(2)}) %collective-permute-start.1) | collective-permute-done | bytes 147488 | tf_op jit(solution)/shard_map/ppermute | solution.py:74
  25.0 2.2 %collective-permute-done.4.wz = bf16[288,1024]{1,0:T(8,128)(2,1)S(1)} collective-permute-done((bf16[288,1024]{1,0:T(8,128)(2,1)S(1)}, bf16[288,1024]{1,0:T(8,128)(2,1)S(1)}, u32[]{:S(2)}, u32[]{:S(2)}) %collective-permute-start.4) | collective-permute-done | bytes 589856 | tf_op jit(solution)/shard_map/ppermute | solution.py:64
  27.2 3.3 %collective-permute-start.6 = (f32[4,144,128]{2,1,0:T(8,128)S(1)}, f32[4,144,128]{2,1,0:T(8,128)S(1)}, u32[]{:S(2)}, u32[]{:S(2)}) collective-permute-start(f32[4,144,128]{2,1,0:T(8,128)S(1)} %sum_x.1.a), channel_id=1, source_target_pairs={{0,64},{1,193},{2,66},{3,195},{4,68},{5,197},{6,70},{7,199},{8,72}... | collective-permute-start | bytes 884744 | tf_op jit(solution)/shard_map/ppermute | solution.py:83
  30.5 4.4 %keep.1.refs_4_ = bf16[4,288,1024]{2,1,0:T(8,128)(2,1)} custom-call(s32[6]{0:T(128)S(1)} %stack.39.pos, bf16[4,288,1024]{2,1,0:T(8,128)(2,1)} %bitcast.32), custom_call_target="tpu_custom_call" | custom-call | tf_op jit(solution)/shard_map/keep/pallas_call | solution.py:133
  34.9 3.5 %collective-permute-done.6.b = f32[4,144,128]{2,1,0:T(8,128)S(1)} collective-permute-done((f32[4,144,128]{2,1,0:T(8,128)S(1)}, f32[4,144,128]{2,1,0:T(8,128)S(1)}, u32[]{:S(2)}, u32[]{:S(2)}) %collective-permute-start.6) | collective-permute-done | bytes 294944 | tf_op jit(solution)/shard_map/ppermute | solution.py:83
  39.0 2.0 %collective-permute-start.8 = (bf16[4,2176,128]{2,1,0:T(8,128)(2,1)S(1)}, bf16[4,2176,128]{2,1,0:T(8,128)(2,1)S(1)}, u32[]{:S(2)}, u32[]{:S(2)}) collective-permute-start(bf16[4,2176,128]{2,1,0:T(8,128)(2,1)S(1)} %all-to-all-done.both.mine), channel_id=1, source_target_pairs={{0,1},{1,0},{2,3},{3,2},{4,5},{5,4},{6,7},{7,6},{8,9},{9,8},{10,11... | collective-permute-start | bytes 6684680 | tf_op jit(solution)/shard_map/ppermute | solution.py:64
  41.0 4.3 %collective-permute-start.7 = (f32[4,144,128]{2,1,0:T(8,128)S(1)}, f32[4,144,128]{2,1,0:T(8,128)S(1)}, u32[]{:S(2)}, u32[]{:S(2)}) collective-permute-start(f32[4,144,128]{2,1,0:T(8,128)S(1)} %sum_h.1.a), channel_id=1, source_target_pairs={{0,192},{1,65},{2,194},{3,67},{4,196},{5,69},{6,198},{7,71},{8,200... | collective-permute-start | bytes 884744 | tf_op jit(solution)/shard_map/ppermute | solution.py:83
  45.3 4.4 %back_product.1 = f32[4,1152,128]{2,1,0:T(8,128)} custom-call(s32[6]{0:T(128)S(1)} %stack.39.pos, bf16[288,1024]{1,0:T(8,128)(2,1)} %copy-done, bf16[288,1024]{1,0:T(8,128)(2,1)} %copy-done.7, bf16[288,1024]{1,0:T(8,128)(2,1)} %copy-done.8, bf16[288,1024]{1,0:T(8,128)(2,1)} %copy-done.9, bf16[4,2176,128]{2,1,0:T(8,128)(2,1)S(1)} %all-to-all-done.both.mine), custom_call_target="tpu_custom_call" | custom-call | tf_op jit(solution)/shard_map/back_product/pallas_call | solution.py:229
  49.7 2.2 %grad_far.1 = (f32[288,512]{1,0:T(8,128)}, f32[288,256]{1,0:T(8,128)}, f32[288,256]{1,0:T(8,128)}) custom-call(s32[6]{0:T(128)S(1)} %stack.39.pos, bf16[4,2176,128]{2,1,0:T(8,128)(2,1)S(1)} %all-to-all-done.both.mine, bf16[4,2176,128]{2,1,0:T(8,128)(2,1)S(1)} %collective-permute-done.8.theirs), custom_call_target="tpu_custom_call" | custom-call | tf_op jit(solution)/shard_map/grad_far/pallas_call | solution.py:271
  52.6 4.8 %all-to-all-start.1 = ((f32[4,1152,128]{2,1,0:T(8,128)}), f32[4,1152,128]{2,1,0:T(8,128)}, u32[]{:S(2)}, u32[]{:S(2)}) async-start(f32[4,1152,128]{2,1,0:T(8,128)} %back_product.1), calls=%async_computation.1 | async-start | bytes 4718592 | tf_op jit(solution)/shard_map/all_to_all | solution.py:69
  58.0 2.0 %collective-permute-start.14 = (f32[288,512]{1,0:T(8,128)}, f32[288,512]{1,0:T(8,128)}, u32[]{:S(2)}, u32[]{:S(2)}) collective-permute-start(f32[288,512]{1,0:T(8,128)} %get-tuple-element.106), channel_id=1, source_target_pairs={{0,2},{1,3},{2,0},{3,1},{4,6},{5,7},{6,4},{7,5},{8,10},{9,11},{10,... | collective-permute-start | bytes 1769480 | tf_op jit(solution)/shard_map/ppermute | solution.py:64
  61.9 2.1 %collective-permute-start.10 = (f32[4,144,128]{2,1,0:T(8,128)S(1)}, f32[4,144,128]{2,1,0:T(8,128)S(1)}, u32[]{:S(2)}, u32[]{:S(2)}) collective-permute-start(f32[4,144,128]{2,1,0:T(8,128)S(1)} %sum_hh.1.totals.refs_0_), channel_id=1, source_target_pairs={{0,16},{16,32},{32,48},{48,0},{64,80},{80,96},{96,112},{112,64},{1... | collective-permute-start | bytes 884744 | tf_op jit(solution)/shard_map/ppermute | solution.py:74
  65.8 2.3 %grad_near.1.own = f32[288,1024]{1,0:T(8,128)} custom-call(s32[6]{0:T(128)S(1)} %stack.39.pos, bf16[4,2176,128]{2,1,0:T(8,128)(2,1)S(1)} %all-to-all-done.both.mine, bf16[4,2176,128]{2,1,0:T(8,128)(2,1)S(1)} %copy-done.2), custom_call_target="tpu_custom_call" | custom-call | tf_op jit(solution)/shard_map/grad_near/pallas_call | solution.py:271
  68.1 4.7 %collective-permute-done.12.refs_3_ = f32[4,144,128]{2,1,0:T(8,128)S(1)} collective-permute-done((f32[4,144,128]{2,1,0:T(8,128)S(1)}, f32[4,144,128]{2,1,0:T(8,128)S(1)}, u32[]{:S(2)}, u32[]{:S(2)}) %collective-permute-start.12) | collective-permute-done | bytes 294944 | tf_op jit(solution)/shard_map/ppermute | solution.py:74
  72.8 1.7 %collective-permute-start.9 = (f32[288,256]{1,0:T(8,128)}, f32[288,256]{1,0:T(8,128)S(1)}, u32[]{:S(2)}, u32[]{:S(2)}) collective-permute-start(f32[288,256]{1,0:T(8,128)} %get-tuple-element.104), channel_id=1, source_target_pairs={{0,2},{1,3},{2,0},{3,1},{4,6},{5,7},{6,4},{7,5},{8,10},{9,11},{10,... | collective-permute-start | bytes 884744 | tf_op jit(solution)/shard_map/ppermute | solution.py:64
  78.3 3.4 %adam.2 = (bf16[4,288,1024]{2,1,0:T(8,128)(2,1)}, f32[288,1024]{1,0:T(8,128)}, f32[288,1024]{1,0:T(8,128)}) custom-call(s32[6]{0:T(128)S(1)} %stack.39.pos, f32[3]{0:T(128)S(1)} %pad_maximum_fusion.rates, f32[288,1024]{1,0:T(8,128)} %grad_near.1.own, f32[288,512]{1,0:T(8,128)} %collective-permute-done.14.far, ...), custom_call_target="tpu_custom_call", output_to_operand_aliasing={{0}: (11, {})} | custom-call | tf_op jit(solution)/shard_map/adam/pallas_call | solution.py:337
  81.8 3.0 %adam.3 = (bf16[4,288,1024]{2,1,0:T(8,128)(2,1)}, f32[288,1024]{1,0:T(8,128)}, f32[288,1024]{1,0:T(8,128)}) custom-call(s32[6]{0:T(128)S(1)} %stack.39.pos, f32[3]{0:T(128)S(1)} %pad_maximum_fusion.rates, f32[288,1024]{1,0:T(8,128)} %grad_near.1.own, ...), custom_call_target="tpu_custom_call", output_to_operand_aliasing={{0}: (11, {}), {1}: (12, {}), {2}: (13, {})} | custom-call | tf_op jit(solution)/shard_map/adam/pallas_call | solution.py:337
  85.5 5.3 %last.1 = (bf16[128,4608]{1,0:T(8,128)(2,1)}, bf16[4,288,1024]{2,1,0:T(8,128)(2,1)}, f32[288,1024]{1,0:T(8,128)}, f32[288,1024]{1,0:T(8,128)}) custom-call(s32[6]{0:T(128)S(1)} %stack.39.pos, f32[3]{0:T(128)S(1)} %pad_maximum_fusion.rates, bf16[128,4608]{1,0:T(8,128)(2,1)} %hidden.3, ...), custom_call_target="tpu_custom_call", output_to_operand_aliasing={{1}: (15, {}), {2}: (16, {}), {3}: (17, {})} | custom-call | tf_op jit(solution)/shard_map/last/pallas_call | solution.py:383
  (47 shorter events, 12.8 us)
Async XLA Ops:
  5.5 33.5 %all-to-all-start = ((bf16[4,2176,128]{2,1,0:T(8,128)(2,1)}), bf16[4,2176,128]{2,1,0:T(8,128)(2,1)S(1)}, u32[]{:S(2)}, u32[]{:S(2)}) async-start(bf16[4,2176,128]{2,1,0:T(8,128)(2,1)} %get-tuple-element.81), calls=%async_computation | async-start | bytes 4456448 | tf_op jit(solution)/shard_map/all_to_all | solution.py:69
  10.4 13.9 %copy-start.3 = (f32[4,288,64]{1,2,0:T(8,128)S(1)}, f32[4,288,64]{1,2,0:T(8,128)}, u32[]{:S(2)}) copy-start(f32[4,288,64]{1,2,0:T(8,128)} %param.16) | copy-start | bytes 884740
  10.4 13.9 %copy-start.5 = (f32[4,288,64]{1,2,0:T(8,128)S(1)}, f32[4,288,64]{1,2,0:T(8,128)}, u32[]{:S(2)}) copy-start(f32[4,288,64]{1,2,0:T(8,128)} %param.17) | copy-start | bytes 884740
  12.4 22.5 %copy-start = (bf16[288,1024]{1,0:T(8,128)(2,1)}, bf16[288,1024]{1,0:T(8,128)(2,1)S(1)}, u32[]{:S(2)}) copy-start(bf16[288,1024]{1,0:T(8,128)(2,1)S(1)} %get-tuple-element.78.w0.slot) | copy-start | bytes 1769476
  12.4 14.8 %collective-permute-start.4 = (bf16[288,1024]{1,0:T(8,128)(2,1)S(1)}, bf16[288,1024]{1,0:T(8,128)(2,1)S(1)}, u32[]{:S(2)}, u32[]{:S(2)}) collective-permute-start(bf16[288,1024]{1,0:T(8,128)(2,1)S(1)} %get-tuple-element.78.w0.slot), channel_id=1, source_target_pairs={{0,2},{1,3},{2,0},{3,1},{4,6},{5,7},{6,4},{7,5},{8,10},{9,11},{10,... | collective-permute-start | bytes 1769480 | tf_op jit(solution)/shard_map/ppermute | solution.py:64
  14.4 6.3 %collective-permute-start = (bf16[4,144,128]{2,1,0:T(8,128)(2,1)S(1)}, bf16[4,144,128]{2,1,0:T(8,128)(2,1)S(1)}, u32[]{:S(2)}, u32[]{:S(2)}) collective-permute-start(bf16[4,144,128]{2,1,0:T(8,128)(2,1)S(1)} %get-tuple-element.68), channel_id=1, source_target_pairs={{0,16},{16,32},{32,48},{48,0},{64,80},{80,96},{96,112},{112,64},{1... | collective-permute-start | bytes 442376 | tf_op jit(solution)/shard_map/ppermute | solution.py:74
  14.9 7.9 %collective-permute-start.1 = (bf16[4,144,128]{2,1,0:T(8,128)(2,1)S(1)}, bf16[4,144,128]{2,1,0:T(8,128)(2,1)S(1)}, u32[]{:S(2)}, u32[]{:S(2)}) collective-permute-start(bf16[4,144,128]{2,1,0:T(8,128)(2,1)S(1)} %get-tuple-element.69), channel_id=1, source_target_pairs={{0,32},{16,48},{32,0},{48,16},{64,96},{80,112},{96,64},{112,80},{1... | collective-permute-start | bytes 442376 | tf_op jit(solution)/shard_map/ppermute | solution.py:74
  17.3 7.0 %collective-permute-start.2 = (bf16[4,144,128]{2,1,0:T(8,128)(2,1)S(1)}, bf16[4,144,128]{2,1,0:T(8,128)(2,1)S(1)}, u32[]{:S(2)}, u32[]{:S(2)}) collective-permute-start(bf16[4,144,128]{2,1,0:T(8,128)(2,1)S(1)} %get-tuple-element.70), channel_id=1, source_target_pairs={{0,48},{16,0},{32,16},{48,32},{64,112},{80,64},{96,80},{112,96},{1... | collective-permute-start | bytes 442376 | tf_op jit(solution)/shard_map/ppermute | solution.py:74
  17.3 13.1 %collective-permute-start.3 = (bf16[288,1024]{1,0:T(8,128)(2,1)S(1)}, bf16[288,1024]{1,0:T(8,128)(2,1)S(1)}, u32[]{:S(2)}, u32[]{:S(2)}) collective-permute-start(bf16[288,1024]{1,0:T(8,128)(2,1)S(1)} %get-tuple-element.78.w0.slot), channel_id=1, source_target_pairs={{0,1},{1,0},{2,3},{3,2},{4,5},{5,4},{6,7},{7,6},{8,9},{9,8},{10,11... | collective-permute-start | bytes 1769480 | tf_op jit(solution)/shard_map/ppermute | solution.py:64
  27.2 7.7 %copy-start.7 = (bf16[288,1024]{1,0:T(8,128)(2,1)}, bf16[288,1024]{1,0:T(8,128)(2,1)S(1)}, u32[]{:S(2)}) copy-start(bf16[288,1024]{1,0:T(8,128)(2,1)S(1)} %collective-permute-done.4.wz) | copy-start | bytes 1769476
  27.2 3.3 %collective-permute-start.5 = (bf16[288,1024]{1,0:T(8,128)(2,1)S(1)}, bf16[288,1024]{1,0:T(8,128)(2,1)S(1)}, u32[]{:S(2)}, u32[]{:S(2)}) collective-permute-start(bf16[288,1024]{1,0:T(8,128)(2,1)S(1)} %collective-permute-done.4.wz), channel_id=1, source_target_pairs={{0,1},{1,0},{2,3},{3,2},{4,5},{5,4},{6,7},{7,6},{8,9},{9,8},{10,11... | collective-permute-start | bytes 1769480 | tf_op jit(solution)/shard_map/ppermute | solution.py:64
  27.2 11.2 %collective-permute-start.6 = (f32[4,144,128]{2,1,0:T(8,128)S(1)}, f32[4,144,128]{2,1,0:T(8,128)S(1)}, u32[]{:S(2)}, u32[]{:S(2)}) collective-permute-start(f32[4,144,128]{2,1,0:T(8,128)S(1)} %sum_x.1.a), channel_id=1, source_target_pairs={{0,64},{1,193},{2,66},{3,195},{4,68},{5,197},{6,70},{7,199},{8,72}... | collective-permute-start | bytes 884744 | tf_op jit(solution)/shard_map/ppermute | solution.py:83
  30.4 4.5 %copy-start.8 = (bf16[288,1024]{1,0:T(8,128)(2,1)}, bf16[288,1024]{1,0:T(8,128)(2,1)S(1)}, u32[]{:S(2)}) copy-start(bf16[288,1024]{1,0:T(8,128)(2,1)S(1)} %collective-permute-done.3.wc) | copy-start | bytes 1769476
  30.4 4.5 %copy-start.9 = (bf16[288,1024]{1,0:T(8,128)(2,1)}, bf16[288,1024]{1,0:T(8,128)(2,1)S(1)}, u32[]{:S(2)}) copy-start(bf16[288,1024]{1,0:T(8,128)(2,1)S(1)} %collective-permute-done.5.wzc) | copy-start | bytes 1769476
  39.0 10.7 %collective-permute-start.8 = (bf16[4,2176,128]{2,1,0:T(8,128)(2,1)S(1)}, bf16[4,2176,128]{2,1,0:T(8,128)(2,1)S(1)}, u32[]{:S(2)}, u32[]{:S(2)}) collective-permute-start(bf16[4,2176,128]{2,1,0:T(8,128)(2,1)S(1)} %all-to-all-done.both.mine), channel_id=1, source_target_pairs={{0,1},{1,0},{2,3},{3,2},{4,5},{5,4},{6,7},{7,6},{8,9},{9,8},{10,11... | collective-permute-start | bytes 6684680 | tf_op jit(solution)/shard_map/ppermute | solution.py:64
  41.0 11.6 %collective-permute-start.7 = (f32[4,144,128]{2,1,0:T(8,128)S(1)}, f32[4,144,128]{2,1,0:T(8,128)S(1)}, u32[]{:S(2)}, u32[]{:S(2)}) collective-permute-start(f32[4,144,128]{2,1,0:T(8,128)S(1)} %sum_h.1.a), channel_id=1, source_target_pairs={{0,192},{1,65},{2,194},{3,67},{4,196},{5,69},{6,198},{7,71},{8,200... | collective-permute-start | bytes 884744 | tf_op jit(solution)/shard_map/ppermute | solution.py:83
  49.7 2.2 %copy-start.1 = (bf16[4,2176,128]{2,1,0:T(8,128)(2,1)}, bf16[4,2176,128]{2,1,0:T(8,128)(2,1)S(1)}, u32[]{:S(2)}) copy-start(bf16[4,2176,128]{2,1,0:T(8,128)(2,1)S(1)} %collective-permute-done.8.theirs) | copy-start | bytes 6684676
  52.6 32.2 %all-to-all-start.1 = ((f32[4,1152,128]{2,1,0:T(8,128)}), f32[4,1152,128]{2,1,0:T(8,128)}, u32[]{:S(2)}, u32[]{:S(2)}) async-start(f32[4,1152,128]{2,1,0:T(8,128)} %back_product.1), calls=%async_computation.1 | async-start | bytes 4718592 | tf_op jit(solution)/shard_map/all_to_all | solution.py:69
  58.0 20.3 %collective-permute-start.14 = (f32[288,512]{1,0:T(8,128)}, f32[288,512]{1,0:T(8,128)}, u32[]{:S(2)}, u32[]{:S(2)}) collective-permute-start(f32[288,512]{1,0:T(8,128)} %get-tuple-element.106), channel_id=1, source_target_pairs={{0,2},{1,3},{2,0},{3,1},{4,6},{5,7},{6,4},{7,5},{8,10},{9,11},{10,... | collective-permute-start | bytes 1769480 | tf_op jit(solution)/shard_map/ppermute | solution.py:64
  59.9 12.9 %collective-permute-start.12 = (f32[4,144,128]{2,1,0:T(8,128)S(1)}, f32[4,144,128]{2,1,0:T(8,128)S(1)}, u32[]{:S(2)}, u32[]{:S(2)}) collective-permute-start(f32[4,144,128]{2,1,0:T(8,128)S(1)} %sum_hh.1.totals.refs_0_), channel_id=1, source_target_pairs={{0,48},{16,0},{32,16},{48,32},{64,112},{80,64},{96,80},{112,96},{1... | collective-permute-start | bytes 884744 | tf_op jit(solution)/shard_map/ppermute | solution.py:74
  60.8 17.5 %collective-permute-start.11 = (f32[4,144,128]{2,1,0:T(8,128)S(1)}, f32[4,144,128]{2,1,0:T(8,128)S(1)}, u32[]{:S(2)}, u32[]{:S(2)}) collective-permute-start(f32[4,144,128]{2,1,0:T(8,128)S(1)} %sum_hh.1.totals.refs_0_), channel_id=1, source_target_pairs={{0,32},{16,48},{32,0},{48,16},{64,96},{80,112},{96,64},{112,80},{1... | collective-permute-start | bytes 884744 | tf_op jit(solution)/shard_map/ppermute | solution.py:74
  61.9 16.4 %collective-permute-start.10 = (f32[4,144,128]{2,1,0:T(8,128)S(1)}, f32[4,144,128]{2,1,0:T(8,128)S(1)}, u32[]{:S(2)}, u32[]{:S(2)}) collective-permute-start(f32[4,144,128]{2,1,0:T(8,128)S(1)} %sum_hh.1.totals.refs_0_), channel_id=1, source_target_pairs={{0,16},{16,32},{32,48},{48,0},{64,80},{80,96},{96,112},{112,64},{1... | collective-permute-start | bytes 884744 | tf_op jit(solution)/shard_map/ppermute | solution.py:74
  64.0 17.8 %collective-permute-start.13 = (f32[288,256]{1,0:T(8,128)}, f32[288,256]{1,0:T(8,128)}, u32[]{:S(2)}, u32[]{:S(2)}) collective-permute-start(f32[288,256]{1,0:T(8,128)} %get-tuple-element.105), channel_id=1, source_target_pairs={{0,2},{1,3},{2,0},{3,1},{4,6},{5,7},{6,4},{7,5},{8,10},{9,11},{10,... | collective-permute-start | bytes 884744 | tf_op jit(solution)/shard_map/ppermute | solution.py:64
  72.8 12.0 %collective-permute-start.9 = (f32[288,256]{1,0:T(8,128)}, f32[288,256]{1,0:T(8,128)S(1)}, u32[]{:S(2)}, u32[]{:S(2)}) collective-permute-start(f32[288,256]{1,0:T(8,128)} %get-tuple-element.104), channel_id=1, source_target_pairs={{0,2},{1,3},{2,0},{3,1},{4,6},{5,7},{6,4},{7,5},{8,10},{9,11},{10,... | collective-permute-start | bytes 884744 | tf_op jit(solution)/shard_map/ppermute | solution.py:64
  (4 other events, 4.3 us)
